TPU v7x, 32 devices: a whole 2x2x4 slice. The times are simulated.
32 devices in a mesh: seq: 4 (over z), head: 8 (over y, x, core).
Axes of the slice: x: 2, y: 2, z: 4, core: 2. Of those that a mesh axis runs over, the one named last changes fastest.
Arguments:
- query: bfloat16 [40, 512, 128], P('head', 'seq'), may hold values from -1024 to 1024
- key: bfloat16 [40, 512, 128], P('head', 'seq'), may hold values from -1024 to 1024
- value: bfloat16 [40, 512, 128], P('head', 'seq'), may hold values from -6 to 6
- q_gain: float32 [40, 128], replicated, may hold values from 0.8 to 2
- k_gain: float32 [40, 128], replicated, may hold values from 0.8 to 2
- order: int32 [40, 512], P('head', 'seq'), may hold values from 0 to 511, as said below
- cluster_rows: int32 [40, 4], P('head'), may hold values from 0 to 256, as said below
- block_map: int32 [40, 8, 8], P('head'), may hold values 0 or 1
Outputs:
- attended: bfloat16 [40, 512, 128], P('head', 'seq')
Inputs may be any that keep to these rules, and one draw needn't show every extreme that they name: `order`: each stream's row lists every token row once: the rows of cluster 0 first, then those of cluster 1, and so on, in the counts of cluster_rows. `cluster_rows`: each stream's counts sum to 512; of the 128 token rows of one seq index at most 64 belong to one cluster, and in every stream one cluster takes exactly 64 rows from every seq index.
All inputs are finite; a program needn't handle non-finite values. No bound on the sum of `block_map` on one device may be relied on, other than what follows from the above.
Results may differ from a plain program's by a relative error of at most 0.012.
The roundings to bfloat16 on the way count: a program that leaves them out, or rounds other values in their place, can miss the bound.
Values may be sent and summed in bfloat16 or wider, within the bound.
No kernel may reach another device: no remote copies, remote signals or barrier semaphores. Data moves between devices by JAX's collectives and lax.ppermute only.
A program may use at most 64 MiB of HBM per device.

v0:
```python
import jax
import jax.numpy as jnp
from jax import lax
from jax.sharding import PartitionSpec as P

BLOCK = 128


epsilon = 1e-06
floor_score = -1e30
key_block = 256


def absorb(running, scores, allowed, value_rows):
    row_peak, denom_sum, numerator = running
    masked = jnp.where(allowed, scores, floor_score)
    new_peak = jnp.maximum(row_peak, jnp.max(masked, axis=2))
    weights = jnp.where(allowed, jnp.exp(masked - new_peak[:, :, None]), 0.0)
    rescale = jnp.exp(row_peak - new_peak)
    denom_sum = denom_sum * rescale + jnp.sum(weights, axis=2)
    numerator = numerator * rescale[:, :, None] + jnp.einsum(
        "sqk,skd->sqd", weights.astype(jnp.bfloat16), value_rows, preferred_element_type=jnp.float32
    )
    return (new_peak, denom_sum, numerator)


def fold_keys(running, key_rows, value_rows, score_fn):
    row_count = key_rows.shape[1]

    def visit_block(block_index, inner_state):
        first_row = block_index * key_block
        key_part = lax.dynamic_slice_in_dim(key_rows, first_row, key_block, 1)
        value_part = lax.dynamic_slice_in_dim(value_rows, first_row, key_block, 1)
        return score_fn(inner_state, key_part, value_part, first_row)

    return lax.fori_loop(0, row_count // key_block, visit_block, running)


def normalize(rows, gain_rows, scale_rows):
    return (rows.astype(jnp.float32) * scale_rows[None, :, None] * gain_rows[:, None, :]).astype(
        jnp.bfloat16
    )


def local(query, key, value, q_gain, k_gain, order, cluster_rows, block_map):
    streams, tok_rows, head_width = query.shape
    head_count = q_gain.shape[0]
    seq_count = lax.axis_size("seq")
    seq_rank = lax.axis_index("seq")
    head_rank = lax.axis_index("head")
    videos = streams * lax.axis_size("head") // head_count
    first_stream = head_rank * streams
    video_pick = (jnp.arange(videos) == first_stream // head_count).astype(jnp.float32)
    square_q = jnp.sum(jnp.square(query.astype(jnp.float32)), axis=(0, 2))
    square_k = jnp.sum(jnp.square(key.astype(jnp.float32)), axis=(0, 2))
    totals = lax.psum((square_q[:, None] * video_pick, square_k[:, None] * video_pick), "head")
    norm_width = head_count * head_width
    scale_q = lax.rsqrt(jnp.sum(totals[0] * video_pick, axis=1) / norm_width + epsilon)
    scale_k = lax.rsqrt(jnp.sum(totals[1] * video_pick, axis=1) / norm_width + epsilon)
    first_head = first_stream % head_count
    normed_q = normalize(query, lax.dynamic_slice_in_dim(q_gain, first_head, streams, 0), scale_q)
    normed_k = normalize(key, lax.dynamic_slice_in_dim(k_gain, first_head, streams, 0), scale_k)
    full_order = lax.all_gather(order, "seq", axis=1, tiled=True)
    seq_length = full_order.shape[1]
    positions = jnp.arange(seq_length, dtype=jnp.int32)
    stream_index = jnp.arange(streams, dtype=jnp.int32)[:, None]
    inverse = (
        jnp.zeros((streams, seq_length), jnp.int32)
        .at[stream_index, full_order]
        .set(jnp.broadcast_to(positions, (streams, seq_length)))
    )
    cluster_start = jnp.cumsum(cluster_rows, axis=1, dtype=jnp.int32) - cluster_rows
    cluster_axis = jnp.arange(seq_count, dtype=jnp.int32)
    owner_index = (
        jnp.sum(
            (cluster_start[:, None, :] <= inverse[:, :, None]).astype(jnp.int32),
            axis=2,
            dtype=jnp.int32,
        )
        - 1
    )
    owner_hit = owner_index[:, :, None] == cluster_axis
    owner_start = jnp.sum(
        jnp.where(owner_hit, cluster_start[:, None, :], 0), axis=2, dtype=jnp.int32
    )
    capacity = 2 * tok_rows
    blocks_per = capacity // BLOCK
    token_block = owner_index * blocks_per + (inverse - owner_start) // BLOCK
    block_count = block_map.shape[2]
    block_axis = jnp.arange(block_count, dtype=jnp.int32)
    score_scale = head_width ** (-0.5)
    my_tokens = seq_rank * tok_rows
    my_block = lax.dynamic_slice_in_dim(token_block, my_tokens, tok_rows, 1)
    row_table = jnp.einsum(
        "stn,snm->stm",
        (my_block[:, :, None] == block_axis).astype(jnp.float32),
        block_map.astype(jnp.float32),
    )

    def score_tokens(inner_state, key_part, value_part, offset):
        key_span = key_part.shape[1]
        key_ids = lax.dynamic_slice_in_dim(token_block, offset, key_span, 1)
        allowed = (
            jnp.einsum(
                "stm,skm->stk", row_table, (key_ids[:, :, None] == block_axis).astype(jnp.float32)
            )
            > 0.5
        )
        allowed = allowed | (my_block[:, :, None] == key_ids[:, None, :])
        scores = (
            jnp.einsum("sqd,skd->sqk", normed_q, key_part, preferred_element_type=jnp.float32)
            * score_scale
        )
        return absorb(inner_state, scores, allowed, value_part)

    start_state = (
        jnp.full((streams, tok_rows), floor_score, jnp.float32),
        jnp.zeros((streams, tok_rows), jnp.float32),
        jnp.zeros((streams, tok_rows, head_width), jnp.float32),
    )
    row_peak, denom_sum, numerator = fold_keys(
        start_state,
        lax.all_gather(normed_k, "seq", axis=1, tiled=True),
        lax.all_gather(value, "seq", axis=1, tiled=True),
        score_tokens,
    )
    result = (numerator / denom_sum[:, :, None]).astype(jnp.bfloat16)
    return result


def solution(mesh):
    return jax.shard_map(
        local,
        mesh=mesh,
        in_specs=(
            P("head", "seq", None),
            P("head", "seq", None),
            P("head", "seq", None),
            P(),
            P(),
            P("head", "seq"),
            P("head", None),
            P("head", None, None),
        ),
        out_specs=P("head", "seq", None),
        check_vma=False,
    )
```

profile of v0, /device:TPU:0, one launch (start us, length us, event | category | flops | bytes accessed | tf_op | source)
XLA Modules:
  0.0 82.5 jit_solution(13312469101359836624)
XLA Ops:
  0.0 0.0 copy-start
  0.0 0.0 copy-start.1
  0.0 1.1 %fusion.21 = f32[128]{0:T(128)S(1)} fusion(bf16[5,128,128]{2,1,0:T(8,128)(2,1)} %param.10), kind=kLoop, calls=%fused_computation.34 | loop fusion | flops 245632 | bytes 164352 | tf_op jit(solution)/shard_map/reduce_sum | solution.py:54
  1.1 0.0 copy-done.1
  1.1 0.1 fusion.18
  1.2 15.1 %all-reduce = (f32[128,1]{0,1:T(1,128)S(1)}, f32[128,1]{0,1:T(1,128)S(1)}) all-reduce(f32[128,1]{0,1:T(1,128)S(1)} %get-tuple-element.254, f32[128,1]{0,1:T(1,128)S(1)} %get-tuple-element.253), channel_id=1, replica_groups=mesh['seq'=4,'head'=8] {'head'}, use_global_device_ids=true, to_apply=%region_1.2 | all-reduce | flops 256 | bytes 2048 | tf_op jit(solution)/shard_map/psum | solution.py:56
  16.3 0.0 copy-start.4
  16.4 0.7 copy-done.4
  17.1 0.1 copy.13
  17.2 0.0 copy-done
  17.2 0.7 constant_dynamic-slice_fusion.2
  17.9 0.0 copy-start.5
  17.9 0.7 copy-done.5
  18.6 13.3 %all_gather.9 = s32[5,512]{1,0:T(8,128)S(1)} all-gather(s32[5,128]{1,0:T(8,128)S(1)} %copy-done.5), channel_id=1, replica_groups=mesh['seq'=4,'head'=8] {'seq'}, dimensions={1}, use_global_device_ids=true | all-gather | bytes 12800 | tf_op jit(solution)/shard_map/all_gather | solution.py:63
  31.9 0.0 copy-start.7
  31.9 0.7 copy-done.7
  32.6 0.0 copy-start.6
  32.6 0.1 and_reduce_fusion
  32.6 0.6 copy-done.6
  33.2 0.1 multiply_reduce_fusion
  33.3 9.9 %scatter_custom_fusion = s32[2560]{0:T(1024)S(1)} fusion(s32[2560]{0:T(1024)S(1)} %reshape.74, s32[2560]{0:T(1024)S(1)} %reshape.76, s32[]{:T(128)} %constant.113.clone.1), kind=kCustom, calls=%fused_computation.60 | custom fusion | bytes 10244
  43.3 0.1 convert_reduce_fusion
  43.4 0.1 select_reduce_fusion
  43.5 0.0 copy-start.8
  43.6 0.7 copy-done.8
  44.2 0.2 fusion.24
  44.4 0.0 copy-start.2
  44.4 0.1 fusion.20
  44.5 0.8 copy-done.2
  45.3 0.1 fusion.23
  45.5 0.0 copy-start.3
  45.5 18.1 %all_gather.10 = bf16[5,512,128]{2,1,0:T(8,128)(2,1)S(1)} all-gather(bf16[5,128,128]{2,1,0:T(8,128)(2,1)S(1)} %fusion.20), channel_id=1, replica_groups=mesh['seq'=4,'head'=8] {'seq'}, dimensions={1}, use_global_device_ids=true | all-gather | bytes 819200 | tf_op jit(solution)/shard_map/all_gather | solution.py:123
  63.6 0.0 copy-done.3
  63.6 15.4 %all_gather.11 = bf16[5,512,128]{2,1,0:T(8,128)(2,1)S(1)} all-gather(bf16[5,128,128]{2,1,0:T(8,128)(2,1)S(1)} %copy-done.3), channel_id=1, replica_groups=mesh['seq'=4,'head'=8] {'seq'}, dimensions={1}, use_global_device_ids=true | all-gather | bytes 819200 | tf_op jit(solution)/shard_map/all_gather | solution.py:124
  78.9 2.8 %while.18 = (s32[]{:T(128)}, f32[5,128]{1,0:T(8,128)S(1)}, f32[5,128]{1,0:T(8,128)S(1)}, f32[5,128,128]{2,1,0:T(8,128)S(1)}, s32[5,512]{1,0:T(8,128)S(1)}, /*ind...) while((s32[]{:T(128)}, f32[5,128]{1,0:T(8,128)S(1)}, ...), condition=%wide.region_11.12_spmd.clone, body=%wide.region_8.11_spmd.clone.sunk | while | flops 88732800 | bytes 4168403 | solution.py:36
  78.9 0.4 fusion.48
  79.4 0.3 fusion.49
  79.7 0.2 fusion.50
  79.9 0.4 convolution_add_fusion.2
  80.3 0.4 fusion.48
  80.8 0.3 fusion.49
  81.1 0.2 fusion.50
  81.3 0.4 convolution_add_fusion.2
  81.7 0.8 %divide_convert_fusion = bf16[5,128,128]{2,1,0:T(8,128)(2,1)} fusion(f32[5,128,128]{2,1,0:T(8,128)S(1)} %get-tuple-element.190, f32[5,128]{1,0:T(8,128)S(1)} %get-tuple-element.191), kind=kLoop, calls=%fused_computation.37 | loop fusion | flops 163840 | bytes 494080 | tf_op jit(solution)/shard_map/convert_element_type | solution.py:127
  (27 shorter events, 0.2 us)
Async XLA Ops:
  0.0 17.2 %copy-start = (f32[40,128]{1,0:T(8,128)S(1)}, f32[40,128]{1,0:T(8,128)}, u32[]{:S(2)}) copy-start(f32[40,128]{1,0:T(8,128)} %param.13) | copy-start | bytes 61444
  0.0 1.1 %copy-start.1 = (bf16[5,128,128]{2,1,0:T(8,128)(2,1)S(1)}, bf16[5,128,128]{2,1,0:T(8,128)(2,1)}, u32[]{:S(2)}) copy-start(bf16[5,128,128]{2,1,0:T(8,128)(2,1)} %param.11) | copy-start | bytes 491524
  16.3 0.7 copy-start.4
  17.9 0.7 copy-start.5
  31.9 0.7 copy-start.7
  32.6 0.7 copy-start.6
  43.5 0.7 copy-start.8
  44.4 0.9 %copy-start.2 = (bf16[5,128,128]{2,1,0:T(8,128)(2,1)S(1)}, bf16[5,128,128]{2,1,0:T(8,128)(2,1)}, u32[]{:S(2)}) copy-start(bf16[5,128,128]{2,1,0:T(8,128)(2,1)} %param.10) | copy-start | bytes 491524
  45.5 18.1 %copy-start.3 = (bf16[5,128,128]{2,1,0:T(8,128)(2,1)S(1)}, bf16[5,128,128]{2,1,0:T(8,128)(2,1)}, u32[]{:S(2)}) copy-start(bf16[5,128,128]{2,1,0:T(8,128)(2,1)} %param.12) | copy-start | bytes 491524
where the time goes:
time: 82.9 us; the launch traced here: 82.5 us
  blocking collectives  61.9 us (75%)
  local copies, waits for them, and re-layouts  14.9 us (18%)
  other arithmetic  3.04 us (4%)
  matrix products  2.46 us (3%)
    all_gather x1, blocking collectives, local(): lax.all_gather(normed_k, 'seq', axis=1, tiled=True)  18.1 us
    all_gather x1, blocking collectives, local(): lax.all_gather(value, 'seq', axis=1, tiled=True)  15.4 us
    psum x1, blocking collectives, local(): lax.psum((square_q[:, None] * video_pick, square_k[:, None] * video_pick)...  15.1 us
    unnamed x20, local copies, waits for them, and re-layouts  14 us
    all_gather x1, blocking collectives, local(): full_order = lax.all_gather(order, 'seq', axis=1, tiled=True)  13.3 us

commit v1 on v0

v1 whole, which is shorter than its diff:
```python
import functools
import math

import jax
import jax.numpy as jnp
from jax import lax
from jax.experimental import pallas as pl
from jax.experimental.pallas import tpu as pltpu
from jax.sharding import PartitionSpec as P

BLOCK = 128
LANES = 128
epsilon = 1e-06
far = -1e30

NT = (((1,), (1,)), ((), ()))
NN = (((1,), (0,)), ((), ()))
VMEM = pl.BlockSpec(memory_space=pltpu.VMEM)
SMEM = pl.BlockSpec(memory_space=pltpu.SMEM)


def dot(a, b, dims, precision=None):
    return lax.dot_general(a, b, dims, precision=precision, preferred_element_type=jnp.float32)


def sums_kernel(streams, query, key, order, sums, order_rows):
    rows = sums.shape[0]
    ones = jnp.ones((8, query.shape[2]), jnp.float32)
    totals = []
    for ref in (query, key):
        total = None
        for s in range(streams):
            wide = ref[s].astype(jnp.float32)
            total = wide * wide if total is None else total + wide * wide
        totals.append(dot(ones, total, NT, lax.Precision.HIGHEST))
    row = lax.broadcasted_iota(jnp.int32, totals[0].shape, 0)
    sums[...] = jnp.zeros_like(sums)
    order_rows[...] = jnp.zeros_like(order_rows)
    sums[0:8, :] = jnp.where(row == 0, totals[0], jnp.where(row == 1, totals[1], 0.0))
    order_rows[2 : 2 + streams, :] = order[...].astype(jnp.float32)


def attend_kernel(plan, place, *refs):
    n, streams, half, heads, tok, width = plan
    notes, refs = refs[:n], refs[n:]
    query, key, value, q_gain, k_gain, bounds, table = refs[:7]
    messages = refs[7 : 7 + n - 1]
    out_own, out_peer = refs[7 + n - 1 :]
    rest = streams - 2 * half
    my_seq, first_head = place[0], place[1]
    parity = lax.rem(my_seq, 2)
    norm_width = heads * width
    factor = width ** (-0.5) * math.log2(math.e)
    columns = [notes[m][...].T for m in range(n)]

    def scale(m, row):
        return lax.rsqrt(columns[m][:, row : row + 1] / norm_width + epsilon)

    scale_k = [scale(m, 1) for m in range(n)]
    scale_q = [scale(m, 0) for m in range(2)]
    base = [lax.bitwise_xor(my_seq, m) * tok for m in range(n)]
    lane_pos = lax.broadcasted_iota(jnp.int32, (tok, tok), 0)
    tokens = [(lane_pos + base[m]).astype(jnp.float32) for m in range(n)]

    def normal(rows, scales, gain):
        return (rows.astype(jnp.float32) * scales * gain).astype(jnp.bfloat16)

    def attend(s, q_rows, k_rows, v_rows):
        gain_q = q_gain[pl.ds(first_head + s, 1), :]
        gain_k = k_gain[pl.ds(first_head + s, 1), :]
        count = len(q_rows)
        low = bounds[pl.ds(2 * s, 1), :]
        high = bounds[pl.ds(2 * s + 1, 1), :]
        blocks = []
        for m in range(n):
            wide = jnp.concatenate([tokens[m]] * (bounds.shape[1] // tok), axis=1)
            blocks.append(((low <= wide) & (wide < high)).astype(jnp.float32).astype(jnp.bfloat16))
        place_block = jnp.concatenate(blocks, axis=0)
        hits = []
        for m in range(n):
            row = []
            for j in range(n):
                ids = notes[j][pl.ds(2 + s, 1), :]
                row.append((tokens[m] == ids).astype(jnp.float32).astype(jnp.bfloat16))
            hits.append(jnp.concatenate(row, axis=1))
        hit = jnp.concatenate(hits, axis=0)
        member = dot(hit, place_block, NN).astype(jnp.bfloat16)
        bias = dot(member[: count * tok], table[s], NN).astype(jnp.bfloat16)
        normed_q = jnp.concatenate([normal(q_rows[m], scale_q[m], gain_q) for m in range(count)], axis=0)
        normed_k = jnp.concatenate([normal(k_rows[m], scale_k[m], gain_k) for m in range(n)], axis=0)
        scores = dot(
            jnp.concatenate([normed_q, bias], axis=1), jnp.concatenate([normed_k, member], axis=1), NT
        )
        peak = jnp.max(scores, axis=1, keepdims=True)
        weights = jnp.exp2((scores - peak) * factor)
        denom = jnp.sum(weights, axis=1, keepdims=True)
        mixed = dot(weights.astype(jnp.bfloat16), jnp.concatenate(v_rows, axis=0), NN)
        return (mixed / denom).astype(jnp.bfloat16)

    for i in range(half):
        s = parity * half + i
        q_rows = [query[s], messages[0][2 * (half + rest) + i]]
        k_rows = [key[s]] + [messages[m - 1][i] for m in range(1, n)]
        v_rows = [value[s]] + [messages[m - 1][half + rest + i] for m in range(1, n)]
        out = attend(s, q_rows, k_rows, v_rows)
        out_own[i] = out[:tok]
        out_peer[i] = out[tok:]
    for i in range(rest):
        s = 2 * half + i
        k_rows = [key[s]] + [messages[m - 1][half + i] for m in range(1, n)]
        v_rows = [value[s]] + [messages[m - 1][half + rest + half + i] for m in range(1, n)]
        out_own[half + i] = attend(s, [query[s]], k_rows, v_rows)


def local(n, query, key, value, q_gain, k_gain, order, cluster_rows, block_map):
    streams, tok, width = query.shape
    heads = q_gain.shape[0]
    seq_rank = lax.axis_index("seq")
    head_rank = lax.axis_index("head")
    half = streams // 2
    rest = streams - 2 * half
    block_count = block_map.shape[2]
    clusters = cluster_rows.shape[1]
    blocks_per = block_count // clusters
    padded = -(-block_count // LANES) * LANES
    parity = seq_rank % 2

    def exchange(rows, m):
        return lax.ppermute(rows, "seq", [(i, i ^ m) for i in range(n)])

    def parcel(rows, member):
        return [lax.dynamic_slice_in_dim(rows, member * half, half, 0), rows[2 * half :]]

    messages = {}
    for m in reversed(range(1, n)):
        member = parity ^ (m & 1)
        parts = parcel(key, member) + parcel(value, member)
        if m == 1:
            parts += parcel(query, member)[:1]
        messages[m] = exchange(jnp.concatenate(parts, axis=0), m)

    note_rows = -(-(streams + 2) // 8) * 8
    sums, order_rows = pl.pallas_call(
        functools.partial(sums_kernel, streams),
        out_shape=[jax.ShapeDtypeStruct((note_rows, tok), jnp.float32)] * 2,
        in_specs=[VMEM] * 3,
        out_specs=[VMEM] * 2,
    )(query, key, order)
    head_size = lax.axis_size("head")
    step = 1
    while step * streams < heads:
        sums = sums + lax.ppermute(sums, "head", [(i, i ^ step) for i in range(head_size)])
        step *= 2
    note = sums + order_rows
    notes = [note] + [None] * (n - 1)
    for m in reversed(range(1, n)):
        notes[m] = exchange(note, m)

    start = jnp.cumsum(cluster_rows, axis=1, dtype=jnp.int32) - cluster_rows
    step_rows = jnp.arange(blocks_per, dtype=jnp.int32) * BLOCK
    low = start[:, :, None] + step_rows
    high = jnp.minimum(low + BLOCK, (start + cluster_rows)[:, :, None])
    bounds = jnp.stack([low.reshape(streams, block_count), high.reshape(streams, block_count)], axis=1)
    bounds = jnp.pad(
        bounds.reshape(2 * streams, block_count).astype(jnp.float32), ((0, 0), (0, padded - block_count))
    )
    allowed = (block_map == 1) | jnp.eye(block_count, dtype=bool)
    pad = (0, padded - block_count)
    table = jnp.pad(jnp.where(allowed, 0.0, far).astype(jnp.bfloat16), ((0, 0), pad, pad))

    place = jnp.stack([seq_rank, (head_rank * streams) % heads]).astype(jnp.int32)
    own, peer = pl.pallas_call(
        functools.partial(attend_kernel, (n, streams, half, heads, tok, width)),
        out_shape=[
            jax.ShapeDtypeStruct((half + rest, tok, width), jnp.bfloat16),
            jax.ShapeDtypeStruct((half, tok, width), jnp.bfloat16),
        ],
        in_specs=[SMEM] + [VMEM] * (n + 7 + n - 1),
        out_specs=[VMEM] * 2,
        compiler_params=pltpu.CompilerParams(vmem_limit_bytes=48 * 1024 * 1024),
    )(place, *notes, query, key, value, q_gain, k_gain, bounds, table, *[messages[m] for m in range(1, n)])
    theirs = exchange(peer, 1)
    first = jnp.where(parity == 0, own[:half], theirs)
    second = jnp.where(parity == 0, theirs, own[:half])
    return jnp.concatenate([first, second, own[half:]], axis=0)


def solution(mesh):
    return jax.shard_map(
        functools.partial(local, mesh.shape["seq"]),
        mesh=mesh,
        in_specs=(
            P("head", "seq", None),
            P("head", "seq", None),
            P("head", "seq", None),
            P(),
            P(),
            P("head", "seq"),
            P("head", None),
            P("head", None, None),
        ),
        out_specs=P("head", "seq", None),
        check_vma=False,
    )
```

time: 82.9 us -> 36.6 us (0.44)
  blocking collectives: 61.9 us -> 0 us
  starting transfers between devices: 0 us -> 15.9 us
  local copies, waits for them, and re-layouts: 14.9 us -> 2.88 us
  waiting for transfers between devices: 0 us -> 11.8 us
  Pallas kernels: 0 us -> 4.69 us
  matrix products: 2.46 us -> 0 us
  other arithmetic: 3.04 us -> 0.98 us
    all_gather x3 -> x0, blocking collectives: 46.8 us -> none  [the longest x1 18.1 us: local(): lax.all_gather(normed_k, 'seq', axis=1, tiled=True)]
    ppermute x0 -> x10, starting transfers between devices: none -> 15.9 us  [the longest x7 12.8 us: exchange(): return lax.ppermute(rows, 'seq', [(i, i ^ m) for i in range(n)])]
    psum x1 -> x0, blocking collectives: 15.1 us -> none  [local(): lax.psum((square_q[:, None] * video_pick, square_k[:, None] * video_pick)...]
    unnamed x20, local copies, waits for them, and re-layouts: 14 us -> 1.02 us
    ppermute x0 -> x10, waiting for transfers between devices: none -> 11.8 us  [the longest x7 6.52 us: exchange(): return lax.ppermute(rows, 'seq', [(i, i ^ m) for i in range(n)])]
    pallas_call x0 -> x2, Pallas kernels: none -> 4.69 us  [the longest x1 2.75 us: local(): pl.pallas_call(functools.partial(attend_kernel, (n, streams, half, heads,...]
    dot_general x7 -> x0, matrix products: 2.46 us -> none  [the longest x2 0.87 us: score_tokens(): jnp.einsum('stm,skm->stk', row_table, (key_ids[:, :, None] == block_axis)...]
    reduce_sum x6 -> x0, other arithmetic: 1.71 us -> none  [the longest x1 1.07 us: local(): square_q = jnp.sum(jnp.square(query.astype(jnp.float32)), axis=(0, 2))]
  transfers between devices with their start and end apart: 0 -> 10, of which waited for: 0 -> 6; matrix products, arithmetic and copies ran while one was open for 0% -> 4% of each run, Pallas kernels for 0% -> 5%
where the time goes in v1:
time: 36.6 us; the launch traced here: 36.4 us
  starting transfers between devices  15.9 us (43%)
  waiting for transfers between devices  11.8 us (32%)
  Pallas kernels  4.69 us (13%)
  local copies, waits for them, and re-layouts  2.88 us (8%)
  other arithmetic  0.98 us (3%)
    ppermute x7, starting transfers between devices, exchange(): return lax.ppermute(rows, 'seq', [(i, i ^ m) for i in range(n)])  12.8 us
    ppermute x7, waiting for transfers between devices, exchange(): return lax.ppermute(rows, 'seq', [(i, i ^ m) for i in range(n)])  6.52 us
    ppermute x3, waiting for transfers between devices, local(): lax.ppermute(sums, 'head', [(i, i ^ step) for i in range(head_size)])  5.27 us
    ppermute x3, starting transfers between devices, local(): lax.ppermute(sums, 'head', [(i, i ^ step) for i in range(head_size)])  3.08 us
    pallas_call x1, Pallas kernels, local(): pl.pallas_call(functools.partial(attend_kernel, (n, streams, half, heads,...  2.75 us
    pallas_call x1, Pallas kernels, local(): pl.pallas_call(functools.partial(sums_kernel, streams), out_shape=[jax.Sh...  1.93 us
    unnamed x20, local copies, waits for them, and re-layouts  1.02 us
    concatenate x1, local copies, waits for them, and re-layouts, local(): messages[m] = exchange(jnp.concatenate(parts, axis=0), m)  0.85 us
  transfers between devices with their start and end apart: 10, of which 6 were waited for; matrix products, arithmetic and copies ran while one was open for 4% of the time, Pallas kernels for 5%

profile of v1, /device:TPU:0, one launch (start us, length us, event | category | flops | bytes accessed | tf_op | source)
XLA Modules:
  0.0 36.4 jit_solution(5951048708100378652)
XLA Ops:
  0.0 0.0 copy-start.2
  0.0 0.9 %constant_dynamic-update-slice_fusion.3 = (bf16[8,128,128]{2,1,0:T(8,128)(2,1)S(1)}, bf16[2,128,128]{2,1,0:T(8,128)(2,1)S(1)}, bf16[2,128,128]{2,1,0:T(8,128)(2,1)S(1)}) fusion(bf16[5,128,128]{2,1,0:T(8,128)(2,1)} %refs_5_.1, s32[]{:T(128)S(6)} %select_n.42, s32[]{:T(128)S(6)} %select_n.43), kind=kLoop, calls=%fused_computation.14 | loop fusion | bytes 327688
  0.9 0.8 %fusion.2 = (bf16[1,128,128]{2,1,0:T(8,128)(2,1)S(1)}, bf16[8,128,128]{2,1,0:T(8,128)(2,1)S(1)}) fusion(bf16[5,128,128]{2,1,0:T(8,128)(2,1)} %refs_5_.1, bf16[8,128,128]{2,1,0:T(8,128)(2,1)S(1)} %get-tuple-element.15), kind=kLoop, calls=%fused_computation.26 | loop fusion | bytes 98304 | tf_op jit(solution)/shard_map/slice | solution.py:132
  1.7 0.0 copy-done.2
  1.8 0.1 pad_maximum_fusion
  1.8 4.1 %collective-permute-start.7 = (bf16[6,128,128]{2,1,0:T(8,128)(2,1)S(1)}, bf16[6,128,128]{2,1,0:T(8,128)(2,1)S(1)}, u32[]{:S(2)}, u32[]{:S(2)}) collective-permute-start(bf16[6,128,128]{2,1,0:T(8,128)(2,1)S(1)} %get-tuple-element.26), channel_id=1, source_target_pairs={{0,16},{8,24},{16,0},{24,8},{1,17},{9,25},{17,1},{25,9},{2,18},{10... | collective-permute-start | bytes 589832 | tf_op jit(solution)/shard_map/ppermute | solution.py:129
  5.9 1.3 %collective-permute-start.8 = (bf16[6,128,128]{2,1,0:T(8,128)(2,1)S(1)}, bf16[6,128,128]{2,1,0:T(8,128)(2,1)S(1)}, u32[]{:S(2)}, u32[]{:S(2)}) collective-permute-start(bf16[6,128,128]{2,1,0:T(8,128)(2,1)S(1)} %get-tuple-element.25), channel_id=1, source_target_pairs={{0,24},{8,16},{16,8},{24,0},{1,25},{9,17},{17,9},{25,1},{2,26},{10... | collective-permute-start | bytes 589832 | tf_op jit(solution)/shard_map/ppermute | solution.py:129
  7.3 0.9 %dynamic-slice_dynamic-update-slice_fusion = bf16[8,128,128]{2,1,0:T(8,128)(2,1)S(1)} fusion(bf16[8,128,128]{2,1,0:T(8,128)(2,1)S(1)} %get-tuple-element.24, bf16[5,128,128]{2,1,0:T(8,128)(2,1)} %refs_4_.1, s32[]{:T(128)S(6)} %select_n.42), kind=kLoop, calls=%fused_computation.7 | loop fusion | bytes 131076 | tf_op jit(solution)/shard_map/concatenate | solution.py:140
  8.1 0.0 copy-start.5
  8.2 0.3 collective-permute-start.6
  8.5 1.9 %shard_map.82 = (f32[8,128]{1,0:T(8,128)}, f32[8,128]{1,0:T(8,128)}) custom-call(bf16[5,128,128]{2,1,0:T(8,128)(2,1)} %refs_4_.1, bf16[5,128,128]{2,1,0:T(8,128)(2,1)} %refs_5_.1, s32[5,128]{1,0:T(8,128)} %order.1), custom_call_target="tpu_custom_call" | custom-call | tf_op jit(solution)/shard_map/pallas_call | solution.py:143
  10.4 0.0 collective-permute-start
  10.4 0.0 copy-done.5
  10.4 0.0 copy-start.7
  10.4 0.0 copy-start.6
  10.4 0.0 copy-start.4
  10.5 1.3 %collective-permute-done = f32[8,128]{1,0:T(8,128)S(1)} collective-permute-done((f32[8,128]{1,0:T(8,128)}, f32[8,128]{1,0:T(8,128)S(1)}, u32[]{:S(2)}, u32[]{:S(2)}) %collective-permute-start) | collective-permute-done | bytes 4128 | tf_op jit(solution)/shard_map/ppermute | solution.py:152
  11.8 0.0 copy-done.7
  11.8 0.0 copy-start.3
  11.8 1.6 %collective-permute-start.1 = (f32[8,128]{1,0:T(8,128)S(1)}, f32[8,128]{1,0:T(8,128)S(1)}, u32[]{:S(2)}, u32[]{:S(2)}) collective-permute-start(f32[8,128]{1,0:T(8,128)S(1)} %add.80), channel_id=1, source_target_pairs={{0,2},{1,3},{2,0},{3,1},{4,6},{5,7},{6,4},{7,5},{8,10},{9,11},{10,... | collective-permute-start | bytes 12296 | tf_op jit(solution)/shard_map/ppermute | solution.py:152
  13.3 0.0 copy-done.6
  13.4 0.0 copy-start.8
  13.4 0.0 copy-start
  13.4 0.0 copy-start.1
  13.4 0.1 add.87
  13.5 2.0 %collective-permute-done.1 = f32[8,128]{1,0:T(8,128)S(1)} collective-permute-done((f32[8,128]{1,0:T(8,128)S(1)}, f32[8,128]{1,0:T(8,128)S(1)}, u32[]{:S(2)}, u32[]{:S(2)}) %collective-permute-start.1) | collective-permute-done | bytes 4128 | tf_op jit(solution)/shard_map/ppermute | solution.py:152
  15.5 1.5 %collective-permute-start.2 = (f32[8,128]{1,0:T(8,128)S(1)}, f32[8,128]{1,0:T(8,128)S(1)}, u32[]{:S(2)}, u32[]{:S(2)}) collective-permute-start(f32[8,128]{1,0:T(8,128)S(1)} %add.81), channel_id=1, source_target_pairs={{0,4},{1,5},{2,6},{3,7},{4,0},{5,1},{6,2},{7,3},{8,12},{9,13},{10,... | collective-permute-start | bytes 12296 | tf_op jit(solution)/shard_map/ppermute | solution.py:152
  17.0 0.1 bitcast_add_fusion
  17.1 2.0 %collective-permute-done.2 = f32[8,128]{1,0:T(8,128)S(1)} collective-permute-done((f32[8,128]{1,0:T(8,128)S(1)}, f32[8,128]{1,0:T(8,128)S(1)}, u32[]{:S(2)}, u32[]{:S(2)}) %collective-permute-start.2) | collective-permute-done | bytes 4128 | tf_op jit(solution)/shard_map/ppermute | solution.py:152
  19.1 0.0 copy-done.8
  19.1 1.8 %collective-permute-start.3 = (f32[8,128]{1,0:T(8,128)S(1)}, f32[8,128]{1,0:T(8,128)S(1)}, u32[]{:S(2)}, u32[]{:S(2)}) collective-permute-start(f32[8,128]{1,0:T(8,128)S(1)} %add_add_fusion.refs_0_), channel_id=1, source_target_pairs={{0,8},{8,0},{16,24},{24,16},{1,9},{9,1},{17,25},{25,17},{2,10},{10... | collective-permute-start | bytes 12296 | tf_op jit(solution)/shard_map/ppermute | solution.py:129
  20.9 1.7 %collective-permute-start.4 = (f32[8,128]{1,0:T(8,128)S(1)}, f32[8,128]{1,0:T(8,128)S(1)}, u32[]{:S(2)}, u32[]{:S(2)}) collective-permute-start(f32[8,128]{1,0:T(8,128)S(1)} %add_add_fusion.refs_0_), channel_id=1, source_target_pairs={{0,16},{8,24},{16,0},{24,8},{1,17},{9,25},{17,1},{25,9},{2,18},{10... | collective-permute-start | bytes 12296 | tf_op jit(solution)/shard_map/ppermute | solution.py:129
  22.6 0.6 %collective-permute-done.3.refs_1_ = f32[8,128]{1,0:T(8,128)S(1)} collective-permute-done((f32[8,128]{1,0:T(8,128)S(1)}, f32[8,128]{1,0:T(8,128)S(1)}, u32[]{:S(2)}, u32[]{:S(2)}) %collective-permute-start.3) | collective-permute-done | bytes 4128 | tf_op jit(solution)/shard_map/ppermute | solution.py:129
  23.1 3.5 %collective-permute-start.5 = (f32[8,128]{1,0:T(8,128)S(1)}, f32[8,128]{1,0:T(8,128)S(1)}, u32[]{:S(2)}, u32[]{:S(2)}) collective-permute-start(f32[8,128]{1,0:T(8,128)S(1)} %add_add_fusion.refs_0_), channel_id=1, source_target_pairs={{0,24},{8,16},{16,8},{24,0},{1,25},{9,17},{17,9},{25,1},{2,26},{10... | collective-permute-start | bytes 12296 | tf_op jit(solution)/shard_map/ppermute | solution.py:129
  26.6 0.1 pad_add_fusion.place
  26.7 0.1 copy.10
  26.8 0.0 collective-permute-done.4.refs_2_
  26.8 1.7 %collective-permute-done.5.refs_3_ = f32[8,128]{1,0:T(8,128)S(1)} collective-permute-done((f32[8,128]{1,0:T(8,128)S(1)}, f32[8,128]{1,0:T(8,128)S(1)}, u32[]{:S(2)}, u32[]{:S(2)}) %collective-permute-start.5) | collective-permute-done | bytes 4128 | tf_op jit(solution)/shard_map/ppermute | solution.py:129
  28.5 0.0 collective-permute-done.7.refs_12_
  28.5 0.0 collective-permute-done.8.refs_13_
  28.5 0.0 collective-permute-done.6.refs_11_
  28.5 0.0 copy-done.4
  28.6 0.0 copy-done.3
  28.6 0.0 copy-done
  28.6 0.0 copy-done.1
  28.6 2.8 %shard_map.83 = (bf16[3,128,128]{2,1,0:T(8,128)(2,1)S(1)}, bf16[2,128,128]{2,1,0:T(8,128)(2,1)S(1)}) custom-call(s32[2]{0:T(128)S(1)} %pad_add_fusion.place, f32[8,128]{1,0:T(8,128)S(1)} %add_add_fusion.refs_0_, f32[8,128]{1,0:T(8,128)S(1)} %collective-permute-done.3.refs_1_, f32[8,128]{1,0:T(8,128)S(1)} %collective-permute-done.4.refs_2_, ...), custom_call_target="tpu_custom_call" | custom-call | tf_op jit(solution)/shard_map/pallas_call | solution.py:172
  31.3 0.1 collective-permute-start.9
  31.4 4.2 %collective-permute-done.9 = bf16[2,128,128]{2,1,0:T(8,128)(2,1)S(1)} collective-permute-done((bf16[2,128,128]{2,1,0:T(8,128)(2,1)S(1)}, bf16[2,128,128]{2,1,0:T(8,128)(2,1)S(1)}, u32[]{:S(2)}, u32[]{:S(2)}) %collective-permute-start.9) | collective-permute-done | bytes 65568 | tf_op jit(solution)/shard_map/ppermute | solution.py:129
  35.7 0.7 %pad_maximum_fusion.4 = bf16[5,128,128]{2,1,0:T(8,128)(2,1)} fusion(bf16[1,128,128]{2,1,0:T(8,128)(2,1)S(1)} %slice.20, bf16[2,128,128]{2,1,0:T(8,128)(2,1)S(1)} %get-tuple-element.18, bf16[2,128,128]{2,1,0:T(8,128)(2,1)S(1)} %get-tuple-element.17), kind=kLoop, calls=%fused_computation.6 | loop fusion | flops 163840 | bytes 327680 | tf_op jit(solution)/shard_map/concatenate | solution.py:185
  (19 shorter events, 0.2 us)
Async XLA Ops:
  0.0 1.7 %copy-start.2 = (bf16[5,128,128]{2,1,0:T(8,128)(2,1)S(1)}, bf16[5,128,128]{2,1,0:T(8,128)(2,1)}, u32[]{:S(2)}) copy-start(bf16[5,128,128]{2,1,0:T(8,128)(2,1)} %refs_6_.1) | copy-start | bytes 491524
  1.8 26.7 %collective-permute-start.7 = (bf16[6,128,128]{2,1,0:T(8,128)(2,1)S(1)}, bf16[6,128,128]{2,1,0:T(8,128)(2,1)S(1)}, u32[]{:S(2)}, u32[]{:S(2)}) collective-permute-start(bf16[6,128,128]{2,1,0:T(8,128)(2,1)S(1)} %get-tuple-element.26), channel_id=1, source_target_pairs={{0,16},{8,24},{16,0},{24,8},{1,17},{9,25},{17,1},{25,9},{2,18},{10... | collective-permute-start | bytes 589832 | tf_op jit(solution)/shard_map/ppermute | solution.py:129
  5.9 22.6 %collective-permute-start.8 = (bf16[6,128,128]{2,1,0:T(8,128)(2,1)S(1)}, bf16[6,128,128]{2,1,0:T(8,128)(2,1)S(1)}, u32[]{:S(2)}, u32[]{:S(2)}) collective-permute-start(bf16[6,128,128]{2,1,0:T(8,128)(2,1)S(1)} %get-tuple-element.25), channel_id=1, source_target_pairs={{0,24},{8,16},{16,8},{24,0},{1,25},{9,17},{17,9},{25,1},{2,26},{10... | collective-permute-start | bytes 589832 | tf_op jit(solution)/shard_map/ppermute | solution.py:129
  8.1 2.3 %copy-start.5 = (s32[5,8,8]{2,1,0:T(8,128)S(1)}, s32[5,8,8]{2,1,0:T(8,128)}, u32[]{:S(2)}) copy-start(s32[5,8,8]{2,1,0:T(8,128)} %param.15) | copy-start | bytes 3844
  8.2 20.4 %collective-permute-start.6 = (bf16[8,128,128]{2,1,0:T(8,128)(2,1)S(1)}, bf16[8,128,128]{2,1,0:T(8,128)(2,1)S(1)}, u32[]{:S(2)}, u32[]{:S(2)}) collective-permute-start(bf16[8,128,128]{2,1,0:T(8,128)(2,1)S(1)} %dynamic-slice_dynamic-update-slice_fusion), channel_id=1, source_target_pairs={{0,8},{8,0},{16,24},{24,16},{1,9},{9,1},{17,25},{25,17},{2,10},{10... | collective-permute-start | bytes 786440 | tf_op jit(solution)/shard_map/ppermute | solution.py:129
  10.4 1.4 %collective-permute-start = (f32[8,128]{1,0:T(8,128)}, f32[8,128]{1,0:T(8,128)S(1)}, u32[]{:S(2)}, u32[]{:S(2)}) collective-permute-start(f32[8,128]{1,0:T(8,128)} %get-tuple-element.9), channel_id=1, source_target_pairs={{0,1},{1,0},{2,3},{3,2},{4,5},{5,4},{6,7},{7,6},{8,9},{9,8},{10,11... | collective-permute-start | bytes 12296 | tf_op jit(solution)/shard_map/ppermute | solution.py:152
  10.4 1.4 %copy-start.7 = (f32[8,128]{1,0:T(8,128)S(1)}, f32[8,128]{1,0:T(8,128)}, u32[]{:S(2)}) copy-start(f32[8,128]{1,0:T(8,128)} %get-tuple-element.9) | copy-start | bytes 12292
  10.4 2.9 %copy-start.6 = (s32[5,4]{0,1:T(4,128)S(1)}, s32[5,4]{0,1:T(4,128)}, u32[]{:S(2)}) copy-start(s32[5,4]{0,1:T(4,128)} %param.14) | copy-start | bytes 244
  10.4 18.1 %copy-start.4 = (f32[40,128]{1,0:T(8,128)S(1)}, f32[40,128]{1,0:T(8,128)}, u32[]{:S(2)}) copy-start(f32[40,128]{1,0:T(8,128)} %refs_8_.1) | copy-start | bytes 61444
  11.8 16.8 %copy-start.3 = (f32[40,128]{1,0:T(8,128)S(1)}, f32[40,128]{1,0:T(8,128)}, u32[]{:S(2)}) copy-start(f32[40,128]{1,0:T(8,128)} %refs_7_.1) | copy-start | bytes 61444
  11.8 3.7 %collective-permute-start.1 = (f32[8,128]{1,0:T(8,128)S(1)}, f32[8,128]{1,0:T(8,128)S(1)}, u32[]{:S(2)}, u32[]{:S(2)}) collective-permute-start(f32[8,128]{1,0:T(8,128)S(1)} %add.80), channel_id=1, source_target_pairs={{0,2},{1,3},{2,0},{3,1},{4,6},{5,7},{6,4},{7,5},{8,10},{9,11},{10,... | collective-permute-start | bytes 12296 | tf_op jit(solution)/shard_map/ppermute | solution.py:152
  13.4 5.7 %copy-start.8 = (f32[8,128]{1,0:T(8,128)S(1)}, f32[8,128]{1,0:T(8,128)}, u32[]{:S(2)}) copy-start(f32[8,128]{1,0:T(8,128)} %get-tuple-element.10) | copy-start | bytes 12292
  13.4 15.2 %copy-start = (bf16[5,128,128]{2,1,0:T(8,128)(2,1)S(1)}, bf16[5,128,128]{2,1,0:T(8,128)(2,1)}, u32[]{:S(2)}) copy-start(bf16[5,128,128]{2,1,0:T(8,128)(2,1)} %refs_5_.1) | copy-start | bytes 491524
  13.4 15.2 %copy-start.1 = (bf16[5,128,128]{2,1,0:T(8,128)(2,1)S(1)}, bf16[5,128,128]{2,1,0:T(8,128)(2,1)}, u32[]{:S(2)}) copy-start(bf16[5,128,128]{2,1,0:T(8,128)(2,1)} %refs_4_.1) | copy-start | bytes 491524
  15.5 3.6 %collective-permute-start.2 = (f32[8,128]{1,0:T(8,128)S(1)}, f32[8,128]{1,0:T(8,128)S(1)}, u32[]{:S(2)}, u32[]{:S(2)}) collective-permute-start(f32[8,128]{1,0:T(8,128)S(1)} %add.81), channel_id=1, source_target_pairs={{0,4},{1,5},{2,6},{3,7},{4,0},{5,1},{6,2},{7,3},{8,12},{9,13},{10,... | collective-permute-start | bytes 12296 | tf_op jit(solution)/shard_map/ppermute | solution.py:152
  19.1 4.1 %collective-permute-start.3 = (f32[8,128]{1,0:T(8,128)S(1)}, f32[8,128]{1,0:T(8,128)S(1)}, u32[]{:S(2)}, u32[]{:S(2)}) collective-permute-start(f32[8,128]{1,0:T(8,128)S(1)} %add_add_fusion.refs_0_), channel_id=1, source_target_pairs={{0,8},{8,0},{16,24},{24,16},{1,9},{9,1},{17,25},{25,17},{2,10},{10... | collective-permute-start | bytes 12296 | tf_op jit(solution)/shard_map/ppermute | solution.py:129
  20.9 5.9 %collective-permute-start.4 = (f32[8,128]{1,0:T(8,128)S(1)}, f32[8,128]{1,0:T(8,128)S(1)}, u32[]{:S(2)}, u32[]{:S(2)}) collective-permute-start(f32[8,128]{1,0:T(8,128)S(1)} %add_add_fusion.refs_0_), channel_id=1, source_target_pairs={{0,16},{8,24},{16,0},{24,8},{1,17},{9,25},{17,1},{25,9},{2,18},{10... | collective-permute-start | bytes 12296 | tf_op jit(solution)/shard_map/ppermute | solution.py:129
  23.1 5.4 %collective-permute-start.5 = (f32[8,128]{1,0:T(8,128)S(1)}, f32[8,128]{1,0:T(8,128)S(1)}, u32[]{:S(2)}, u32[]{:S(2)}) collective-permute-start(f32[8,128]{1,0:T(8,128)S(1)} %add_add_fusion.refs_0_), channel_id=1, source_target_pairs={{0,24},{8,16},{16,8},{24,0},{1,25},{9,17},{17,9},{25,1},{2,26},{10... | collective-permute-start | bytes 12296 | tf_op jit(solution)/shard_map/ppermute | solution.py:129
  31.3 4.3 %collective-permute-start.9 = (bf16[2,128,128]{2,1,0:T(8,128)(2,1)S(1)}, bf16[2,128,128]{2,1,0:T(8,128)(2,1)S(1)}, u32[]{:S(2)}, u32[]{:S(2)}) collective-permute-start(bf16[2,128,128]{2,1,0:T(8,128)(2,1)S(1)} %get-tuple-element.12), channel_id=1, source_target_pairs={{0,8},{8,0},{16,24},{24,16},{1,9},{9,1},{17,25},{25,17},{2,10},{10... | collective-permute-start | bytes 196616 | tf_op jit(solution)/shard_map/ppermute | solution.py:129

commit v2 on v1

v2 whole, which is shorter than its diff:
```python
import functools
import math

import jax
import jax.numpy as jnp
from jax import lax
from jax.experimental import pallas as pl
from jax.experimental.pallas import tpu as pltpu
from jax.sharding import PartitionSpec as P

BLOCK = 128
LANES = 128
epsilon = 1e-06
far = -1e30
weight = 20_000_000_000

NT = (((1,), (1,)), ((), ()))
NN = (((1,), (0,)), ((), ()))
VMEM = pl.BlockSpec(memory_space=pltpu.VMEM)
ANY = pl.BlockSpec(memory_space=pl.ANY)
limit = pltpu.CompilerParams(vmem_limit_bytes=48 * 1024 * 1024)


def dot(a, b, dims, precision=None):
    return lax.dot_general(a, b, dims, precision=precision, preferred_element_type=jnp.float32)


def one_hot(hit):
    return hit.astype(jnp.float32).astype(jnp.bfloat16)


def call(body, shapes, args, cost=None, **more):
    return pl.pallas_call(
        body,
        out_shape=shapes,
        in_specs=[VMEM] * len(args),
        out_specs=jax.tree.map(lambda _: VMEM, shapes),
        compiler_params=limit,
        cost_estimate=cost and pl.CostEstimate(flops=cost, bytes_accessed=0, transcendentals=0),
        **more,
    )(*args)


def prep_kernel(half, tail, query, key, value, order, note, same, other, plain, q_in, k_in, order_in, sems):
    streams, tok, width = query.shape
    rest = streams - 2 * half
    parity = lax.rem(lax.axis_index("seq"), 2)
    pairs = [(query, q_in), (key, k_in), (order, order_in)]
    for target, side in ((plain, 1 - parity), (same, parity), (other, 1 - parity)):
        for i in range(half):
            pairs.append((value.at[side * half + i], target.at[pl.ds(i * tok, tok)]))
        if target is plain:
            continue
        for i, s in enumerate(range(2 * half, streams)):
            for j, ref in enumerate((value, key)):
                pairs.append((ref.at[s], target.at[pl.ds((half + 2 * i + j) * tok, tok)]))
        if target is other:
            for i in range(half):
                pairs.append((query.at[side * half + i], target.at[pl.ds((half + 2 * rest + i) * tok, tok)]))
    copies = [pltpu.make_async_copy(src, dst, sems.at[i]) for i, (src, dst) in enumerate(pairs)]
    for copy in copies:
        copy.start()
    ones = jnp.ones((8, width), jnp.float32)
    totals = []
    for copy, ref in zip(copies, (q_in, k_in)):
        copy.wait()
        total = None
        for s in range(streams):
            wide = ref[s].astype(jnp.float32)
            total = wide * wide if total is None else total + wide * wide
        totals.append(dot(ones, total, NT, lax.Precision.HIGHEST))
    row = lax.broadcasted_iota(jnp.int32, totals[0].shape, 0)
    note[...] = jnp.where(row == 0, totals[0], jnp.where(row == 1, totals[1], 0.0))
    copies[2].wait()
    row = lax.broadcasted_iota(jnp.int32, (tail, tok), 0)
    for side, targets in ((1 - parity, (plain, other)), (parity, (same,))):
        rows = jnp.zeros((tail, tok), jnp.float32)
        for i in range(streams - half):
            s = side * half + i if i < half else half + i
            ids = order_in[pl.ds(s, 1), :].astype(jnp.float32)
            high = jnp.floor(ids / tok)
            rows = jnp.where(row == 2 * i, high, jnp.where(row == 2 * i + 1, ids - high * tok, rows))
        for target in targets:
            target[target.shape[0] - tail :, :] = rows.astype(jnp.bfloat16)
    for copy in copies[3:]:
        copy.wait()


def norm_kernel(half, heads, totals, query, key, q_gain, k_gain, same, other, own):
    streams, tok, width = query.shape
    kept = streams - half
    parity = lax.rem(lax.axis_index("seq"), 2)
    first_head = lax.rem(lax.axis_index("head") * streams, heads)
    scales = lax.rsqrt(totals[...] / (heads * width) + epsilon)
    columns = scales.T

    def normal(ref, gains, s, column):
        gain = gains[pl.ds(first_head + s, 1), :]
        return (ref[s].astype(jnp.float32) * columns[:, column : column + 1] * gain).astype(jnp.bfloat16)

    row = lax.broadcasted_iota(jnp.int32, (16, tok), 0)
    rows = jnp.zeros((16, tok), jnp.float32)
    for j in range(2):
        piece = scales[j : j + 1, :]
        for i in range(3):
            cut = piece.astype(jnp.bfloat16).astype(jnp.float32)
            rows = jnp.where(row == 3 * j + i, cut, rows)
            piece = piece - cut
    rows = rows.astype(jnp.bfloat16)
    for target in (same, other):
        target[target.shape[0] - 16 :, :] = rows
    for i in range(half):
        mine, theirs = parity * half + i, (1 - parity) * half + i
        at = pl.ds(i * tok, tok)
        same[at, :] = normal(key, k_gain, mine, 1)
        other[at, :] = normal(key, k_gain, theirs, 1)
        own[at, :] = normal(query, q_gain, mine, 0)
    for s in range(2 * half, streams):
        own[pl.ds((s - half) * tok, tok), :] = normal(query, q_gain, s, 0)
        own[pl.ds((kept + s - 2 * half) * tok, tok), :] = normal(key, k_gain, s, 1)


def table_kernel(half, i, block_map, table):
    count = block_map.shape[1]
    s = lax.rem(lax.axis_index("seq"), 2) * half + i if i < half else half + i
    row = lax.broadcasted_iota(jnp.int32, (count, count), 0)
    column = lax.broadcasted_iota(jnp.int32, (count, count), 1)
    table[...] = jnp.zeros_like(table)
    table[:count, :count] = jnp.where((block_map[s] == 1) | (row == column), 0.0, far)


def blocks_kernel(half, i, bounds, table, *refs):
    notes, member, bias_out = refs[:-2], refs[-2], refs[-1]
    n = len(notes)
    tok = notes[0].shape[1]
    padded = bounds.shape[1]
    tail = notes[0].shape[0] % tok
    my_seq = lax.axis_index("seq")
    s = lax.rem(my_seq, 2) * half + i if i < half else half + i
    row_in = lax.broadcasted_iota(jnp.int32, (tok, LANES), 0)
    tokens = [(row_in + lax.bitwise_xor(my_seq, m) * tok).astype(jnp.float32) for m in range(n)]
    low = bounds[pl.ds(2 * s, 1), :]
    high = bounds[pl.ds(2 * s + 1, 1), :]
    blocks = []
    ids = []
    for m in range(n):
        wide = jnp.concatenate([tokens[m]] * (padded // LANES), axis=1)
        blocks.append(one_hot((low <= wide) & (wide < high)))
        rows = notes[m][notes[m].shape[0] - tail :, :].astype(jnp.float32)
        ids.append(rows[2 * i : 2 * i + 1, :] * tok + rows[2 * i + 1 : 2 * i + 2, :])
    place_block = jnp.concatenate(blocks, axis=0)
    hit = jnp.concatenate(
        [jnp.concatenate([one_hot(tokens[m] == ids[j]) for j in range(n)], axis=1) for m in range(n)], axis=0
    )
    found = dot(hit, place_block, NN).astype(jnp.bfloat16)
    member[...] = found
    bias_out[...] = dot(found[: bias_out.shape[0]], table[...].astype(jnp.bfloat16), NN).astype(jnp.bfloat16)


def mix(normed_q, bias, normed_k, member, values):
    factor = normed_q.shape[1] ** (-0.5) * math.log2(math.e)
    scores = dot(jnp.concatenate([normed_q, bias], axis=1), jnp.concatenate([normed_k, member], axis=1), NT)
    peak = jnp.max(scores, axis=1, keepdims=True)
    weights = jnp.exp2((scores - peak) * factor)
    denom = jnp.sum(weights, axis=1, keepdims=True)
    mixed = dot(weights.astype(jnp.bfloat16), values, NN)
    return (mixed / denom).astype(jnp.bfloat16)


def peer_kernel(n, half, streams, tok, heads, q_gain, *refs):
    keys, values, member, bias, out = refs[:n], refs[n : 2 * n], refs[2 * n : 2 * n + half], refs[2 * n + half : -1], refs[-1]
    first_head = lax.rem(lax.axis_index("head") * streams, heads) + lax.rem(lax.axis_index("seq"), 2) * half
    scale = scales_of(keys[1], 0).T[:, :1]
    for i in range(half):
        at = pl.ds(i * tok, tok)
        normed_k = jnp.concatenate([keys[m][at, :] for m in range(n)], axis=0)
        value_rows = jnp.concatenate([values[m][at, :] for m in range(n)], axis=0)
        raw = values[1][pl.ds((2 * streams - 3 * half + i) * tok, tok), :].astype(jnp.float32)
        normed_q = (raw * scale * q_gain[pl.ds(first_head + i, 1), :]).astype(jnp.bfloat16)
        out[i] = mix(normed_q, bias[i][tok:], normed_k, member[i][...], value_rows)


def scales_of(message, kind):
    rows = message[message.shape[0] - 16 :, :].astype(jnp.float32)
    row = (rows[3 * kind : 3 * kind + 1, :] + rows[3 * kind + 1 : 3 * kind + 2, :]) + rows[3 * kind + 2 : 3 * kind + 3, :]
    return jnp.concatenate([row] * 8, axis=0)


def own_kernel(n, half, kept, tok, heads, k_gain, own, *refs):
    keys, values, member, refs = refs[:n], refs[n : 2 * n], refs[2 * n : 2 * n + kept], refs[2 * n + kept :]
    bias, further, out = refs[:kept], dict(zip([m for m in range(n) if m & (m - 1)], refs[kept:-1])), refs[-1]
    streams = half + kept
    first_head = lax.rem(lax.axis_index("head") * streams, heads)
    if kept > half:
        scales = [None] + [scales_of(keys[m], 1).T[:, :1] for m in range(1, n)]
    for i in range(kept):
        at = pl.ds(i * tok, tok)
        if i < half:
            parts = [keys[m][at, :] for m in range(n)]
            value_rows = jnp.concatenate([values[m][at, :] for m in range(n)], axis=0)
        else:
            gain = k_gain[pl.ds(first_head + half + i, 1), :]
            parts, value_rows = [own[pl.ds((kept + i - half) * tok, tok), :]], []
            for m in range(n):
                ref, start = (values[m], half) if m & (m - 1) == 0 else (further[m], 0)
                start = (start + 2 * (i - half)) * tok
                value_rows.append(ref[start : start + tok, :])
                if m:
                    raw = ref[start + tok : start + 2 * tok, :].astype(jnp.float32)
                    parts.append((raw * scales[m] * gain).astype(jnp.bfloat16))
            value_rows = jnp.concatenate(value_rows, axis=0)
        out[i] = mix(own[at, :], bias[i][:tok], jnp.concatenate(parts, axis=0), member[i][...], value_rows)


def local(n, query, key, value, q_gain, k_gain, order, cluster_rows, block_map):
    streams, tok, width = query.shape
    heads = q_gain.shape[0]
    half = streams // 2
    rest = streams - 2 * half
    kept = half + rest
    block_count = block_map.shape[2]
    clusters = cluster_rows.shape[1]
    blocks_per = block_count // clusters
    padded = -(-block_count // LANES) * LANES
    bf16, f32 = jnp.bfloat16, jnp.float32
    head_size = lax.axis_size("head")

    def exchange(rows, m):
        return lax.ppermute(rows, "seq", [(i, i ^ m) for i in range(n)])

    def after(rows, done):
        return lax.optimization_barrier((rows, done))[0]

    tail = -(-2 * kept // 16) * 16
    sized = lambda count: pltpu.VMEM((count * tok + tail, width), bf16)
    note, v_same, v_other, v_plain = pl.pallas_call(
        functools.partial(prep_kernel, half, tail),
        out_shape=[pltpu.VMEM((8, tok), f32), sized(half + 2 * rest), sized(2 * half + 2 * rest), sized(half)],
        in_specs=[ANY] * 4,
        out_specs=[VMEM] * 4,
        scratch_shapes=[
            pltpu.VMEM(query.shape, bf16),
            pltpu.VMEM(key.shape, bf16),
            pltpu.VMEM(order.shape, jnp.int32),
            pltpu.SemaphoreType.DMA((3 + 4 * half + 4 * rest,)),
        ],
        compiler_params=limit,
    )(*[pltpu.with_memory_space_constraint(x, pltpu.HBM) for x in (query, key, value, order)])

    values, tables = [v_same] + [None] * (n - 1), [None] * kept

    chain = [2**i for i in range(max(heads // streams, 1).bit_length() - 1)]
    launches = [[] for _ in range(len(chain) + 1)]
    fillers = [[] for _ in range(len(chain) + 1)]
    for m in reversed(range(1, n)):
        launches[min(m % 2, len(chain))].append(m)
    for i in range(kept):
        fillers[min(1 + (i > 0), len(chain))].append(i)

    def beside(at, note):
        for m in launches[at]:
            message = v_other if m == 1 else v_plain if m % 2 else v_same
            values[m] = exchange(after(message, note) if at else message, m)
        for i in fillers[at]:
            tables[i] = call(
                functools.partial(table_kernel, half, i),
                jax.ShapeDtypeStruct((padded, padded), f32),
                [after(block_map, note)],
                cost=weight,
            )

    beside(0, note)
    for at, step in enumerate(chain):
        note = note + lax.ppermute(note, "head", [(i, i ^ step) for i in range(head_size)])
        beside(at + 1, note)
    rows = lambda count, more: jax.ShapeDtypeStruct((count * tok + more, width), bf16)
    k_same, k_other, own_rows = call(
        functools.partial(norm_kernel, half, heads),
        [rows(half, 16), rows(half, 16), rows(kept + rest, 0)],
        [note, query, key, q_gain, k_gain],
    )
    keys = [k_same] + [None] * (n - 1)
    for m in reversed(range(1, n)):
        message = k_other if m % 2 else k_same
        if m == 1 and n > 2:
            message = after(message, values[2])
        keys[m] = exchange(message, m)

    further, across = {}, n // 2
    held = {}
    while rest and across:
        group = sorted(held)
        if group:
            sent = held[group[0]] if len(group) == 1 else jnp.concatenate([held[m] for m in group], axis=0)
            got = exchange(sent, across)
            size = 2 * rest * tok
            for at, m in enumerate(group):
                held[m ^ across] = further[m ^ across] = got if len(group) == 1 else got[at * size : (at + 1) * size]
        held[across] = values[across][half * tok : (half + 2 * rest) * tok]
        across //= 2

    cluster_rows = after(cluster_rows, note)
    start = jnp.cumsum(cluster_rows, axis=1, dtype=jnp.int32) - cluster_rows
    step_rows = jnp.arange(blocks_per, dtype=jnp.int32) * BLOCK
    low = start[:, :, None] + step_rows
    high = jnp.minimum(low + BLOCK, (start + cluster_rows)[:, :, None])
    bounds = jnp.stack([low.reshape(streams, block_count), high.reshape(streams, block_count)], axis=1)
    bounds = jnp.pad(bounds.reshape(2 * streams, block_count).astype(f32), ((0, 0), (0, padded - block_count)))

    member, bias = [None] * kept, [None] * kept
    for i in range(kept):
        member[i], bias[i] = call(
            functools.partial(blocks_kernel, half, i),
            [
                jax.ShapeDtypeStruct((n * tok, padded), bf16),
                jax.ShapeDtypeStruct(((2 if i < half else 1) * tok, padded), bf16),
            ],
            [bounds, tables[i], *values],
        )
    peer = call(
        functools.partial(peer_kernel, n, half, streams, tok, heads),
        jax.ShapeDtypeStruct((half, tok, width), bf16),
        [q_gain, *keys, *values, *member[:half], *bias[:half]],
    )
    theirs = exchange(peer, 1)
    own = call(
        functools.partial(own_kernel, n, half, kept, tok, heads),
        jax.ShapeDtypeStruct((kept, tok, width), bf16),
        [k_gain, own_rows, *keys, *values, *member, *bias, *[further[m] for m in sorted(further)]],
    )
    even = lax.axis_index("seq") % 2 == 0
    lower = jnp.where(even, own[:half], theirs)
    upper = jnp.where(even, theirs, own[:half])
    return jnp.concatenate([lower, upper, own[half:]], axis=0)


def solution(mesh):
    return jax.shard_map(
        functools.partial(local, mesh.shape["seq"]),
        mesh=mesh,
        in_specs=(
            P("head", "seq", None),
            P("head", "seq", None),
            P("head", "seq", None),
            P(),
            P(),
            P("head", "seq"),
            P("head", None),
            P("head", None, None),
        ),
        out_specs=P("head", "seq", None),
        check_vma=False,
    )
```

time: 36.6 us -> 29 us (0.79)
  waiting for transfers between devices: 11.8 us -> 6.14 us
  local copies, waits for them, and re-layouts: 2.88 us -> 0.24 us
  Pallas kernels: 4.69 us -> 5.29 us
    ppermute x3, waiting for transfers between devices: 5.27 us -> 2.07 us  [local(): lax.ppermute(note, 'head', [(i, i ^ step) for i in range(head_size)])]
    ppermute x7 -> x8, waiting for transfers between devices: 6.52 us -> 4.07 us  [exchange(): return lax.ppermute(rows, 'seq', [(i, i ^ m) for i in range(n)])]
    unnamed x20 -> x12, local copies, waits for them, and re-layouts: 1.02 us -> 0.03 us
    concatenate x1 -> x0, local copies, waits for them, and re-layouts: 0.85 us -> none  [local(): messages[m] = exchange(jnp.concatenate(parts, axis=0), m)]
    slice x3 -> x2, local copies, waits for them, and re-layouts: 0.8 us -> 0.01 us  [the longest x1 0.01 us: local(): held[across] = values[across][half * tok:(half + 2 * rest) * tok]]
    pallas_call x2 -> x10, Pallas kernels: 4.69 us -> 5.29 us  [the longest x9 3.56 us: call(): pl.pallas_call(body, out_shape=shapes, in_specs=[VMEM] * len(args), out_s...]
    ppermute x3, starting transfers between devices: 3.08 us -> 3.66 us  [local(): lax.ppermute(note, 'head', [(i, i ^ step) for i in range(head_size)])]
    ppermute x7 -> x8, starting transfers between devices: 12.8 us -> 12.5 us  [exchange(): return lax.ppermute(rows, 'seq', [(i, i ^ m) for i in range(n)])]
  transfers between devices with their start and end apart: 10 -> 11, of which waited for: 6 -> 4; matrix products, arithmetic and copies ran while one was open for 4% -> 1% of each run, Pallas kernels for 5% -> 12%
where the time goes in v2:
time: 29 us; the launch traced here: 28.8 us
  starting transfers between devices  16.1 us (56%)
  waiting for transfers between devices  6.14 us (21%)
  Pallas kernels  5.29 us (18%)
  other arithmetic  0.84 us (3%)
    ppermute x8, starting transfers between devices, exchange(): return lax.ppermute(rows, 'seq', [(i, i ^ m) for i in range(n)])  12.5 us
    ppermute x8, waiting for transfers between devices, exchange(): return lax.ppermute(rows, 'seq', [(i, i ^ m) for i in range(n)])  4.07 us
    ppermute x3, starting transfers between devices, local(): lax.ppermute(note, 'head', [(i, i ^ step) for i in range(head_size)])  3.66 us
    pallas_call x9, Pallas kernels, call(): pl.pallas_call(body, out_shape=shapes, in_specs=[VMEM] * len(args), out_s...  3.56 us
    ppermute x3, waiting for transfers between devices, local(): lax.ppermute(note, 'head', [(i, i ^ step) for i in range(head_size)])  2.07 us
    pallas_call x1, Pallas kernels, local(): pl.pallas_call(functools.partial(prep_kernel, half, tail), out_shape=[plt...  1.73 us
    concatenate x1, other arithmetic, local(): return jnp.concatenate([lower, upper, own[half:]], axis=0)  0.69 us
  transfers between devices with their start and end apart: 11, of which 4 were waited for; matrix products, arithmetic and copies ran while one was open for 1% of the time, Pallas kernels for 12%

profile of v2, /device:TPU:0, one launch (start us, length us, event | category | flops | bytes accessed | tf_op | source)
XLA Modules:
  0.0 28.8 jit_solution(13434676839487167757)
XLA Ops:
  0.0 1.7 %shard_map.82 = (f32[8,128]{1,0:T(8,128)S(1)}, bf16[528,128]{1,0:T(8,128)(2,1)S(1)}, bf16[784,128]{1,0:T(8,128)(2,1)S(1)}, bf16[272,128]{1,0:T(8,128)(2,1)S(1)}) custom-call(bf16[5,128,128]{2,1,0:T(8,128)(2,1)} %query.3, bf16[5,128,128]{2,1,0:T(8,128)(2,1)} %key.3, bf16[5,128,128]{2,1,0:T(8,128)(2,1)} %value.1, s32[5,128]{1,0:T(8,128)} %order.1), custom_call_target="tpu_custom_call" | custom-call | tf_op jit(solution)/shard_map/pallas_call | solution.py:236
  1.7 0.5 %collective-permute-start = (f32[8,128]{1,0:T(8,128)S(1)}, f32[8,128]{1,0:T(8,128)S(1)}, u32[]{:S(2)}, u32[]{:S(2)}) collective-permute-start(f32[8,128]{1,0:T(8,128)S(1)} %get-tuple-element.24), channel_id=1, source_target_pairs={{0,1},{1,0},{2,3},{3,2},{4,5},{5,4},{6,7},{7,6},{8,9},{9,8},{10,11... | collective-permute-start | bytes 12296 | tf_op jit(solution)/shard_map/ppermute | solution.py:274
  2.3 3.7 %collective-permute-start.3 = (bf16[528,128]{1,0:T(8,128)(2,1)S(1)}, bf16[528,128]{1,0:T(8,128)(2,1)S(1)}, u32[]{:S(2)}, u32[]{:S(2)}) collective-permute-start(bf16[528,128]{1,0:T(8,128)(2,1)S(1)} %get-tuple-element.28.refs_0_.refs_4_), channel_id=1, source_target_pairs={{0,16},{8,24},{16,0},{24,8},{1,17},{9,25},{17,1},{25,9},{2,18},{10... | collective-permute-start | bytes 405512 | tf_op jit(solution)/shard_map/ppermute | solution.py:229
  5.9 0.0 copy-start.4
  5.9 0.1 add.66
  6.0 0.0 collective-permute-done
  6.0 1.6 %collective-permute-start.1 = (f32[8,128]{1,0:T(8,128)S(1)}, f32[8,128]{1,0:T(8,128)S(1)}, u32[]{:S(2)}, u32[]{:S(2)}) collective-permute-start(f32[8,128]{1,0:T(8,128)S(1)} %add.60), channel_id=1, source_target_pairs={{0,2},{1,3},{2,0},{3,1},{4,6},{5,7},{6,4},{7,5},{8,10},{9,11},{10,... | collective-permute-start | bytes 12296 | tf_op jit(solution)/shard_map/ppermute | solution.py:274
  7.6 1.6 %collective-permute-start.7 = (bf16[784,128]{1,0:T(8,128)(2,1)S(1)}, bf16[784,128]{1,0:T(8,128)(2,1)S(1)}, u32[]{:S(2)}, u32[]{:S(2)}) collective-permute-start(bf16[784,128]{1,0:T(8,128)(2,1)S(1)} %get-tuple-element.31), channel_id=1, source_target_pairs={{0,8},{8,0},{16,24},{24,16},{1,9},{9,1},{17,25},{25,17},{2,10},{10... | collective-permute-start | bytes 602120 | tf_op jit(solution)/shard_map/ppermute | solution.py:229
  9.2 0.8 %collective-permute-start.8 = (bf16[272,128]{1,0:T(8,128)(2,1)S(1)}, bf16[272,128]{1,0:T(8,128)(2,1)S(1)}, u32[]{:S(2)}, u32[]{:S(2)}) collective-permute-start(bf16[272,128]{1,0:T(8,128)(2,1)S(1)} %get-tuple-element.33), channel_id=1, source_target_pairs={{0,24},{8,16},{16,8},{24,0},{1,25},{9,17},{17,9},{25,1},{2,26},{10... | collective-permute-start | bytes 208904 | tf_op jit(solution)/shard_map/ppermute | solution.py:229
  10.0 0.0 copy-done.4
  10.0 0.0 collective-permute-done.1
  10.0 0.0 copy-start
  10.0 0.0 copy-start.1
  10.0 1.6 %collective-permute-start.2 = (f32[8,128]{1,0:T(8,128)S(1)}, f32[8,128]{1,0:T(8,128)S(1)}, u32[]{:S(2)}, u32[]{:S(2)}) collective-permute-start(f32[8,128]{1,0:T(8,128)S(1)} %add.61), channel_id=1, source_target_pairs={{0,4},{1,5},{2,6},{3,7},{4,0},{5,1},{6,2},{7,3},{8,12},{9,13},{10,... | collective-permute-start | bytes 12296 | tf_op jit(solution)/shard_map/ppermute | solution.py:274
  11.6 0.0 copy-start.2
  11.6 0.0 copy-start.3
  11.6 2.1 %collective-permute-done.2 = f32[8,128]{1,0:T(8,128)S(1)} collective-permute-done((f32[8,128]{1,0:T(8,128)S(1)}, f32[8,128]{1,0:T(8,128)S(1)}, u32[]{:S(2)}, u32[]{:S(2)}) %collective-permute-start.2) | collective-permute-done | bytes 4128 | tf_op jit(solution)/shard_map/ppermute | solution.py:274
  13.7 0.0 copy-done
  13.7 0.0 copy-done.1
  13.7 0.0 copy-done.2
  13.7 0.0 copy-done.3
  13.7 0.2 shard_map.83
  14.0 0.0 copy-start.5
  14.0 1.2 %collective-permute-start.5 = (bf16[272,128]{1,0:T(8,128)(2,1)S(1)}, bf16[272,128]{1,0:T(8,128)(2,1)S(1)}, u32[]{:S(2)}, u32[]{:S(2)}) collective-permute-start(bf16[272,128]{1,0:T(8,128)(2,1)S(1)} %get-tuple-element.26.refs_0_), channel_id=1, source_target_pairs={{0,16},{8,24},{16,0},{24,8},{1,17},{9,25},{17,1},{25,9},{2,18},{10... | collective-permute-start | bytes 208904 | tf_op jit(solution)/shard_map/ppermute | solution.py:229
  15.1 2.5 %collective-permute-start.6 = (bf16[272,128]{1,0:T(8,128)(2,1)S(1)}, bf16[272,128]{1,0:T(8,128)(2,1)S(1)}, u32[]{:S(2)}, u32[]{:S(2)}) collective-permute-start(bf16[272,128]{1,0:T(8,128)(2,1)S(1)} %get-tuple-element.29), channel_id=1, source_target_pairs={{0,24},{8,16},{16,8},{24,0},{1,25},{9,17},{17,9},{25,1},{2,26},{10... | collective-permute-start | bytes 208904 | tf_op jit(solution)/shard_map/ppermute | solution.py:229
  17.6 0.0 copy-done.5
  17.7 0.1 bitcast_add_fusion
  17.8 0.0 collective-permute-done.3.refs_2_.refs_6_
  17.8 0.0 collective-permute-start.4
  17.8 0.1 copy.10
  17.9 0.0 collective-permute-done.8.refs_3_.refs_7_
  17.9 2.1 %collective-permute-start.9 = (bf16[256,128]{1,0:T(8,128)(2,1)S(1)}, bf16[256,128]{1,0:T(8,128)(2,1)S(1)}, u32[]{:S(2)}, u32[]{:S(2)}) collective-permute-start(bf16[256,128]{1,0:T(8,128)(2,1)S(1)} %slice.13), channel_id=1, source_target_pairs={{0,8},{8,0},{16,24},{24,16},{1,9},{9,1},{17,25},{25,17},{2,10},{10... | collective-permute-start | bytes 196616 | tf_op jit(solution)/shard_map/ppermute | solution.py:229
  20.0 0.0 collective-permute-done.7.refs_1_.refs_5_
  20.0 0.5 %shard_map.85 = (bf16[512,128]{1,0:T(8,128)(2,1)S(1)}, bf16[256,128]{1,0:T(8,128)(2,1)S(1)}) custom-call(f32[10,128]{1,0:T(8,128)S(1)} %pad.4.bounds, f32[128,128]{1,0:T(8,128)S(1)} %shard_map.84.table, bf16[528,128]{1,0:T(8,128)(2,1)S(1)} %get-tuple-element.28.refs_0_.refs_4_, bf16[784,128]{1,0:T(8,128)(2,1)S(1)} %collective-permute-done.7.refs_1_.refs_5_, ...), custom_call_target="tpu_custom_call" | custom-call | tf_op jit(solution)/shard_map/pallas_call | solution.py:33
  20.5 0.5 %shard_map.87 = (bf16[512,128]{1,0:T(8,128)(2,1)S(1)}, bf16[256,128]{1,0:T(8,128)(2,1)S(1)}) custom-call(f32[10,128]{1,0:T(8,128)S(1)} %pad.4.bounds, f32[128,128]{1,0:T(8,128)S(1)} %shard_map.86.table, bf16[528,128]{1,0:T(8,128)(2,1)S(1)} %get-tuple-element.28.refs_0_.refs_4_, bf16[784,128]{1,0:T(8,128)(2,1)S(1)} %collective-permute-done.7.refs_1_.refs_5_, ...), custom_call_target="tpu_custom_call" | custom-call | tf_op jit(solution)/shard_map/pallas_call | solution.py:33
  21.0 0.0 collective-permute-done.5.refs_2_
  21.0 1.2 %collective-permute-done.6.refs_3_ = bf16[272,128]{1,0:T(8,128)(2,1)S(1)} collective-permute-done((bf16[272,128]{1,0:T(8,128)(2,1)S(1)}, bf16[272,128]{1,0:T(8,128)(2,1)S(1)}, u32[]{:S(2)}, u32[]{:S(2)}) %collective-permute-start.6) | collective-permute-done | bytes 69664 | tf_op jit(solution)/shard_map/ppermute | solution.py:229
  22.2 0.7 %collective-permute-done.4.refs_1_ = bf16[272,128]{1,0:T(8,128)(2,1)S(1)} collective-permute-done((bf16[272,128]{1,0:T(8,128)(2,1)S(1)}, bf16[272,128]{1,0:T(8,128)(2,1)S(1)}, u32[]{:S(2)}, u32[]{:S(2)}) %collective-permute-start.4) | collective-permute-done | bytes 69664 | tf_op jit(solution)/shard_map/ppermute | solution.py:229
  22.9 0.9 %shard_map.91 = bf16[2,128,128]{2,1,0:T(8,128)(2,1)S(1)} custom-call(f32[40,128]{1,0:T(8,128)S(1)} %copy-done.2, bf16[272,128]{1,0:T(8,128)(2,1)S(1)} %get-tuple-element.26.refs_0_, bf16[272,128]{1,0:T(8,128)(2,1)S(1)} %collective-permute-done.4.refs_1_, bf16[272,128]{1,0:T(8,128)(2,1)S(1)} %collective-permute-done.5.refs_2_, ...), custom_call_target="tpu_custom_call" | custom-call | tf_op jit(solution)/shard_map/pallas_call | solution.py:33
  23.8 0.7 %collective-permute-start.10 = (bf16[2,128,128]{2,1,0:T(8,128)(2,1)S(1)}, bf16[2,128,128]{2,1,0:T(8,128)(2,1)S(1)}, u32[]{:S(2)}, u32[]{:S(2)}) collective-permute-start(bf16[2,128,128]{2,1,0:T(8,128)(2,1)S(1)} %shard_map.91), channel_id=1, source_target_pairs={{0,8},{8,0},{16,24},{24,16},{1,9},{9,1},{17,25},{25,17},{2,10},{10... | collective-permute-start | bytes 196616 | tf_op jit(solution)/shard_map/ppermute | solution.py:229
  24.5 0.5 %shard_map.89 = (bf16[512,128]{1,0:T(8,128)(2,1)S(1)}, bf16[128,128]{1,0:T(8,128)(2,1)S(1)}) custom-call(f32[10,128]{1,0:T(8,128)S(1)} %pad.4.bounds, f32[128,128]{1,0:T(8,128)S(1)} %shard_map.88.table, bf16[528,128]{1,0:T(8,128)(2,1)S(1)} %get-tuple-element.28.refs_0_.refs_4_, bf16[784,128]{1,0:T(8,128)(2,1)S(1)} %collective-permute-done.7.refs_1_.refs_5_, ...), custom_call_target="tpu_custom_call" | custom-call | tf_op jit(solution)/shard_map/pallas_call | solution.py:33
  24.9 0.0 collective-permute-done.9.refs_14_
  24.9 1.1 %shard_map.90 = bf16[3,128,128]{2,1,0:T(8,128)(2,1)S(1)} custom-call(f32[40,128]{1,0:T(8,128)S(1)} %copy-done.3, bf16[512,128]{1,0:T(8,128)(2,1)S(1)} %get-tuple-element.25.own, bf16[272,128]{1,0:T(8,128)(2,1)S(1)} %get-tuple-element.26.refs_0_, bf16[272,128]{1,0:T(8,128)(2,1)S(1)} %collective-permute-done.4.refs_1_, ...), custom_call_target="tpu_custom_call" | custom-call | tf_op jit(solution)/shard_map/pallas_call | solution.py:33
  26.1 2.1 %collective-permute-done.10 = bf16[2,128,128]{2,1,0:T(8,128)(2,1)S(1)} collective-permute-done((bf16[2,128,128]{2,1,0:T(8,128)(2,1)S(1)}, bf16[2,128,128]{2,1,0:T(8,128)(2,1)S(1)}, u32[]{:S(2)}, u32[]{:S(2)}) %collective-permute-start.10) | collective-permute-done | bytes 65568 | tf_op jit(solution)/shard_map/ppermute | solution.py:229
  28.1 0.7 %pad_maximum_fusion = bf16[5,128,128]{2,1,0:T(8,128)(2,1)} fusion(bf16[1,128,128]{2,1,0:T(8,128)(2,1)S(1)} %slice.15, bf16[2,128,128]{2,1,0:T(8,128)(2,1)S(1)} %get-tuple-element.44, bf16[2,128,128]{2,1,0:T(8,128)(2,1)S(1)} %get-tuple-element.43), kind=kLoop, calls=%fused_computation | loop fusion | flops 163840 | bytes 327680 | tf_op jit(solution)/shard_map/concatenate | solution.py:334
  (18 shorter events, 0.1 us)
Async XLA Ops:
  1.7 4.3 %collective-permute-start = (f32[8,128]{1,0:T(8,128)S(1)}, f32[8,128]{1,0:T(8,128)S(1)}, u32[]{:S(2)}, u32[]{:S(2)}) collective-permute-start(f32[8,128]{1,0:T(8,128)S(1)} %get-tuple-element.24), channel_id=1, source_target_pairs={{0,1},{1,0},{2,3},{3,2},{4,5},{5,4},{6,7},{7,6},{8,9},{9,8},{10,11... | collective-permute-start | bytes 12296 | tf_op jit(solution)/shard_map/ppermute | solution.py:274
  2.3 15.5 %collective-permute-start.3 = (bf16[528,128]{1,0:T(8,128)(2,1)S(1)}, bf16[528,128]{1,0:T(8,128)(2,1)S(1)}, u32[]{:S(2)}, u32[]{:S(2)}) collective-permute-start(bf16[528,128]{1,0:T(8,128)(2,1)S(1)} %get-tuple-element.28.refs_0_.refs_4_), channel_id=1, source_target_pairs={{0,16},{8,24},{16,0},{24,8},{1,17},{9,25},{17,1},{25,9},{2,18},{10... | collective-permute-start | bytes 405512 | tf_op jit(solution)/shard_map/ppermute | solution.py:229
  5.9 4.0 %copy-start.4 = (s32[5,8,8]{2,1,0:T(8,128)S(1)}, s32[5,8,8]{2,1,0:T(8,128)}, u32[]{:S(2)}) copy-start(s32[5,8,8]{2,1,0:T(8,128)} %block_map.2) | copy-start | bytes 3844
  6.0 4.0 %collective-permute-start.1 = (f32[8,128]{1,0:T(8,128)S(1)}, f32[8,128]{1,0:T(8,128)S(1)}, u32[]{:S(2)}, u32[]{:S(2)}) collective-permute-start(f32[8,128]{1,0:T(8,128)S(1)} %add.60), channel_id=1, source_target_pairs={{0,2},{1,3},{2,0},{3,1},{4,6},{5,7},{6,4},{7,5},{8,10},{9,11},{10,... | collective-permute-start | bytes 12296 | tf_op jit(solution)/shard_map/ppermute | solution.py:274
  7.6 12.4 %collective-permute-start.7 = (bf16[784,128]{1,0:T(8,128)(2,1)S(1)}, bf16[784,128]{1,0:T(8,128)(2,1)S(1)}, u32[]{:S(2)}, u32[]{:S(2)}) collective-permute-start(bf16[784,128]{1,0:T(8,128)(2,1)S(1)} %get-tuple-element.31), channel_id=1, source_target_pairs={{0,8},{8,0},{16,24},{24,16},{1,9},{9,1},{17,25},{25,17},{2,10},{10... | collective-permute-start | bytes 602120 | tf_op jit(solution)/shard_map/ppermute | solution.py:229
  9.2 8.8 %collective-permute-start.8 = (bf16[272,128]{1,0:T(8,128)(2,1)S(1)}, bf16[272,128]{1,0:T(8,128)(2,1)S(1)}, u32[]{:S(2)}, u32[]{:S(2)}) collective-permute-start(bf16[272,128]{1,0:T(8,128)(2,1)S(1)} %get-tuple-element.33), channel_id=1, source_target_pairs={{0,24},{8,16},{16,8},{24,0},{1,25},{9,17},{17,9},{25,1},{2,26},{10... | collective-permute-start | bytes 208904 | tf_op jit(solution)/shard_map/ppermute | solution.py:229
  10.0 3.7 %copy-start = (bf16[5,128,128]{2,1,0:T(8,128)(2,1)S(1)}, bf16[5,128,128]{2,1,0:T(8,128)(2,1)}, u32[]{:S(2)}) copy-start(bf16[5,128,128]{2,1,0:T(8,128)(2,1)} %query.3) | copy-start | bytes 491524
  10.0 3.7 %copy-start.1 = (bf16[5,128,128]{2,1,0:T(8,128)(2,1)S(1)}, bf16[5,128,128]{2,1,0:T(8,128)(2,1)}, u32[]{:S(2)}) copy-start(bf16[5,128,128]{2,1,0:T(8,128)(2,1)} %key.3) | copy-start | bytes 491524
  10.0 3.7 %collective-permute-start.2 = (f32[8,128]{1,0:T(8,128)S(1)}, f32[8,128]{1,0:T(8,128)S(1)}, u32[]{:S(2)}, u32[]{:S(2)}) collective-permute-start(f32[8,128]{1,0:T(8,128)S(1)} %add.61), channel_id=1, source_target_pairs={{0,4},{1,5},{2,6},{3,7},{4,0},{5,1},{6,2},{7,3},{8,12},{9,13},{10,... | collective-permute-start | bytes 12296 | tf_op jit(solution)/shard_map/ppermute | solution.py:274
  11.6 2.1 %copy-start.2 = (f32[40,128]{1,0:T(8,128)S(1)}, f32[40,128]{1,0:T(8,128)}, u32[]{:S(2)}) copy-start(f32[40,128]{1,0:T(8,128)} %q_gain.3) | copy-start | bytes 61444
  11.6 2.1 %copy-start.3 = (f32[40,128]{1,0:T(8,128)S(1)}, f32[40,128]{1,0:T(8,128)}, u32[]{:S(2)}) copy-start(f32[40,128]{1,0:T(8,128)} %k_gain.3) | copy-start | bytes 61444
  14.0 3.7 %copy-start.5 = (s32[5,4]{0,1:T(4,128)S(1)}, s32[5,4]{0,1:T(4,128)}, u32[]{:S(2)}) copy-start(s32[5,4]{0,1:T(4,128)} %param.14) | copy-start | bytes 244
  14.0 7.0 %collective-permute-start.5 = (bf16[272,128]{1,0:T(8,128)(2,1)S(1)}, bf16[272,128]{1,0:T(8,128)(2,1)S(1)}, u32[]{:S(2)}, u32[]{:S(2)}) collective-permute-start(bf16[272,128]{1,0:T(8,128)(2,1)S(1)} %get-tuple-element.26.refs_0_), channel_id=1, source_target_pairs={{0,16},{8,24},{16,0},{24,8},{1,17},{9,25},{17,1},{25,9},{2,18},{10... | collective-permute-start | bytes 208904 | tf_op jit(solution)/shard_map/ppermute | solution.py:229
  15.1 7.1 %collective-permute-start.6 = (bf16[272,128]{1,0:T(8,128)(2,1)S(1)}, bf16[272,128]{1,0:T(8,128)(2,1)S(1)}, u32[]{:S(2)}, u32[]{:S(2)}) collective-permute-start(bf16[272,128]{1,0:T(8,128)(2,1)S(1)} %get-tuple-element.29), channel_id=1, source_target_pairs={{0,24},{8,16},{16,8},{24,0},{1,25},{9,17},{17,9},{25,1},{2,26},{10... | collective-permute-start | bytes 208904 | tf_op jit(solution)/shard_map/ppermute | solution.py:229
  17.8 5.2 %collective-permute-start.4 = (bf16[272,128]{1,0:T(8,128)(2,1)S(1)}, bf16[272,128]{1,0:T(8,128)(2,1)S(1)}, u32[]{:S(2)}, u32[]{:S(2)}) collective-permute-start(bf16[272,128]{1,0:T(8,128)(2,1)S(1)} %get-tuple-element.29), channel_id=1, source_target_pairs={{0,8},{8,0},{16,24},{24,16},{1,9},{9,1},{17,25},{25,17},{2,10},{10... | collective-permute-start | bytes 208904 | tf_op jit(solution)/shard_map/ppermute | solution.py:229
  17.9 7.0 %collective-permute-start.9 = (bf16[256,128]{1,0:T(8,128)(2,1)S(1)}, bf16[256,128]{1,0:T(8,128)(2,1)S(1)}, u32[]{:S(2)}, u32[]{:S(2)}) collective-permute-start(bf16[256,128]{1,0:T(8,128)(2,1)S(1)} %slice.13), channel_id=1, source_target_pairs={{0,8},{8,0},{16,24},{24,16},{1,9},{9,1},{17,25},{25,17},{2,10},{10... | collective-permute-start | bytes 196616 | tf_op jit(solution)/shard_map/ppermute | solution.py:229
  23.8 4.3 %collective-permute-start.10 = (bf16[2,128,128]{2,1,0:T(8,128)(2,1)S(1)}, bf16[2,128,128]{2,1,0:T(8,128)(2,1)S(1)}, u32[]{:S(2)}, u32[]{:S(2)}) collective-permute-start(bf16[2,128,128]{2,1,0:T(8,128)(2,1)S(1)} %shard_map.91), channel_id=1, source_target_pairs={{0,8},{8,0},{16,24},{24,16},{1,9},{9,1},{17,25},{25,17},{2,10},{10... | collective-permute-start | bytes 196616 | tf_op jit(solution)/shard_map/ppermute | solution.py:229

commit v3 on v2

--- a/solution.py
+++ b/solution.py
@@ -41,37 +41,34 @@
     )(*args)
 
 
-def prep_kernel(half, tail, query, key, value, order, note, same, other, plain, q_in, k_in, order_in, sems):
+def prep_kernel(half, early, tail, query, key, value, order, note, same, other, plain, q_in, k_in, order_in, sems):
     streams, tok, width = query.shape
     rest = streams - 2 * half
     parity = lax.rem(lax.axis_index("seq"), 2)
-    pairs = [(query, q_in), (key, k_in), (order, order_in)]
+    pairs = [(ref.at[s], there.at[s]) for ref, there in ((query, q_in), (key, k_in)) for s in range(streams)]
+    pairs.append((order, order_in))
     for target, side in ((plain, 1 - parity), (same, parity), (other, 1 - parity)):
-        for i in range(half):
-            pairs.append((value.at[side * half + i], target.at[pl.ds(i * tok, tok)]))
-        if target is plain:
-            continue
-        for i, s in enumerate(range(2 * half, streams)):
-            for j, ref in enumerate((value, key)):
-                pairs.append((ref.at[s], target.at[pl.ds((half + 2 * i + j) * tok, tok)]))
+        rows = [(value, side * half + i) for i in range(half)] + [(key, side * half + i) for i in range(early)]
+        if target is not plain:
+            for s in range(2 * half, streams):
+                rows += [(value, s), (key, s)]
         if target is other:
-            for i in range(half):
-                pairs.append((query.at[side * half + i], target.at[pl.ds((half + 2 * rest + i) * tok, tok)]))
+            rows += [(query, side * half + i) for i in range(half)]
+        pairs += [(ref.at[s], target.at[pl.ds(at * tok, tok)]) for at, (ref, s) in enumerate(rows)]
     copies = [pltpu.make_async_copy(src, dst, sems.at[i]) for i, (src, dst) in enumerate(pairs)]
     for copy in copies:
         copy.start()
-    ones = jnp.ones((8, width), jnp.float32)
     totals = []
-    for copy, ref in zip(copies, (q_in, k_in)):
-        copy.wait()
+    for j, ref in enumerate((q_in, k_in)):
         total = None
-        for s in range(streams):
-            wide = ref[s].astype(jnp.float32)
+        for i in range(streams):
+            copies[j * streams + i].wait()
+            wide = ref[i].astype(jnp.float32)
             total = wide * wide if total is None else total + wide * wide
-        totals.append(dot(ones, total, NT, lax.Precision.HIGHEST))
-    row = lax.broadcasted_iota(jnp.int32, totals[0].shape, 0)
+        totals.append(jnp.sum(total.T, axis=0, keepdims=True))
+    row = lax.broadcasted_iota(jnp.int32, (8, tok), 0)
     note[...] = jnp.where(row == 0, totals[0], jnp.where(row == 1, totals[1], 0.0))
-    copies[2].wait()
+    copies[2 * streams].wait()
     row = lax.broadcasted_iota(jnp.int32, (tail, tok), 0)
     for side, targets in ((1 - parity, (plain, other)), (parity, (same,))):
         rows = jnp.zeros((tail, tok), jnp.float32)
@@ -82,11 +79,11 @@
             rows = jnp.where(row == 2 * i, high, jnp.where(row == 2 * i + 1, ids - high * tok, rows))
         for target in targets:
             target[target.shape[0] - tail :, :] = rows.astype(jnp.bfloat16)
-    for copy in copies[3:]:
+    for copy in copies[2 * streams + 1 :]:
         copy.wait()
 
 
-def norm_kernel(half, heads, totals, query, key, q_gain, k_gain, same, other, own):
+def norm_kernel(half, early, heads, totals, query, key, q_gain, k_gain, same, other, own):
     streams, tok, width = query.shape
     kept = streams - half
     parity = lax.rem(lax.axis_index("seq"), 2)
@@ -111,10 +108,13 @@
         target[target.shape[0] - 16 :, :] = rows
     for i in range(half):
         mine, theirs = parity * half + i, (1 - parity) * half + i
-        at = pl.ds(i * tok, tok)
-        same[at, :] = normal(key, k_gain, mine, 1)
-        other[at, :] = normal(key, k_gain, theirs, 1)
-        own[at, :] = normal(query, q_gain, mine, 0)
+        own[pl.ds(i * tok, tok), :] = normal(query, q_gain, mine, 0)
+        if i < early:
+            own[pl.ds((2 * kept - half + i) * tok, tok), :] = normal(key, k_gain, mine, 1)
+        else:
+            at = pl.ds((i - early) * tok, tok)
+            same[at, :] = normal(key, k_gain, mine, 1)
+            other[at, :] = normal(key, k_gain, theirs, 1)
     for s in range(2 * half, streams):
         own[pl.ds((s - half) * tok, tok), :] = normal(query, q_gain, s, 0)
         own[pl.ds((kept + s - 2 * half) * tok, tok), :] = normal(key, k_gain, s, 1)
@@ -167,16 +167,27 @@
     return (mixed / denom).astype(jnp.bfloat16)
 
 
-def peer_kernel(n, half, streams, tok, heads, q_gain, *refs):
-    keys, values, member, bias, out = refs[:n], refs[n : 2 * n], refs[2 * n : 2 * n + half], refs[2 * n + half : -1], refs[-1]
+def peer_kernel(n, half, early, streams, tok, heads, q_gain, k_gain, own, *refs):
+    keys, values, refs = refs[:n], refs[n : 2 * n], refs[2 * n :]
+    member, bias, (out, normed) = refs[:half], refs[half : 2 * half], refs[2 * half :]
     first_head = lax.rem(lax.axis_index("head") * streams, heads) + lax.rem(lax.axis_index("seq"), 2) * half
-    scale = scales_of(keys[1], 0).T[:, :1]
+    scale_q = scales_of(keys[1], 0).T[:, :1]
+    scale_k = [None] + [scales_of(keys[m], 1).T[:, :1] for m in range(1, n)]
+    queries = values[1].shape[0] // tok - half
     for i in range(half):
-        at = pl.ds(i * tok, tok)
-        normed_k = jnp.concatenate([keys[m][at, :] for m in range(n)], axis=0)
-        value_rows = jnp.concatenate([values[m][at, :] for m in range(n)], axis=0)
-        raw = values[1][pl.ds((2 * streams - 3 * half + i) * tok, tok), :].astype(jnp.float32)
-        normed_q = (raw * scale * q_gain[pl.ds(first_head + i, 1), :]).astype(jnp.bfloat16)
+        if i < early:
+            gain = k_gain[pl.ds(first_head + i, 1), :]
+            parts = [own[pl.ds((2 * streams - 3 * half + i) * tok, tok), :]]
+            for m in range(1, n):
+                raw = values[m][pl.ds((half + i) * tok, tok), :].astype(jnp.float32)
+                parts.append((raw * scale_k[m] * gain).astype(jnp.bfloat16))
+            normed_k = jnp.concatenate(parts, axis=0)
+            normed[i] = normed_k
+        else:
+            normed_k = jnp.concatenate([keys[m][pl.ds((i - early) * tok, tok), :] for m in range(n)], axis=0)
+        value_rows = jnp.concatenate([values[m][pl.ds(i * tok, tok), :] for m in range(n)], axis=0)
+        raw = values[1][pl.ds((queries + i) * tok, tok), :].astype(jnp.float32)
+        normed_q = (raw * scale_q * q_gain[pl.ds(first_head + i, 1), :]).astype(jnp.bfloat16)
         out[i] = mix(normed_q, bias[i][tok:], normed_k, member[i][...], value_rows)
 
 
@@ -186,7 +197,7 @@
     return jnp.concatenate([row] * 8, axis=0)
 
 
-def own_kernel(n, half, kept, tok, heads, k_gain, own, *refs):
+def own_kernel(n, half, early, kept, tok, heads, k_gain, own, normed, *refs):
     keys, values, member, refs = refs[:n], refs[n : 2 * n], refs[2 * n : 2 * n + kept], refs[2 * n + kept :]
     bias, further, out = refs[:kept], dict(zip([m for m in range(n) if m & (m - 1)], refs[kept:-1])), refs[-1]
     streams = half + kept
@@ -196,13 +207,13 @@
     for i in range(kept):
         at = pl.ds(i * tok, tok)
         if i < half:
-            parts = [keys[m][at, :] for m in range(n)]
+            parts = [normed[i]] if i < early else [keys[m][pl.ds((i - early) * tok, tok), :] for m in range(n)]
             value_rows = jnp.concatenate([values[m][at, :] for m in range(n)], axis=0)
         else:
             gain = k_gain[pl.ds(first_head + half + i, 1), :]
             parts, value_rows = [own[pl.ds((kept + i - half) * tok, tok), :]], []
             for m in range(n):
-                ref, start = (values[m], half) if m & (m - 1) == 0 else (further[m], 0)
+                ref, start = (values[m], half + early) if m & (m - 1) == 0 else (further[m], 0)
                 start = (start + 2 * (i - half)) * tok
                 value_rows.append(ref[start : start + tok, :])
                 if m:
@@ -232,17 +243,19 @@
         return lax.optimization_barrier((rows, done))[0]
 
     tail = -(-2 * kept // 16) * 16
+    early = half - half // 2
+    lead = half + early
     sized = lambda count: pltpu.VMEM((count * tok + tail, width), bf16)
     note, v_same, v_other, v_plain = pl.pallas_call(
-        functools.partial(prep_kernel, half, tail),
-        out_shape=[pltpu.VMEM((8, tok), f32), sized(half + 2 * rest), sized(2 * half + 2 * rest), sized(half)],
+        functools.partial(prep_kernel, half, early, tail),
+        out_shape=[pltpu.VMEM((8, tok), f32), sized(lead + 2 * rest), sized(lead + 2 * rest + half), sized(lead)],
         in_specs=[ANY] * 4,
         out_specs=[VMEM] * 4,
         scratch_shapes=[
             pltpu.VMEM(query.shape, bf16),
             pltpu.VMEM(key.shape, bf16),
             pltpu.VMEM(order.shape, jnp.int32),
-            pltpu.SemaphoreType.DMA((3 + 4 * half + 4 * rest,)),
+            pltpu.SemaphoreType.DMA((2 * streams + 1 + 3 * lead + 4 * rest + half,)),
         ],
         compiler_params=limit,
     )(*[pltpu.with_memory_space_constraint(x, pltpu.HBM) for x in (query, key, value, order)])
@@ -275,14 +288,14 @@
         beside(at + 1, note)
     rows = lambda count, more: jax.ShapeDtypeStruct((count * tok + more, width), bf16)
     k_same, k_other, own_rows = call(
-        functools.partial(norm_kernel, half, heads),
-        [rows(half, 16), rows(half, 16), rows(kept + rest, 0)],
+        functools.partial(norm_kernel, half, early, heads),
+        [rows(half - early, 16), rows(half - early, 16), rows(kept + rest + early, 0)],
         [note, query, key, q_gain, k_gain],
     )
     keys = [k_same] + [None] * (n - 1)
     for m in reversed(range(1, n)):
         message = k_other if m % 2 else k_same
-        if m == 1 and n > 2:
+        if m <= 2 < n:
             message = after(message, values[2])
         keys[m] = exchange(message, m)
 
@@ -296,7 +309,7 @@
             size = 2 * rest * tok
             for at, m in enumerate(group):
                 held[m ^ across] = further[m ^ across] = got if len(group) == 1 else got[at * size : (at + 1) * size]
-        held[across] = values[across][half * tok : (half + 2 * rest) * tok]
+        held[across] = values[across][lead * tok : (lead + 2 * rest) * tok]
         across //= 2
 
     cluster_rows = after(cluster_rows, note)
@@ -317,16 +330,19 @@
             ],
             [bounds, tables[i], *values],
         )
-    peer = call(
-        functools.partial(peer_kernel, n, half, streams, tok, heads),
-        jax.ShapeDtypeStruct((half, tok, width), bf16),
-        [q_gain, *keys, *values, *member[:half], *bias[:half]],
+    peer, normed = call(
+        functools.partial(peer_kernel, n, half, early, streams, tok, heads),
+        [
+            jax.ShapeDtypeStruct((half, tok, width), bf16),
+            jax.ShapeDtypeStruct((early, n * tok, width), bf16),
+        ],
+        [q_gain, k_gain, own_rows, *keys, *values, *member[:half], *bias[:half]],
     )
     theirs = exchange(peer, 1)
     own = call(
-        functools.partial(own_kernel, n, half, kept, tok, heads),
+        functools.partial(own_kernel, n, half, early, kept, tok, heads),
         jax.ShapeDtypeStruct((kept, tok, width), bf16),
-        [k_gain, own_rows, *keys, *values, *member, *bias, *[further[m] for m in sorted(further)]],
+        [k_gain, own_rows, normed, *keys, *values, *member, *bias, *[further[m] for m in sorted(further)]],
     )
     even = lax.axis_index("seq") % 2 == 0
     lower = jnp.where(even, own[:half], theirs)

time: 29 us -> 28.1 us (0.969)
  waiting for transfers between devices: 6.14 us -> 5.08 us
  starting transfers between devices: 16.1 us -> 16.4 us
    ppermute x8, waiting for transfers between devices: 4.07 us -> 3.03 us  [exchange(): return lax.ppermute(rows, 'seq', [(i, i ^ m) for i in range(n)])]
    pallas_call x1, Pallas kernels: 1.73 us -> 1.35 us  [local(): pl.pallas_call(functools.partial(prep_kernel, half, early, tail), out_sha...]
  transfers between devices with their start and end apart: 11 -> 11, of which waited for: 4 -> 3; matrix products, arithmetic and copies ran while one was open for 1% -> 1% of each run, Pallas kernels for 12% -> 13%
where the time goes in v3:
time: 28.1 us; the launch traced here: 27.9 us
  starting transfers between devices  16.4 us (58%)
  Pallas kernels  5.11 us (18%)
  waiting for transfers between devices  5.08 us (18%)
  other arithmetic  0.84 us (3%)
    ppermute x8, starting transfers between devices, exchange(): return lax.ppermute(rows, 'seq', [(i, i ^ m) for i in range(n)])  12.8 us
    pallas_call x9, Pallas kernels, call(): pl.pallas_call(body, out_shape=shapes, in_specs=[VMEM] * len(args), out_s...  3.76 us
    ppermute x3, starting transfers between devices, local(): lax.ppermute(note, 'head', [(i, i ^ step) for i in range(head_size)])  3.66 us
    ppermute x8, waiting for transfers between devices, exchange(): return lax.ppermute(rows, 'seq', [(i, i ^ m) for i in range(n)])  3.03 us
    ppermute x3, waiting for transfers between devices, local(): lax.ppermute(note, 'head', [(i, i ^ step) for i in range(head_size)])  2.06 us
    pallas_call x1, Pallas kernels, local(): pl.pallas_call(functools.partial(prep_kernel, half, early, tail), out_sha...  1.35 us
    concatenate x1, other arithmetic, local(): return jnp.concatenate([lower, upper, own[half:]], axis=0)  0.69 us
  transfers between devices with their start and end apart: 11, of which 3 were waited for; matrix products, arithmetic and copies ran while one was open for 1% of the time, Pallas kernels for 13%

profile of v3, /device:TPU:0, one launch (start us, length us, event | category | flops | bytes accessed | tf_op | source)
XLA Modules:
  0.0 27.9 jit_solution(2842174970970585679)
XLA Ops:
  0.0 1.3 %shard_map.82 = (f32[8,128]{1,0:T(8,128)S(1)}, bf16[656,128]{1,0:T(8,128)(2,1)S(1)}, bf16[912,128]{1,0:T(8,128)(2,1)S(1)}, bf16[400,128]{1,0:T(8,128)(2,1)S(1)}) custom-call(bf16[5,128,128]{2,1,0:T(8,128)(2,1)} %query.3, bf16[5,128,128]{2,1,0:T(8,128)(2,1)} %key.3, bf16[5,128,128]{2,1,0:T(8,128)(2,1)} %value.1, s32[5,128]{1,0:T(8,128)} %order.1), custom_call_target="tpu_custom_call" | custom-call | tf_op jit(solution)/shard_map/pallas_call | solution.py:249
  1.4 0.5 %collective-permute-start = (f32[8,128]{1,0:T(8,128)S(1)}, f32[8,128]{1,0:T(8,128)S(1)}, u32[]{:S(2)}, u32[]{:S(2)}) collective-permute-start(f32[8,128]{1,0:T(8,128)S(1)} %get-tuple-element.27), channel_id=1, source_target_pairs={{0,1},{1,0},{2,3},{3,2},{4,5},{5,4},{6,7},{7,6},{8,9},{9,8},{10,11... | collective-permute-start | bytes 12296 | tf_op jit(solution)/shard_map/ppermute | solution.py:287
  1.9 3.7 %collective-permute-start.3 = (bf16[656,128]{1,0:T(8,128)(2,1)S(1)}, bf16[656,128]{1,0:T(8,128)(2,1)S(1)}, u32[]{:S(2)}, u32[]{:S(2)}) collective-permute-start(bf16[656,128]{1,0:T(8,128)(2,1)S(1)} %get-tuple-element.31.refs_0_.refs_4_), channel_id=1, source_target_pairs={{0,16},{8,24},{16,0},{24,8},{1,17},{9,25},{17,1},{25,9},{2,18},{10... | collective-permute-start | bytes 503816 | tf_op jit(solution)/shard_map/ppermute | solution.py:240
  5.5 0.0 copy-start.4
  5.5 0.1 add.66
  5.6 0.0 collective-permute-done
  5.6 1.6 %collective-permute-start.1 = (f32[8,128]{1,0:T(8,128)S(1)}, f32[8,128]{1,0:T(8,128)S(1)}, u32[]{:S(2)}, u32[]{:S(2)}) collective-permute-start(f32[8,128]{1,0:T(8,128)S(1)} %add.60), channel_id=1, source_target_pairs={{0,2},{1,3},{2,0},{3,1},{4,6},{5,7},{6,4},{7,5},{8,10},{9,11},{10,... | collective-permute-start | bytes 12296 | tf_op jit(solution)/shard_map/ppermute | solution.py:287
  7.2 1.6 %collective-permute-start.7 = (bf16[912,128]{1,0:T(8,128)(2,1)S(1)}, bf16[912,128]{1,0:T(8,128)(2,1)S(1)}, u32[]{:S(2)}, u32[]{:S(2)}) collective-permute-start(bf16[912,128]{1,0:T(8,128)(2,1)S(1)} %get-tuple-element.35), channel_id=1, source_target_pairs={{0,8},{8,0},{16,24},{24,16},{1,9},{9,1},{17,25},{25,17},{2,10},{10... | collective-permute-start | bytes 700424 | tf_op jit(solution)/shard_map/ppermute | solution.py:240
  8.8 0.8 %collective-permute-start.8 = (bf16[400,128]{1,0:T(8,128)(2,1)S(1)}, bf16[400,128]{1,0:T(8,128)(2,1)S(1)}, u32[]{:S(2)}, u32[]{:S(2)}) collective-permute-start(bf16[400,128]{1,0:T(8,128)(2,1)S(1)} %get-tuple-element.37), channel_id=1, source_target_pairs={{0,24},{8,16},{16,8},{24,0},{1,25},{9,17},{17,9},{25,1},{2,26},{10... | collective-permute-start | bytes 307208 | tf_op jit(solution)/shard_map/ppermute | solution.py:240
  9.6 0.0 copy-done.4
  9.6 0.0 collective-permute-done.1
  9.6 0.0 copy-start
  9.6 0.0 copy-start.1
  9.6 1.6 %collective-permute-start.2 = (f32[8,128]{1,0:T(8,128)S(1)}, f32[8,128]{1,0:T(8,128)S(1)}, u32[]{:S(2)}, u32[]{:S(2)}) collective-permute-start(f32[8,128]{1,0:T(8,128)S(1)} %add.61), channel_id=1, source_target_pairs={{0,4},{1,5},{2,6},{3,7},{4,0},{5,1},{6,2},{7,3},{8,12},{9,13},{10,... | collective-permute-start | bytes 12296 | tf_op jit(solution)/shard_map/ppermute | solution.py:287
  11.2 0.0 copy-start.5
  11.2 0.0 copy-start.3
  11.3 0.0 copy-start.2
  11.3 2.1 %collective-permute-done.2 = f32[8,128]{1,0:T(8,128)S(1)} collective-permute-done((f32[8,128]{1,0:T(8,128)S(1)}, f32[8,128]{1,0:T(8,128)S(1)}, u32[]{:S(2)}, u32[]{:S(2)}) %collective-permute-start.2) | collective-permute-done | bytes 4128 | tf_op jit(solution)/shard_map/ppermute | solution.py:287
  13.3 0.0 copy-done.5
  13.4 0.0 copy-done
  13.4 0.0 copy-done.1
  13.4 0.0 copy-done.3
  13.4 0.0 copy-done.2
  13.4 0.2 shard_map.83
  13.6 3.1 %collective-permute-start.6 = (bf16[144,128]{1,0:T(8,128)(2,1)S(1)}, bf16[144,128]{1,0:T(8,128)(2,1)S(1)}, u32[]{:S(2)}, u32[]{:S(2)}) collective-permute-start(bf16[144,128]{1,0:T(8,128)(2,1)S(1)} %get-tuple-element.32), channel_id=1, source_target_pairs={{0,24},{8,16},{16,8},{24,0},{1,25},{9,17},{17,9},{25,1},{2,26},{10... | collective-permute-start | bytes 110600 | tf_op jit(solution)/shard_map/ppermute | solution.py:240
  16.7 0.1 bitcast_add_fusion
  16.8 0.0 collective-permute-done.3.refs_2_.refs_6_
  16.8 0.0 collective-permute-start.5
  16.8 1.5 %collective-permute-start.4 = (bf16[144,128]{1,0:T(8,128)(2,1)S(1)}, bf16[144,128]{1,0:T(8,128)(2,1)S(1)}, u32[]{:S(2)}, u32[]{:S(2)}) collective-permute-start(bf16[144,128]{1,0:T(8,128)(2,1)S(1)} %get-tuple-element.32), channel_id=1, source_target_pairs={{0,8},{8,0},{16,24},{24,16},{1,9},{9,1},{17,25},{25,17},{2,10},{10... | collective-permute-start | bytes 110600 | tf_op jit(solution)/shard_map/ppermute | solution.py:240
  18.2 0.1 copy.10
  18.4 0.9 %collective-permute-done.8.refs_3_.refs_7_ = bf16[400,128]{1,0:T(8,128)(2,1)S(1)} collective-permute-done((bf16[400,128]{1,0:T(8,128)(2,1)S(1)}, bf16[400,128]{1,0:T(8,128)(2,1)S(1)}, u32[]{:S(2)}, u32[]{:S(2)}) %collective-permute-start.8) | collective-permute-done | bytes 102432 | tf_op jit(solution)/shard_map/ppermute | solution.py:240
  19.3 1.5 %collective-permute-start.9 = (bf16[256,128]{1,0:T(8,128)(2,1)S(1)}, bf16[256,128]{1,0:T(8,128)(2,1)S(1)}, u32[]{:S(2)}, u32[]{:S(2)}) collective-permute-start(bf16[256,128]{1,0:T(8,128)(2,1)S(1)} %slice.13), channel_id=1, source_target_pairs={{0,8},{8,0},{16,24},{24,16},{1,9},{9,1},{17,25},{25,17},{2,10},{10... | collective-permute-start | bytes 196616 | tf_op jit(solution)/shard_map/ppermute | solution.py:240
  20.8 0.0 collective-permute-done.7.refs_1_.refs_5_
  20.8 0.5 %shard_map.87 = (bf16[512,128]{1,0:T(8,128)(2,1)S(1)}, bf16[256,128]{1,0:T(8,128)(2,1)S(1)}) custom-call(f32[10,128]{1,0:T(8,128)S(1)} %pad.4.bounds, f32[128,128]{1,0:T(8,128)S(1)} %shard_map.86.table, bf16[656,128]{1,0:T(8,128)(2,1)S(1)} %get-tuple-element.31.refs_0_.refs_4_, bf16[912,128]{1,0:T(8,128)(2,1)S(1)} %collective-permute-done.7.refs_1_.refs_5_, ...), custom_call_target="tpu_custom_call" | custom-call | tf_op jit(solution)/shard_map/pallas_call | solution.py:33
  21.3 0.5 %shard_map.85 = (bf16[512,128]{1,0:T(8,128)(2,1)S(1)}, bf16[256,128]{1,0:T(8,128)(2,1)S(1)}) custom-call(f32[10,128]{1,0:T(8,128)S(1)} %pad.4.bounds, f32[128,128]{1,0:T(8,128)S(1)} %shard_map.84.table, bf16[656,128]{1,0:T(8,128)(2,1)S(1)} %get-tuple-element.31.refs_0_.refs_4_, bf16[912,128]{1,0:T(8,128)(2,1)S(1)} %collective-permute-done.7.refs_1_.refs_5_, ...), custom_call_target="tpu_custom_call" | custom-call | tf_op jit(solution)/shard_map/pallas_call | solution.py:33
  21.7 0.0 collective-permute-done.6.refs_3_
  21.8 0.0 collective-permute-done.5.refs_2_
  21.8 0.0 collective-permute-done.4.refs_1_
  21.8 1.1 %shard_map.88 = (bf16[2,128,128]{2,1,0:T(8,128)(2,1)S(1)}, bf16[1,512,128]{2,1,0:T(8,128)(2,1)S(1)}) custom-call(f32[40,128]{1,0:T(8,128)S(1)} %copy-done.3, f32[40,128]{1,0:T(8,128)S(1)} %copy-done.2, bf16[640,128]{1,0:T(8,128)(2,1)S(1)} %get-tuple-element.28.own, bf16[144,128]{1,0:T(8,128)(2,1)S(1)} %get-tuple-element.33.refs_0_, ...), custom_call_target="tpu_custom_call" | custom-call | tf_op jit(solution)/shard_map/pallas_call | solution.py:33
  22.8 0.7 %collective-permute-start.10 = (bf16[2,128,128]{2,1,0:T(8,128)(2,1)S(1)}, bf16[2,128,128]{2,1,0:T(8,128)(2,1)S(1)}, u32[]{:S(2)}, u32[]{:S(2)}) collective-permute-start(bf16[2,128,128]{2,1,0:T(8,128)(2,1)S(1)} %get-tuple-element.48), channel_id=1, source_target_pairs={{0,8},{8,0},{16,24},{24,16},{1,9},{9,1},{17,25},{25,17},{2,10},{10... | collective-permute-start | bytes 196616 | tf_op jit(solution)/shard_map/ppermute | solution.py:240
  23.5 0.4 %shard_map.90 = (bf16[512,128]{1,0:T(8,128)(2,1)S(1)}, bf16[128,128]{1,0:T(8,128)(2,1)S(1)}) custom-call(f32[10,128]{1,0:T(8,128)S(1)} %pad.4.bounds, f32[128,128]{1,0:T(8,128)S(1)} %shard_map.89.table, bf16[656,128]{1,0:T(8,128)(2,1)S(1)} %get-tuple-element.31.refs_0_.refs_4_, bf16[912,128]{1,0:T(8,128)(2,1)S(1)} %collective-permute-done.7.refs_1_.refs_5_, ...), custom_call_target="tpu_custom_call" | custom-call | tf_op jit(solution)/shard_map/pallas_call | solution.py:33
  24.0 0.0 collective-permute-done.9.refs_14_
  24.0 1.1 %shard_map.91 = bf16[3,128,128]{2,1,0:T(8,128)(2,1)S(1)} custom-call(f32[40,128]{1,0:T(8,128)S(1)} %copy-done.2, bf16[640,128]{1,0:T(8,128)(2,1)S(1)} %get-tuple-element.28.own, bf16[1,512,128]{2,1,0:T(8,128)(2,1)S(1)} %get-tuple-element.45.normed, bf16[144,128]{1,0:T(8,128)(2,1)S(1)} %get-tuple-element.33.refs_0_, ...), custom_call_target="tpu_custom_call" | custom-call | tf_op jit(solution)/shard_map/pallas_call | solution.py:33
  25.1 2.1 %collective-permute-done.10 = bf16[2,128,128]{2,1,0:T(8,128)(2,1)S(1)} collective-permute-done((bf16[2,128,128]{2,1,0:T(8,128)(2,1)S(1)}, bf16[2,128,128]{2,1,0:T(8,128)(2,1)S(1)}, u32[]{:S(2)}, u32[]{:S(2)}) %collective-permute-start.10) | collective-permute-done | bytes 65568 | tf_op jit(solution)/shard_map/ppermute | solution.py:240
  27.2 0.7 %pad_maximum_fusion = bf16[5,128,128]{2,1,0:T(8,128)(2,1)} fusion(bf16[1,128,128]{2,1,0:T(8,128)(2,1)S(1)} %slice.15, bf16[2,128,128]{2,1,0:T(8,128)(2,1)S(1)} %get-tuple-element.50, bf16[2,128,128]{2,1,0:T(8,128)(2,1)S(1)} %get-tuple-element.49), kind=kLoop, calls=%fused_computation | loop fusion | flops 163840 | bytes 327680 | tf_op jit(solution)/shard_map/concatenate | solution.py:350
  (18 shorter events, 0.1 us)
Async XLA Ops:
  1.4 4.3 %collective-permute-start = (f32[8,128]{1,0:T(8,128)S(1)}, f32[8,128]{1,0:T(8,128)S(1)}, u32[]{:S(2)}, u32[]{:S(2)}) collective-permute-start(f32[8,128]{1,0:T(8,128)S(1)} %get-tuple-element.27), channel_id=1, source_target_pairs={{0,1},{1,0},{2,3},{3,2},{4,5},{5,4},{6,7},{7,6},{8,9},{9,8},{10,11... | collective-permute-start | bytes 12296 | tf_op jit(solution)/shard_map/ppermute | solution.py:287
  1.9 14.9 %collective-permute-start.3 = (bf16[656,128]{1,0:T(8,128)(2,1)S(1)}, bf16[656,128]{1,0:T(8,128)(2,1)S(1)}, u32[]{:S(2)}, u32[]{:S(2)}) collective-permute-start(bf16[656,128]{1,0:T(8,128)(2,1)S(1)} %get-tuple-element.31.refs_0_.refs_4_), channel_id=1, source_target_pairs={{0,16},{8,24},{16,0},{24,8},{1,17},{9,25},{17,1},{25,9},{2,18},{10... | collective-permute-start | bytes 503816 | tf_op jit(solution)/shard_map/ppermute | solution.py:240
  5.5 4.0 %copy-start.4 = (s32[5,8,8]{2,1,0:T(8,128)S(1)}, s32[5,8,8]{2,1,0:T(8,128)}, u32[]{:S(2)}) copy-start(s32[5,8,8]{2,1,0:T(8,128)} %block_map.2) | copy-start | bytes 3844
  5.6 4.0 %collective-permute-start.1 = (f32[8,128]{1,0:T(8,128)S(1)}, f32[8,128]{1,0:T(8,128)S(1)}, u32[]{:S(2)}, u32[]{:S(2)}) collective-permute-start(f32[8,128]{1,0:T(8,128)S(1)} %add.60), channel_id=1, source_target_pairs={{0,2},{1,3},{2,0},{3,1},{4,6},{5,7},{6,4},{7,5},{8,10},{9,11},{10,... | collective-permute-start | bytes 12296 | tf_op jit(solution)/shard_map/ppermute | solution.py:287
  7.2 13.6 %collective-permute-start.7 = (bf16[912,128]{1,0:T(8,128)(2,1)S(1)}, bf16[912,128]{1,0:T(8,128)(2,1)S(1)}, u32[]{:S(2)}, u32[]{:S(2)}) collective-permute-start(bf16[912,128]{1,0:T(8,128)(2,1)S(1)} %get-tuple-element.35), channel_id=1, source_target_pairs={{0,8},{8,0},{16,24},{24,16},{1,9},{9,1},{17,25},{25,17},{2,10},{10... | collective-permute-start | bytes 700424 | tf_op jit(solution)/shard_map/ppermute | solution.py:240
  8.8 10.5 %collective-permute-start.8 = (bf16[400,128]{1,0:T(8,128)(2,1)S(1)}, bf16[400,128]{1,0:T(8,128)(2,1)S(1)}, u32[]{:S(2)}, u32[]{:S(2)}) collective-permute-start(bf16[400,128]{1,0:T(8,128)(2,1)S(1)} %get-tuple-element.37), channel_id=1, source_target_pairs={{0,24},{8,16},{16,8},{24,0},{1,25},{9,17},{17,9},{25,1},{2,26},{10... | collective-permute-start | bytes 307208 | tf_op jit(solution)/shard_map/ppermute | solution.py:240
  9.6 3.8 %copy-start = (bf16[5,128,128]{2,1,0:T(8,128)(2,1)S(1)}, bf16[5,128,128]{2,1,0:T(8,128)(2,1)}, u32[]{:S(2)}) copy-start(bf16[5,128,128]{2,1,0:T(8,128)(2,1)} %query.3) | copy-start | bytes 491524
  9.6 3.7 %copy-start.1 = (bf16[5,128,128]{2,1,0:T(8,128)(2,1)S(1)}, bf16[5,128,128]{2,1,0:T(8,128)(2,1)}, u32[]{:S(2)}) copy-start(bf16[5,128,128]{2,1,0:T(8,128)(2,1)} %key.3) | copy-start | bytes 491524
  9.6 3.7 %collective-permute-start.2 = (f32[8,128]{1,0:T(8,128)S(1)}, f32[8,128]{1,0:T(8,128)S(1)}, u32[]{:S(2)}, u32[]{:S(2)}) collective-permute-start(f32[8,128]{1,0:T(8,128)S(1)} %add.61), channel_id=1, source_target_pairs={{0,4},{1,5},{2,6},{3,7},{4,0},{5,1},{6,2},{7,3},{8,12},{9,13},{10,... | collective-permute-start | bytes 12296 | tf_op jit(solution)/shard_map/ppermute | solution.py:287
  11.2 2.1 %copy-start.5 = (s32[5,4]{0,1:T(4,128)S(1)}, s32[5,4]{0,1:T(4,128)}, u32[]{:S(2)}) copy-start(s32[5,4]{0,1:T(4,128)} %param.14) | copy-start | bytes 244
  11.2 2.1 %copy-start.3 = (f32[40,128]{1,0:T(8,128)S(1)}, f32[40,128]{1,0:T(8,128)}, u32[]{:S(2)}) copy-start(f32[40,128]{1,0:T(8,128)} %q_gain.3) | copy-start | bytes 61444
  11.3 2.1 %copy-start.2 = (f32[40,128]{1,0:T(8,128)S(1)}, f32[40,128]{1,0:T(8,128)}, u32[]{:S(2)}) copy-start(f32[40,128]{1,0:T(8,128)} %k_gain.5) | copy-start | bytes 61444
  13.6 8.1 %collective-permute-start.6 = (bf16[144,128]{1,0:T(8,128)(2,1)S(1)}, bf16[144,128]{1,0:T(8,128)(2,1)S(1)}, u32[]{:S(2)}, u32[]{:S(2)}) collective-permute-start(bf16[144,128]{1,0:T(8,128)(2,1)S(1)} %get-tuple-element.32), channel_id=1, source_target_pairs={{0,24},{8,16},{16,8},{24,0},{1,25},{9,17},{17,9},{25,1},{2,26},{10... | collective-permute-start | bytes 110600 | tf_op jit(solution)/shard_map/ppermute | solution.py:240
  16.8 5.0 %collective-permute-start.5 = (bf16[144,128]{1,0:T(8,128)(2,1)S(1)}, bf16[144,128]{1,0:T(8,128)(2,1)S(1)}, u32[]{:S(2)}, u32[]{:S(2)}) collective-permute-start(bf16[144,128]{1,0:T(8,128)(2,1)S(1)} %get-tuple-element.33.refs_0_), channel_id=1, source_target_pairs={{0,16},{8,24},{16,0},{24,8},{1,17},{9,25},{17,1},{25,9},{2,18},{10... | collective-permute-start | bytes 110600 | tf_op jit(solution)/shard_map/ppermute | solution.py:240
  16.8 5.0 %collective-permute-start.4 = (bf16[144,128]{1,0:T(8,128)(2,1)S(1)}, bf16[144,128]{1,0:T(8,128)(2,1)S(1)}, u32[]{:S(2)}, u32[]{:S(2)}) collective-permute-start(bf16[144,128]{1,0:T(8,128)(2,1)S(1)} %get-tuple-element.32), channel_id=1, source_target_pairs={{0,8},{8,0},{16,24},{24,16},{1,9},{9,1},{17,25},{25,17},{2,10},{10... | collective-permute-start | bytes 110600 | tf_op jit(solution)/shard_map/ppermute | solution.py:240
  19.3 4.7 %collective-permute-start.9 = (bf16[256,128]{1,0:T(8,128)(2,1)S(1)}, bf16[256,128]{1,0:T(8,128)(2,1)S(1)}, u32[]{:S(2)}, u32[]{:S(2)}) collective-permute-start(bf16[256,128]{1,0:T(8,128)(2,1)S(1)} %slice.13), channel_id=1, source_target_pairs={{0,8},{8,0},{16,24},{24,16},{1,9},{9,1},{17,25},{25,17},{2,10},{10... | collective-permute-start | bytes 196616 | tf_op jit(solution)/shard_map/ppermute | solution.py:240
  22.8 4.3 %collective-permute-start.10 = (bf16[2,128,128]{2,1,0:T(8,128)(2,1)S(1)}, bf16[2,128,128]{2,1,0:T(8,128)(2,1)S(1)}, u32[]{:S(2)}, u32[]{:S(2)}) collective-permute-start(bf16[2,128,128]{2,1,0:T(8,128)(2,1)S(1)} %get-tuple-element.48), channel_id=1, source_target_pairs={{0,8},{8,0},{16,24},{24,16},{1,9},{9,1},{17,25},{25,17},{2,10},{10... | collective-permute-start | bytes 196616 | tf_op jit(solution)/shard_map/ppermute | solution.py:240

commit v4 on v3

--- a/solution.py
+++ b/solution.py
@@ -49,7 +49,7 @@
     pairs.append((order, order_in))
     for target, side in ((plain, 1 - parity), (same, parity), (other, 1 - parity)):
         rows = [(value, side * half + i) for i in range(half)] + [(key, side * half + i) for i in range(early)]
-        if target is not plain:
+        if target is same:
             for s in range(2 * half, streams):
                 rows += [(value, s), (key, s)]
         if target is other:
@@ -129,8 +129,7 @@
     table[:count, :count] = jnp.where((block_map[s] == 1) | (row == column), 0.0, far)
 
 
-def blocks_kernel(half, i, bounds, table, *refs):
-    notes, member, bias_out = refs[:-2], refs[-2], refs[-1]
+def blocks_of(half, i, bounds, notes):
     n = len(notes)
     tok = notes[0].shape[1]
     padded = bounds.shape[1]
@@ -148,32 +147,42 @@
         blocks.append(one_hot((low <= wide) & (wide < high)))
         rows = notes[m][notes[m].shape[0] - tail :, :].astype(jnp.float32)
         ids.append(rows[2 * i : 2 * i + 1, :] * tok + rows[2 * i + 1 : 2 * i + 2, :])
-    place_block = jnp.concatenate(blocks, axis=0)
     hit = jnp.concatenate(
         [jnp.concatenate([one_hot(tokens[m] == ids[j]) for j in range(n)], axis=1) for m in range(n)], axis=0
     )
-    found = dot(hit, place_block, NN).astype(jnp.bfloat16)
-    member[...] = found
-    bias_out[...] = dot(found[: bias_out.shape[0]], table[...].astype(jnp.bfloat16), NN).astype(jnp.bfloat16)
-
-
-def mix(normed_q, bias, normed_k, member, values):
-    factor = normed_q.shape[1] ** (-0.5) * math.log2(math.e)
-    scores = dot(jnp.concatenate([normed_q, bias], axis=1), jnp.concatenate([normed_k, member], axis=1), NT)
-    peak = jnp.max(scores, axis=1, keepdims=True)
-    weights = jnp.exp2((scores - peak) * factor)
-    denom = jnp.sum(weights, axis=1, keepdims=True)
-    mixed = dot(weights.astype(jnp.bfloat16), values, NN)
-    return (mixed / denom).astype(jnp.bfloat16)
+    return dot(hit, jnp.concatenate(blocks, axis=0), NN).astype(jnp.bfloat16)
+
+
+def blocks_kernel(half, picks, bounds, *refs):
+    tables, refs = refs[: len(picks)], refs[len(picks) :]
+    notes, outs = refs[: -2 * len(picks)], refs[-2 * len(picks) :]
+    found = [blocks_of(half, i, bounds, notes) for i in picks]
+    for at in range(len(picks)):
+        outs[2 * at][...] = found[at]
+        count = outs[2 * at + 1].shape[0]
+        outs[2 * at + 1][...] = dot(found[at][:count], tables[at][...].astype(jnp.bfloat16), NN).astype(jnp.bfloat16)
+
+
+def mix_all(tasks):
+    factor = tasks[0][0].shape[1] ** (-0.5) * math.log2(math.e)
+    scores = []
+    for normed_q, bias, normed_k, member, _ in tasks:
+        scores.append(dot(jnp.concatenate([normed_q, bias], axis=1), jnp.concatenate([normed_k, member], axis=1), NT))
+    peaks = [jnp.max(score, axis=1, keepdims=True) for score in scores]
+    weights = [jnp.exp2((score - peak) * factor) for score, peak in zip(scores, peaks)]
+    denoms = [jnp.sum(weight, axis=1, keepdims=True) for weight in weights]
+    mixed = [dot(weight.astype(jnp.bfloat16), task[4], NN) for weight, task in zip(weights, tasks)]
+    return [(rows / denom).astype(jnp.bfloat16) for rows, denom in zip(mixed, denoms)]
 
 
 def peer_kernel(n, half, early, streams, tok, heads, q_gain, k_gain, own, *refs):
     keys, values, refs = refs[:n], refs[n : 2 * n], refs[2 * n :]
     member, bias, (out, normed) = refs[:half], refs[half : 2 * half], refs[2 * half :]
     first_head = lax.rem(lax.axis_index("head") * streams, heads) + lax.rem(lax.axis_index("seq"), 2) * half
-    scale_q = scales_of(keys[1], 0).T[:, :1]
-    scale_k = [None] + [scales_of(keys[m], 1).T[:, :1] for m in range(1, n)]
+    scale_q, *scale_k = columns_of([(keys[1], 0)] + [(keys[m], 1) for m in range(1, n)])
+    scale_k = [None] + scale_k
     queries = values[1].shape[0] // tok - half
+    tasks = []
     for i in range(half):
         if i < early:
             gain = k_gain[pl.ds(first_head + i, 1), :]
@@ -188,22 +197,28 @@
         value_rows = jnp.concatenate([values[m][pl.ds(i * tok, tok), :] for m in range(n)], axis=0)
         raw = values[1][pl.ds((queries + i) * tok, tok), :].astype(jnp.float32)
         normed_q = (raw * scale_q * q_gain[pl.ds(first_head + i, 1), :]).astype(jnp.bfloat16)
-        out[i] = mix(normed_q, bias[i][tok:], normed_k, member[i][...], value_rows)
-
-
-def scales_of(message, kind):
-    rows = message[message.shape[0] - 16 :, :].astype(jnp.float32)
-    row = (rows[3 * kind : 3 * kind + 1, :] + rows[3 * kind + 1 : 3 * kind + 2, :]) + rows[3 * kind + 2 : 3 * kind + 3, :]
-    return jnp.concatenate([row] * 8, axis=0)
+        tasks.append((normed_q, bias[i][tok:], normed_k, member[i][...], value_rows))
+    for i, rows in enumerate(mix_all(tasks)):
+        out[i] = rows
+
+
+def columns_of(picks):
+    rows = []
+    for message, kind in picks:
+        tail = message[message.shape[0] - 16 :, :].astype(jnp.float32)
+        rows.append((tail[3 * kind : 3 * kind + 1, :] + tail[3 * kind + 1 : 3 * kind + 2, :]) + tail[3 * kind + 2 : 3 * kind + 3, :])
+    columns = jnp.concatenate(rows + [rows[0]] * (-len(rows) % 8), axis=0).T
+    return [columns[:, at : at + 1] for at in range(len(picks))]
 
 
 def own_kernel(n, half, early, kept, tok, heads, k_gain, own, normed, *refs):
     keys, values, member, refs = refs[:n], refs[n : 2 * n], refs[2 * n : 2 * n + kept], refs[2 * n + kept :]
-    bias, further, out = refs[:kept], dict(zip([m for m in range(n) if m & (m - 1)], refs[kept:-1])), refs[-1]
+    bias, further, out = refs[:kept], refs[kept:-1], refs[-1]
     streams = half + kept
+    tasks = []
     first_head = lax.rem(lax.axis_index("head") * streams, heads)
     if kept > half:
-        scales = [None] + [scales_of(keys[m], 1).T[:, :1] for m in range(1, n)]
+        scales = [None] + columns_of([(keys[m], 1) for m in range(1, n)])
     for i in range(kept):
         at = pl.ds(i * tok, tok)
         if i < half:
@@ -213,14 +228,16 @@
             gain = k_gain[pl.ds(first_head + half + i, 1), :]
             parts, value_rows = [own[pl.ds((kept + i - half) * tok, tok), :]], []
             for m in range(n):
-                ref, start = (values[m], half + early) if m & (m - 1) == 0 else (further[m], 0)
+                ref, start = further[m], 0
                 start = (start + 2 * (i - half)) * tok
                 value_rows.append(ref[start : start + tok, :])
                 if m:
                     raw = ref[start + tok : start + 2 * tok, :].astype(jnp.float32)
                     parts.append((raw * scales[m] * gain).astype(jnp.bfloat16))
             value_rows = jnp.concatenate(value_rows, axis=0)
-        out[i] = mix(own[at, :], bias[i][:tok], jnp.concatenate(parts, axis=0), member[i][...], value_rows)
+        tasks.append((own[at, :], bias[i][:tok], jnp.concatenate(parts, axis=0), member[i][...], value_rows))
+    for i, rows in enumerate(mix_all(tasks)):
+        out[i] = rows
 
 
 def local(n, query, key, value, q_gain, k_gain, order, cluster_rows, block_map):
@@ -248,14 +265,14 @@
     sized = lambda count: pltpu.VMEM((count * tok + tail, width), bf16)
     note, v_same, v_other, v_plain = pl.pallas_call(
         functools.partial(prep_kernel, half, early, tail),
-        out_shape=[pltpu.VMEM((8, tok), f32), sized(lead + 2 * rest), sized(lead + 2 * rest + half), sized(lead)],
+        out_shape=[pltpu.VMEM((8, tok), f32), sized(lead + 2 * rest), sized(lead + half), sized(lead)],
         in_specs=[ANY] * 4,
         out_specs=[VMEM] * 4,
         scratch_shapes=[
             pltpu.VMEM(query.shape, bf16),
             pltpu.VMEM(key.shape, bf16),
             pltpu.VMEM(order.shape, jnp.int32),
-            pltpu.SemaphoreType.DMA((2 * streams + 1 + 3 * lead + 4 * rest + half,)),
+            pltpu.SemaphoreType.DMA((2 * streams + 1 + 3 * lead + 2 * rest + half,)),
         ],
         compiler_params=limit,
     )(*[pltpu.with_memory_space_constraint(x, pltpu.HBM) for x in (query, key, value, order)])
@@ -266,9 +283,9 @@
     launches = [[] for _ in range(len(chain) + 1)]
     fillers = [[] for _ in range(len(chain) + 1)]
     for m in reversed(range(1, n)):
-        launches[min(m % 2, len(chain))].append(m)
+        launches[min(0 if m % 2 == 0 else 1 if m == 1 else 2, len(chain))].append(m)
     for i in range(kept):
-        fillers[min(1 + (i > 0), len(chain))].append(i)
+        fillers[min(i, len(chain))].append(i)
 
     def beside(at, note):
         for m in launches[at]:
@@ -295,22 +312,7 @@
     keys = [k_same] + [None] * (n - 1)
     for m in reversed(range(1, n)):
         message = k_other if m % 2 else k_same
-        if m <= 2 < n:
-            message = after(message, values[2])
         keys[m] = exchange(message, m)
-
-    further, across = {}, n // 2
-    held = {}
-    while rest and across:
-        group = sorted(held)
-        if group:
-            sent = held[group[0]] if len(group) == 1 else jnp.concatenate([held[m] for m in group], axis=0)
-            got = exchange(sent, across)
-            size = 2 * rest * tok
-            for at, m in enumerate(group):
-                held[m ^ across] = further[m ^ across] = got if len(group) == 1 else got[at * size : (at + 1) * size]
-        held[across] = values[across][lead * tok : (lead + 2 * rest) * tok]
-        across //= 2
 
     cluster_rows = after(cluster_rows, note)
     start = jnp.cumsum(cluster_rows, axis=1, dtype=jnp.int32) - cluster_rows
@@ -321,15 +323,33 @@
     bounds = jnp.pad(bounds.reshape(2 * streams, block_count).astype(f32), ((0, 0), (0, padded - block_count)))
 
     member, bias = [None] * kept, [None] * kept
-    for i in range(kept):
-        member[i], bias[i] = call(
-            functools.partial(blocks_kernel, half, i),
-            [
-                jax.ShapeDtypeStruct((n * tok, padded), bf16),
-                jax.ShapeDtypeStruct(((2 if i < half else 1) * tok, padded), bf16),
-            ],
-            [bounds, tables[i], *values],
+    for picks in [list(range(half)), list(range(half, kept))][: 1 + (rest > 0)]:
+        shapes = []
+        for i in picks:
+            shapes.append(jax.ShapeDtypeStruct((n * tok, padded), bf16))
+            shapes.append(jax.ShapeDtypeStruct(((2 if i < half else 1) * tok, padded), bf16))
+        made = call(
+            functools.partial(blocks_kernel, half, picks),
+            shapes,
+            [bounds, *[tables[i] for i in picks], *values],
         )
+        for at, i in enumerate(picks):
+            member[i], bias[i] = made[2 * at], made[2 * at + 1]
+    across = n // 2
+    held = {0: values[0][lead * tok : (lead + 2 * rest) * tok]}
+    while rest and across:
+        if across == n // 2 and n > 2:
+            held[across] = values[across][lead * tok : (lead + 2 * rest) * tok]
+        else:
+            group = sorted(held)
+            sent = jnp.concatenate([held[m] for m in group], axis=0)
+            got = exchange(after(sent, member[0]), across)
+            size = 2 * rest * tok
+            for at, m in enumerate(group):
+                held[m ^ across] = got[at * size : (at + 1) * size]
+        across //= 2
+    further = held if rest else {}
+
     peer, normed = call(
         functools.partial(peer_kernel, n, half, early, streams, tok, heads),
         [

time: 28.1 us -> 27.5 us (0.979)
  Pallas kernels: 5.11 us -> 3.96 us
  starting transfers between devices: 16.4 us -> 17.4 us
  waiting for transfers between devices: 5.08 us -> 4.78 us
    ppermute x3, waiting for transfers between devices: 2.06 us -> 0.42 us  [local(): lax.ppermute(note, 'head', [(i, i ^ step) for i in range(head_size)])]
    ppermute x8, waiting for transfers between devices: 3.03 us -> 4.36 us  [exchange(): return lax.ppermute(rows, 'seq', [(i, i ^ m) for i in range(n)])]
    pallas_call x9 -> x8, Pallas kernels: 3.76 us -> 2.64 us  [call(): pl.pallas_call(body, out_shape=shapes, in_specs=[VMEM] * len(args), out_s...]
    ppermute x8, starting transfers between devices: 12.8 us -> 13.7 us  [exchange(): return lax.ppermute(rows, 'seq', [(i, i ^ m) for i in range(n)])]
  transfers between devices with their start and end apart: 11 -> 11, of which waited for: 3 -> 6; matrix products, arithmetic and copies ran while one was open for 1% -> 1% of each run, Pallas kernels for 13% -> 10%
where the time goes in v4:
time: 27.5 us; the launch traced here: 27.3 us
  starting transfers between devices  17.4 us (63%)
  waiting for transfers between devices  4.78 us (17%)
  Pallas kernels  3.96 us (14%)
  other arithmetic  0.85 us (3%)
    ppermute x8, starting transfers between devices, exchange(): return lax.ppermute(rows, 'seq', [(i, i ^ m) for i in range(n)])  13.7 us
    ppermute x8, waiting for transfers between devices, exchange(): return lax.ppermute(rows, 'seq', [(i, i ^ m) for i in range(n)])  4.36 us
    ppermute x3, starting transfers between devices, local(): lax.ppermute(note, 'head', [(i, i ^ step) for i in range(head_size)])  3.65 us
    pallas_call x8, Pallas kernels, call(): pl.pallas_call(body, out_shape=shapes, in_specs=[VMEM] * len(args), out_s...  2.64 us
    pallas_call x1, Pallas kernels, local(): pl.pallas_call(functools.partial(prep_kernel, half, early, tail), out_sha...  1.32 us
    concatenate x1, other arithmetic, local(): return jnp.concatenate([lower, upper, own[half:]], axis=0)  0.69 us
  transfers between devices with their start and end apart: 11, of which 6 were waited for; matrix products, arithmetic and copies ran while one was open for 1% of the time, Pallas kernels for 10%

profile of v4, /device:TPU:0, one launch (start us, length us, event | category | flops | bytes accessed | tf_op | source)
XLA Modules:
  0.0 27.3 jit_solution(5402331049041253085)
XLA Ops:
  0.0 0.0 copy-start.4
  0.0 1.3 %shard_map.82 = (f32[8,128]{1,0:T(8,128)S(1)}, bf16[656,128]{1,0:T(8,128)(2,1)S(1)}, bf16[656,128]{1,0:T(8,128)(2,1)S(1)}, bf16[400,128]{1,0:T(8,128)(2,1)S(1)}) custom-call(bf16[5,128,128]{2,1,0:T(8,128)(2,1)} %query.3, bf16[5,128,128]{2,1,0:T(8,128)(2,1)} %key.3, bf16[5,128,128]{2,1,0:T(8,128)(2,1)} %value.1, s32[5,128]{1,0:T(8,128)} %order.1), custom_call_target="tpu_custom_call" | custom-call | tf_op jit(solution)/shard_map/pallas_call | solution.py:266
  1.3 0.5 %collective-permute-start = (f32[8,128]{1,0:T(8,128)S(1)}, f32[8,128]{1,0:T(8,128)S(1)}, u32[]{:S(2)}, u32[]{:S(2)}) collective-permute-start(f32[8,128]{1,0:T(8,128)S(1)} %get-tuple-element.27), channel_id=1, source_target_pairs={{0,1},{1,0},{2,3},{3,2},{4,5},{5,4},{6,7},{7,6},{8,9},{9,8},{10,11... | collective-permute-start | bytes 12296 | tf_op jit(solution)/shard_map/ppermute | solution.py:304
  1.8 3.7 %collective-permute-start.7 = (bf16[656,128]{1,0:T(8,128)(2,1)S(1)}, bf16[656,128]{1,0:T(8,128)(2,1)S(1)}, u32[]{:S(2)}, u32[]{:S(2)}) collective-permute-start(bf16[656,128]{1,0:T(8,128)(2,1)S(1)} %get-tuple-element.31.refs_2_.refs_4_.refs_1_), channel_id=1, source_target_pairs={{0,16},{8,24},{16,0},{24,8},{1,17},{9,25},{17,1},{25,9},{2,18},{10... | collective-permute-start | bytes 503816 | tf_op jit(solution)/shard_map/ppermute | solution.py:257
  5.5 0.0 copy-done.4
  5.5 0.0 collective-permute-done
  5.5 1.6 %collective-permute-start.1 = (f32[8,128]{1,0:T(8,128)S(1)}, f32[8,128]{1,0:T(8,128)S(1)}, u32[]{:S(2)}, u32[]{:S(2)}) collective-permute-start(f32[8,128]{1,0:T(8,128)S(1)} %add.60), channel_id=1, source_target_pairs={{0,2},{1,3},{2,0},{3,1},{4,6},{5,7},{6,4},{7,5},{8,10},{9,11},{10,... | collective-permute-start | bytes 12296 | tf_op jit(solution)/shard_map/ppermute | solution.py:304
  7.1 0.1 add.66
  7.2 1.6 %collective-permute-start.6 = (bf16[656,128]{1,0:T(8,128)(2,1)S(1)}, bf16[656,128]{1,0:T(8,128)(2,1)S(1)}, u32[]{:S(2)}, u32[]{:S(2)}) collective-permute-start(bf16[656,128]{1,0:T(8,128)(2,1)S(1)} %get-tuple-element.33), channel_id=1, source_target_pairs={{0,8},{8,0},{16,24},{24,16},{1,9},{9,1},{17,25},{25,17},{2,10},{10... | collective-permute-start | bytes 503816 | tf_op jit(solution)/shard_map/ppermute | solution.py:257
  8.8 0.4 %collective-permute-done.1 = f32[8,128]{1,0:T(8,128)S(1)} collective-permute-done((f32[8,128]{1,0:T(8,128)S(1)}, f32[8,128]{1,0:T(8,128)S(1)}, u32[]{:S(2)}, u32[]{:S(2)}) %collective-permute-start.1) | collective-permute-done | bytes 4128 | tf_op jit(solution)/shard_map/ppermute | solution.py:304
  9.2 0.0 copy-start
  9.2 0.0 copy-start.1
  9.2 1.6 %collective-permute-start.2 = (f32[8,128]{1,0:T(8,128)S(1)}, f32[8,128]{1,0:T(8,128)S(1)}, u32[]{:S(2)}, u32[]{:S(2)}) collective-permute-start(f32[8,128]{1,0:T(8,128)S(1)} %add.61), channel_id=1, source_target_pairs={{0,4},{1,5},{2,6},{3,7},{4,0},{5,1},{6,2},{7,3},{8,12},{9,13},{10,... | collective-permute-start | bytes 12296 | tf_op jit(solution)/shard_map/ppermute | solution.py:304
  10.8 0.0 copy-start.2
  10.8 0.0 copy-start.3
  10.8 0.0 copy-start.5
  10.8 2.1 %collective-permute-start.8 = (bf16[400,128]{1,0:T(8,128)(2,1)S(1)}, bf16[400,128]{1,0:T(8,128)(2,1)S(1)}, u32[]{:S(2)}, u32[]{:S(2)}) collective-permute-start(bf16[400,128]{1,0:T(8,128)(2,1)S(1)} %get-tuple-element.35), channel_id=1, source_target_pairs={{0,24},{8,16},{16,8},{24,0},{1,25},{9,17},{17,9},{25,1},{2,26},{10... | collective-permute-start | bytes 307208 | tf_op jit(solution)/shard_map/ppermute | solution.py:257
  12.9 0.0 collective-permute-done.2
  12.9 0.0 copy-done
  12.9 0.0 copy-done.1
  12.9 0.0 copy-done.2
  12.9 0.0 copy-done.3
  12.9 0.2 shard_map.83
  13.2 1.6 %collective-permute-start.3 = (bf16[144,128]{1,0:T(8,128)(2,1)S(1)}, bf16[144,128]{1,0:T(8,128)(2,1)S(1)}, u32[]{:S(2)}, u32[]{:S(2)}) collective-permute-start(bf16[144,128]{1,0:T(8,128)(2,1)S(1)} %get-tuple-element.30), channel_id=1, source_target_pairs={{0,8},{8,0},{16,24},{24,16},{1,9},{9,1},{17,25},{25,17},{2,10},{10... | collective-permute-start | bytes 110600 | tf_op jit(solution)/shard_map/ppermute | solution.py:257
  14.8 0.9 %collective-permute-start.5 = (bf16[144,128]{1,0:T(8,128)(2,1)S(1)}, bf16[144,128]{1,0:T(8,128)(2,1)S(1)}, u32[]{:S(2)}, u32[]{:S(2)}) collective-permute-start(bf16[144,128]{1,0:T(8,128)(2,1)S(1)} %get-tuple-element.30), channel_id=1, source_target_pairs={{0,24},{8,16},{16,8},{24,0},{1,25},{9,17},{17,9},{25,1},{2,26},{10... | collective-permute-start | bytes 110600 | tf_op jit(solution)/shard_map/ppermute | solution.py:257
  15.7 0.0 copy-done.5
  15.8 0.1 bitcast_add_fusion
  15.9 0.1 copy.10
  16.0 0.0 collective-permute-done.7.refs_4_.refs_6_.refs_3_
  16.0 1.1 %collective-permute-start.4 = (bf16[144,128]{1,0:T(8,128)(2,1)S(1)}, bf16[144,128]{1,0:T(8,128)(2,1)S(1)}, u32[]{:S(2)}, u32[]{:S(2)}) collective-permute-start(bf16[144,128]{1,0:T(8,128)(2,1)S(1)} %get-tuple-element.29.refs_0_), channel_id=1, source_target_pairs={{0,16},{8,24},{16,0},{24,8},{1,17},{9,25},{17,1},{25,9},{2,18},{10... | collective-permute-start | bytes 110600 | tf_op jit(solution)/shard_map/ppermute | solution.py:257
  17.1 1.1 %collective-permute-done.8.refs_5_.refs_7_.refs_4_ = bf16[400,128]{1,0:T(8,128)(2,1)S(1)} collective-permute-done((bf16[400,128]{1,0:T(8,128)(2,1)S(1)}, bf16[400,128]{1,0:T(8,128)(2,1)S(1)}, u32[]{:S(2)}, u32[]{:S(2)}) %collective-permute-start.8) | collective-permute-done | bytes 102432 | tf_op jit(solution)/shard_map/ppermute | solution.py:257
  18.1 0.8 %collective-permute-done.6.refs_3_.refs_5_.refs_2_ = bf16[656,128]{1,0:T(8,128)(2,1)S(1)} collective-permute-done((bf16[656,128]{1,0:T(8,128)(2,1)S(1)}, bf16[656,128]{1,0:T(8,128)(2,1)S(1)}, u32[]{:S(2)}, u32[]{:S(2)}) %collective-permute-start.6) | collective-permute-done | bytes 167968 | tf_op jit(solution)/shard_map/ppermute | solution.py:257
  18.9 0.5 %shard_map.86 = (bf16[512,128]{1,0:T(8,128)(2,1)S(1)}, bf16[256,128]{1,0:T(8,128)(2,1)S(1)}, bf16[512,128]{1,0:T(8,128)(2,1)S(1)}, bf16[256,128]{1,0:T(8,128)(2,1)S(1)}) custom-call(f32[10,128]{1,0:T(8,128)S(1)} %pad.4.bounds, f32[128,128]{1,0:T(8,128)S(1)} %shard_map.84.refs_0_, f32[128,128]{1,0:T(8,128)S(1)} %shard_map.85.refs_1_, ...), custom_call_target="tpu_custom_call" | custom-call | tf_op jit(solution)/shard_map/pallas_call | solution.py:33
  19.4 1.9 %collective-permute-start.9 = (bf16[512,128]{1,0:T(8,128)(2,1)S(1)}, bf16[512,128]{1,0:T(8,128)(2,1)S(1)}, u32[]{:S(2)}, u32[]{:S(2)}) collective-permute-start(bf16[512,128]{1,0:T(8,128)(2,1)S(1)} %pad_maximum_fusion.1), channel_id=1, source_target_pairs={{0,8},{8,0},{16,24},{24,16},{1,9},{9,1},{17,25},{25,17},{2,10},{10... | collective-permute-start | bytes 393224 | tf_op jit(solution)/shard_map/ppermute | solution.py:257
  21.4 0.2 collective-permute-done.4.refs_2_
  21.6 0.0 collective-permute-done.3.refs_1_
  21.6 0.0 collective-permute-done.5.refs_3_
  21.6 0.7 %shard_map.87 = (bf16[2,128,128]{2,1,0:T(8,128)(2,1)S(1)}, bf16[1,512,128]{2,1,0:T(8,128)(2,1)S(1)}) custom-call(f32[40,128]{1,0:T(8,128)S(1)} %copy-done.3, f32[40,128]{1,0:T(8,128)S(1)} %copy-done.2, bf16[640,128]{1,0:T(8,128)(2,1)S(1)} %get-tuple-element.28.own, bf16[144,128]{1,0:T(8,128)(2,1)S(1)} %get-tuple-element.29.refs_0_, ...), custom_call_target="tpu_custom_call" | custom-call | tf_op jit(solution)/shard_map/pallas_call | solution.py:33
  22.3 0.8 %collective-permute-start.10 = (bf16[2,128,128]{2,1,0:T(8,128)(2,1)S(1)}, bf16[2,128,128]{2,1,0:T(8,128)(2,1)S(1)}, u32[]{:S(2)}, u32[]{:S(2)}) collective-permute-start(bf16[2,128,128]{2,1,0:T(8,128)(2,1)S(1)} %get-tuple-element.48), channel_id=1, source_target_pairs={{0,8},{8,0},{16,24},{24,16},{1,9},{9,1},{17,25},{25,17},{2,10},{10... | collective-permute-start | bytes 196616 | tf_op jit(solution)/shard_map/ppermute | solution.py:257
  23.1 0.5 %shard_map.89 = (bf16[512,128]{1,0:T(8,128)(2,1)S(1)}, bf16[128,128]{1,0:T(8,128)(2,1)S(1)}) custom-call(f32[10,128]{1,0:T(8,128)S(1)} %pad.4.bounds, f32[128,128]{1,0:T(8,128)S(1)} %shard_map.88.refs_0_, bf16[656,128]{1,0:T(8,128)(2,1)S(1)} %get-tuple-element.31.refs_2_.refs_4_.refs_1_, bf16[656,128]{1,0:T(8,128)(2,1)S(1)} %collective-permute-done.6.refs_3_.refs_5_.refs_2_, ...), custom_call_target="tpu_custom_call" | custom-call | tf_op jit(solution)/shard_map/pallas_call | solution.py:33
  23.6 1.8 %collective-permute-done.9 = bf16[512,128]{1,0:T(8,128)(2,1)S(1)} collective-permute-done((bf16[512,128]{1,0:T(8,128)(2,1)S(1)}, bf16[512,128]{1,0:T(8,128)(2,1)S(1)}, u32[]{:S(2)}, u32[]{:S(2)}) %collective-permute-start.9) | collective-permute-done | bytes 131104 | tf_op jit(solution)/shard_map/ppermute | solution.py:257
  25.4 0.7 %shard_map.90 = bf16[3,128,128]{2,1,0:T(8,128)(2,1)S(1)} custom-call(f32[40,128]{1,0:T(8,128)S(1)} %copy-done.2, bf16[640,128]{1,0:T(8,128)(2,1)S(1)} %get-tuple-element.28.own, bf16[1,512,128]{2,1,0:T(8,128)(2,1)S(1)} %get-tuple-element.43.normed, bf16[144,128]{1,0:T(8,128)(2,1)S(1)} %get-tuple-element.29.refs_0_, ...), custom_call_target="tpu_custom_call" | custom-call | tf_op jit(solution)/shard_map/pallas_call | solution.py:33
  26.1 0.5 %collective-permute-done.10 = bf16[2,128,128]{2,1,0:T(8,128)(2,1)S(1)} collective-permute-done((bf16[2,128,128]{2,1,0:T(8,128)(2,1)S(1)}, bf16[2,128,128]{2,1,0:T(8,128)(2,1)S(1)}, u32[]{:S(2)}, u32[]{:S(2)}) %collective-permute-start.10) | collective-permute-done | bytes 65568 | tf_op jit(solution)/shard_map/ppermute | solution.py:257
  26.7 0.7 %pad_maximum_fusion = bf16[5,128,128]{2,1,0:T(8,128)(2,1)} fusion(bf16[1,128,128]{2,1,0:T(8,128)(2,1)S(1)} %slice.29, bf16[2,128,128]{2,1,0:T(8,128)(2,1)S(1)} %get-tuple-element.50, bf16[2,128,128]{2,1,0:T(8,128)(2,1)S(1)} %get-tuple-element.49), kind=kLoop, calls=%fused_computation | loop fusion | flops 163840 | bytes 327680 | tf_op jit(solution)/shard_map/concatenate | solution.py:370
  (21 shorter events, 0.2 us)
Async XLA Ops:
  0.0 5.5 %copy-start.4 = (s32[5,8,8]{2,1,0:T(8,128)S(1)}, s32[5,8,8]{2,1,0:T(8,128)}, u32[]{:S(2)}) copy-start(s32[5,8,8]{2,1,0:T(8,128)} %block_map.2) | copy-start | bytes 3844
  1.3 4.2 %collective-permute-start = (f32[8,128]{1,0:T(8,128)S(1)}, f32[8,128]{1,0:T(8,128)S(1)}, u32[]{:S(2)}, u32[]{:S(2)}) collective-permute-start(f32[8,128]{1,0:T(8,128)S(1)} %get-tuple-element.27), channel_id=1, source_target_pairs={{0,1},{1,0},{2,3},{3,2},{4,5},{5,4},{6,7},{7,6},{8,9},{9,8},{10,11... | collective-permute-start | bytes 12296 | tf_op jit(solution)/shard_map/ppermute | solution.py:304
  1.8 14.1 %collective-permute-start.7 = (bf16[656,128]{1,0:T(8,128)(2,1)S(1)}, bf16[656,128]{1,0:T(8,128)(2,1)S(1)}, u32[]{:S(2)}, u32[]{:S(2)}) collective-permute-start(bf16[656,128]{1,0:T(8,128)(2,1)S(1)} %get-tuple-element.31.refs_2_.refs_4_.refs_1_), channel_id=1, source_target_pairs={{0,16},{8,24},{16,0},{24,8},{1,17},{9,25},{17,1},{25,9},{2,18},{10... | collective-permute-start | bytes 503816 | tf_op jit(solution)/shard_map/ppermute | solution.py:257
  5.5 3.7 %collective-permute-start.1 = (f32[8,128]{1,0:T(8,128)S(1)}, f32[8,128]{1,0:T(8,128)S(1)}, u32[]{:S(2)}, u32[]{:S(2)}) collective-permute-start(f32[8,128]{1,0:T(8,128)S(1)} %add.60), channel_id=1, source_target_pairs={{0,2},{1,3},{2,0},{3,1},{4,6},{5,7},{6,4},{7,5},{8,10},{9,11},{10,... | collective-permute-start | bytes 12296 | tf_op jit(solution)/shard_map/ppermute | solution.py:304
  7.2 11.7 %collective-permute-start.6 = (bf16[656,128]{1,0:T(8,128)(2,1)S(1)}, bf16[656,128]{1,0:T(8,128)(2,1)S(1)}, u32[]{:S(2)}, u32[]{:S(2)}) collective-permute-start(bf16[656,128]{1,0:T(8,128)(2,1)S(1)} %get-tuple-element.33), channel_id=1, source_target_pairs={{0,8},{8,0},{16,24},{24,16},{1,9},{9,1},{17,25},{25,17},{2,10},{10... | collective-permute-start | bytes 503816 | tf_op jit(solution)/shard_map/ppermute | solution.py:257
  9.2 3.7 %copy-start = (bf16[5,128,128]{2,1,0:T(8,128)(2,1)S(1)}, bf16[5,128,128]{2,1,0:T(8,128)(2,1)}, u32[]{:S(2)}) copy-start(bf16[5,128,128]{2,1,0:T(8,128)(2,1)} %query.3) | copy-start | bytes 491524
  9.2 3.7 %copy-start.1 = (bf16[5,128,128]{2,1,0:T(8,128)(2,1)S(1)}, bf16[5,128,128]{2,1,0:T(8,128)(2,1)}, u32[]{:S(2)}) copy-start(bf16[5,128,128]{2,1,0:T(8,128)(2,1)} %key.3) | copy-start | bytes 491524
  9.2 3.7 %collective-permute-start.2 = (f32[8,128]{1,0:T(8,128)S(1)}, f32[8,128]{1,0:T(8,128)S(1)}, u32[]{:S(2)}, u32[]{:S(2)}) collective-permute-start(f32[8,128]{1,0:T(8,128)S(1)} %add.61), channel_id=1, source_target_pairs={{0,4},{1,5},{2,6},{3,7},{4,0},{5,1},{6,2},{7,3},{8,12},{9,13},{10,... | collective-permute-start | bytes 12296 | tf_op jit(solution)/shard_map/ppermute | solution.py:304
  10.8 2.1 %copy-start.2 = (f32[40,128]{1,0:T(8,128)S(1)}, f32[40,128]{1,0:T(8,128)}, u32[]{:S(2)}) copy-start(f32[40,128]{1,0:T(8,128)} %k_gain.5) | copy-start | bytes 61444
  10.8 2.1 %copy-start.3 = (f32[40,128]{1,0:T(8,128)S(1)}, f32[40,128]{1,0:T(8,128)}, u32[]{:S(2)}) copy-start(f32[40,128]{1,0:T(8,128)} %q_gain.3) | copy-start | bytes 61444
  10.8 4.9 %copy-start.5 = (s32[5,4]{0,1:T(4,128)S(1)}, s32[5,4]{0,1:T(4,128)}, u32[]{:S(2)}) copy-start(s32[5,4]{0,1:T(4,128)} %param.14) | copy-start | bytes 244
  10.8 7.3 %collective-permute-start.8 = (bf16[400,128]{1,0:T(8,128)(2,1)S(1)}, bf16[400,128]{1,0:T(8,128)(2,1)S(1)}, u32[]{:S(2)}, u32[]{:S(2)}) collective-permute-start(bf16[400,128]{1,0:T(8,128)(2,1)S(1)} %get-tuple-element.35), channel_id=1, source_target_pairs={{0,24},{8,16},{16,8},{24,0},{1,25},{9,17},{17,9},{25,1},{2,26},{10... | collective-permute-start | bytes 307208 | tf_op jit(solution)/shard_map/ppermute | solution.py:257
  13.2 8.4 %collective-permute-start.3 = (bf16[144,128]{1,0:T(8,128)(2,1)S(1)}, bf16[144,128]{1,0:T(8,128)(2,1)S(1)}, u32[]{:S(2)}, u32[]{:S(2)}) collective-permute-start(bf16[144,128]{1,0:T(8,128)(2,1)S(1)} %get-tuple-element.30), channel_id=1, source_target_pairs={{0,8},{8,0},{16,24},{24,16},{1,9},{9,1},{17,25},{25,17},{2,10},{10... | collective-permute-start | bytes 110600 | tf_op jit(solution)/shard_map/ppermute | solution.py:257
  14.8 6.8 %collective-permute-start.5 = (bf16[144,128]{1,0:T(8,128)(2,1)S(1)}, bf16[144,128]{1,0:T(8,128)(2,1)S(1)}, u32[]{:S(2)}, u32[]{:S(2)}) collective-permute-start(bf16[144,128]{1,0:T(8,128)(2,1)S(1)} %get-tuple-element.30), channel_id=1, source_target_pairs={{0,24},{8,16},{16,8},{24,0},{1,25},{9,17},{17,9},{25,1},{2,26},{10... | collective-permute-start | bytes 110600 | tf_op jit(solution)/shard_map/ppermute | solution.py:257
  16.0 5.6 %collective-permute-start.4 = (bf16[144,128]{1,0:T(8,128)(2,1)S(1)}, bf16[144,128]{1,0:T(8,128)(2,1)S(1)}, u32[]{:S(2)}, u32[]{:S(2)}) collective-permute-start(bf16[144,128]{1,0:T(8,128)(2,1)S(1)} %get-tuple-element.29.refs_0_), channel_id=1, source_target_pairs={{0,16},{8,24},{16,0},{24,8},{1,17},{9,25},{17,1},{25,9},{2,18},{10... | collective-permute-start | bytes 110600 | tf_op jit(solution)/shard_map/ppermute | solution.py:257
  19.4 6.0 %collective-permute-start.9 = (bf16[512,128]{1,0:T(8,128)(2,1)S(1)}, bf16[512,128]{1,0:T(8,128)(2,1)S(1)}, u32[]{:S(2)}, u32[]{:S(2)}) collective-permute-start(bf16[512,128]{1,0:T(8,128)(2,1)S(1)} %pad_maximum_fusion.1), channel_id=1, source_target_pairs={{0,8},{8,0},{16,24},{24,16},{1,9},{9,1},{17,25},{25,17},{2,10},{10... | collective-permute-start | bytes 393224 | tf_op jit(solution)/shard_map/ppermute | solution.py:257
  22.3 4.3 %collective-permute-start.10 = (bf16[2,128,128]{2,1,0:T(8,128)(2,1)S(1)}, bf16[2,128,128]{2,1,0:T(8,128)(2,1)S(1)}, u32[]{:S(2)}, u32[]{:S(2)}) collective-permute-start(bf16[2,128,128]{2,1,0:T(8,128)(2,1)S(1)} %get-tuple-element.48), channel_id=1, source_target_pairs={{0,8},{8,0},{16,24},{24,16},{1,9},{9,1},{17,25},{25,17},{2,10},{10... | collective-permute-start | bytes 196616 | tf_op jit(solution)/shard_map/ppermute | solution.py:257

commit v5 on v4

--- a/solution.py
+++ b/solution.py
@@ -45,8 +45,8 @@
     streams, tok, width = query.shape
     rest = streams - 2 * half
     parity = lax.rem(lax.axis_index("seq"), 2)
-    pairs = [(ref.at[s], there.at[s]) for ref, there in ((query, q_in), (key, k_in)) for s in range(streams)]
-    pairs.append((order, order_in))
+    pairs = [(order, order_in)]
+    pairs += [(ref.at[s], there.at[s]) for ref, there in ((query, q_in), (key, k_in)) for s in range(streams)]
     for target, side in ((plain, 1 - parity), (same, parity), (other, 1 - parity)):
         rows = [(value, side * half + i) for i in range(half)] + [(key, side * half + i) for i in range(early)]
         if target is same:
@@ -58,17 +58,7 @@
     copies = [pltpu.make_async_copy(src, dst, sems.at[i]) for i, (src, dst) in enumerate(pairs)]
     for copy in copies:
         copy.start()
-    totals = []
-    for j, ref in enumerate((q_in, k_in)):
-        total = None
-        for i in range(streams):
-            copies[j * streams + i].wait()
-            wide = ref[i].astype(jnp.float32)
-            total = wide * wide if total is None else total + wide * wide
-        totals.append(jnp.sum(total.T, axis=0, keepdims=True))
-    row = lax.broadcasted_iota(jnp.int32, (8, tok), 0)
-    note[...] = jnp.where(row == 0, totals[0], jnp.where(row == 1, totals[1], 0.0))
-    copies[2 * streams].wait()
+    copies[0].wait()
     row = lax.broadcasted_iota(jnp.int32, (tail, tok), 0)
     for side, targets in ((1 - parity, (plain, other)), (parity, (same,))):
         rows = jnp.zeros((tail, tok), jnp.float32)
@@ -79,6 +69,16 @@
             rows = jnp.where(row == 2 * i, high, jnp.where(row == 2 * i + 1, ids - high * tok, rows))
         for target in targets:
             target[target.shape[0] - tail :, :] = rows.astype(jnp.bfloat16)
+    totals = []
+    for j, ref in enumerate((q_in, k_in)):
+        total = None
+        for i in range(streams):
+            copies[1 + j * streams + i].wait()
+            wide = ref[i].astype(jnp.float32)
+            total = wide * wide if total is None else total + wide * wide
+        totals.append(jnp.sum(total.T, axis=0, keepdims=True))
+    row = lax.broadcasted_iota(jnp.int32, (8, tok), 0)
+    note[...] = jnp.where(row == 0, totals[0], jnp.where(row == 1, totals[1], 0.0))
     for copy in copies[2 * streams + 1 :]:
         copy.wait()
 

time: 27.5 us -> 27.5 us (level)
  no operation moved by 1% of the time
where the time goes in v5:
time: 27.5 us; the launch traced here: 27.3 us
  starting transfers between devices  17.4 us (63%)
  waiting for transfers between devices  4.78 us (17%)
  Pallas kernels  3.96 us (14%)
  other arithmetic  0.85 us (3%)
    ppermute x8, starting transfers between devices, exchange(): return lax.ppermute(rows, 'seq', [(i, i ^ m) for i in range(n)])  13.7 us
    ppermute x8, waiting for transfers between devices, exchange(): return lax.ppermute(rows, 'seq', [(i, i ^ m) for i in range(n)])  4.36 us
    ppermute x3, starting transfers between devices, local(): lax.ppermute(note, 'head', [(i, i ^ step) for i in range(head_size)])  3.65 us
    pallas_call x8, Pallas kernels, call(): pl.pallas_call(body, out_shape=shapes, in_specs=[VMEM] * len(args), out_s...  2.64 us
    pallas_call x1, Pallas kernels, local(): pl.pallas_call(functools.partial(prep_kernel, half, early, tail), out_sha...  1.32 us
    concatenate x1, other arithmetic, local(): return jnp.concatenate([lower, upper, own[half:]], axis=0)  0.69 us
  transfers between devices with their start and end apart: 11, of which 6 were waited for; matrix products, arithmetic and copies ran while one was open for 1% of the time, Pallas kernels for 10%

profile of v5, /device:TPU:0, one launch (start us, length us, event | category | flops | bytes accessed | tf_op | source)
XLA Modules:
  0.0 27.3 jit_solution(17192255496758373163)
XLA Ops:
  0.0 0.0 copy-start.4
  0.0 1.3 %shard_map.82 = (f32[8,128]{1,0:T(8,128)S(1)}, bf16[656,128]{1,0:T(8,128)(2,1)S(1)}, bf16[656,128]{1,0:T(8,128)(2,1)S(1)}, bf16[400,128]{1,0:T(8,128)(2,1)S(1)}) custom-call(bf16[5,128,128]{2,1,0:T(8,128)(2,1)} %query.3, bf16[5,128,128]{2,1,0:T(8,128)(2,1)} %key.3, bf16[5,128,128]{2,1,0:T(8,128)(2,1)} %value.1, s32[5,128]{1,0:T(8,128)} %order.1), custom_call_target="tpu_custom_call" | custom-call | tf_op jit(solution)/shard_map/pallas_call | solution.py:266
  1.3 0.5 %collective-permute-start = (f32[8,128]{1,0:T(8,128)S(1)}, f32[8,128]{1,0:T(8,128)S(1)}, u32[]{:S(2)}, u32[]{:S(2)}) collective-permute-start(f32[8,128]{1,0:T(8,128)S(1)} %get-tuple-element.27), channel_id=1, source_target_pairs={{0,1},{1,0},{2,3},{3,2},{4,5},{5,4},{6,7},{7,6},{8,9},{9,8},{10,11... | collective-permute-start | bytes 12296 | tf_op jit(solution)/shard_map/ppermute | solution.py:304
  1.8 3.7 %collective-permute-start.7 = (bf16[656,128]{1,0:T(8,128)(2,1)S(1)}, bf16[656,128]{1,0:T(8,128)(2,1)S(1)}, u32[]{:S(2)}, u32[]{:S(2)}) collective-permute-start(bf16[656,128]{1,0:T(8,128)(2,1)S(1)} %get-tuple-element.31.refs_2_.refs_4_.refs_1_), channel_id=1, source_target_pairs={{0,16},{8,24},{16,0},{24,8},{1,17},{9,25},{17,1},{25,9},{2,18},{10... | collective-permute-start | bytes 503816 | tf_op jit(solution)/shard_map/ppermute | solution.py:257
  5.5 0.0 copy-done.4
  5.5 0.0 collective-permute-done
  5.5 1.6 %collective-permute-start.1 = (f32[8,128]{1,0:T(8,128)S(1)}, f32[8,128]{1,0:T(8,128)S(1)}, u32[]{:S(2)}, u32[]{:S(2)}) collective-permute-start(f32[8,128]{1,0:T(8,128)S(1)} %add.60), channel_id=1, source_target_pairs={{0,2},{1,3},{2,0},{3,1},{4,6},{5,7},{6,4},{7,5},{8,10},{9,11},{10,... | collective-permute-start | bytes 12296 | tf_op jit(solution)/shard_map/ppermute | solution.py:304
  7.1 0.1 add.66
  7.2 1.6 %collective-permute-start.6 = (bf16[656,128]{1,0:T(8,128)(2,1)S(1)}, bf16[656,128]{1,0:T(8,128)(2,1)S(1)}, u32[]{:S(2)}, u32[]{:S(2)}) collective-permute-start(bf16[656,128]{1,0:T(8,128)(2,1)S(1)} %get-tuple-element.33), channel_id=1, source_target_pairs={{0,8},{8,0},{16,24},{24,16},{1,9},{9,1},{17,25},{25,17},{2,10},{10... | collective-permute-start | bytes 503816 | tf_op jit(solution)/shard_map/ppermute | solution.py:257
  8.8 0.4 %collective-permute-done.1 = f32[8,128]{1,0:T(8,128)S(1)} collective-permute-done((f32[8,128]{1,0:T(8,128)S(1)}, f32[8,128]{1,0:T(8,128)S(1)}, u32[]{:S(2)}, u32[]{:S(2)}) %collective-permute-start.1) | collective-permute-done | bytes 4128 | tf_op jit(solution)/shard_map/ppermute | solution.py:304
  9.2 0.0 copy-start
  9.2 0.0 copy-start.1
  9.2 1.6 %collective-permute-start.2 = (f32[8,128]{1,0:T(8,128)S(1)}, f32[8,128]{1,0:T(8,128)S(1)}, u32[]{:S(2)}, u32[]{:S(2)}) collective-permute-start(f32[8,128]{1,0:T(8,128)S(1)} %add.61), channel_id=1, source_target_pairs={{0,4},{1,5},{2,6},{3,7},{4,0},{5,1},{6,2},{7,3},{8,12},{9,13},{10,... | collective-permute-start | bytes 12296 | tf_op jit(solution)/shard_map/ppermute | solution.py:304
  10.8 0.0 copy-start.2
  10.8 0.0 copy-start.3
  10.8 0.0 copy-start.5
  10.8 2.1 %collective-permute-start.8 = (bf16[400,128]{1,0:T(8,128)(2,1)S(1)}, bf16[400,128]{1,0:T(8,128)(2,1)S(1)}, u32[]{:S(2)}, u32[]{:S(2)}) collective-permute-start(bf16[400,128]{1,0:T(8,128)(2,1)S(1)} %get-tuple-element.35), channel_id=1, source_target_pairs={{0,24},{8,16},{16,8},{24,0},{1,25},{9,17},{17,9},{25,1},{2,26},{10... | collective-permute-start | bytes 307208 | tf_op jit(solution)/shard_map/ppermute | solution.py:257
  12.9 0.0 collective-permute-done.2
  12.9 0.0 copy-done
  12.9 0.0 copy-done.1
  12.9 0.0 copy-done.2
  12.9 0.0 copy-done.3
  12.9 0.2 shard_map.83
  13.2 1.6 %collective-permute-start.3 = (bf16[144,128]{1,0:T(8,128)(2,1)S(1)}, bf16[144,128]{1,0:T(8,128)(2,1)S(1)}, u32[]{:S(2)}, u32[]{:S(2)}) collective-permute-start(bf16[144,128]{1,0:T(8,128)(2,1)S(1)} %get-tuple-element.30), channel_id=1, source_target_pairs={{0,8},{8,0},{16,24},{24,16},{1,9},{9,1},{17,25},{25,17},{2,10},{10... | collective-permute-start | bytes 110600 | tf_op jit(solution)/shard_map/ppermute | solution.py:257
  14.8 0.9 %collective-permute-start.5 = (bf16[144,128]{1,0:T(8,128)(2,1)S(1)}, bf16[144,128]{1,0:T(8,128)(2,1)S(1)}, u32[]{:S(2)}, u32[]{:S(2)}) collective-permute-start(bf16[144,128]{1,0:T(8,128)(2,1)S(1)} %get-tuple-element.30), channel_id=1, source_target_pairs={{0,24},{8,16},{16,8},{24,0},{1,25},{9,17},{17,9},{25,1},{2,26},{10... | collective-permute-start | bytes 110600 | tf_op jit(solution)/shard_map/ppermute | solution.py:257
  15.7 0.0 copy-done.5
  15.8 0.1 bitcast_add_fusion
  15.9 0.1 copy.10
  16.0 0.0 collective-permute-done.7.refs_4_.refs_6_.refs_3_
  16.0 1.1 %collective-permute-start.4 = (bf16[144,128]{1,0:T(8,128)(2,1)S(1)}, bf16[144,128]{1,0:T(8,128)(2,1)S(1)}, u32[]{:S(2)}, u32[]{:S(2)}) collective-permute-start(bf16[144,128]{1,0:T(8,128)(2,1)S(1)} %get-tuple-element.29.refs_0_), channel_id=1, source_target_pairs={{0,16},{8,24},{16,0},{24,8},{1,17},{9,25},{17,1},{25,9},{2,18},{10... | collective-permute-start | bytes 110600 | tf_op jit(solution)/shard_map/ppermute | solution.py:257
  17.1 1.1 %collective-permute-done.8.refs_5_.refs_7_.refs_4_ = bf16[400,128]{1,0:T(8,128)(2,1)S(1)} collective-permute-done((bf16[400,128]{1,0:T(8,128)(2,1)S(1)}, bf16[400,128]{1,0:T(8,128)(2,1)S(1)}, u32[]{:S(2)}, u32[]{:S(2)}) %collective-permute-start.8) | collective-permute-done | bytes 102432 | tf_op jit(solution)/shard_map/ppermute | solution.py:257
  18.1 0.8 %collective-permute-done.6.refs_3_.refs_5_.refs_2_ = bf16[656,128]{1,0:T(8,128)(2,1)S(1)} collective-permute-done((bf16[656,128]{1,0:T(8,128)(2,1)S(1)}, bf16[656,128]{1,0:T(8,128)(2,1)S(1)}, u32[]{:S(2)}, u32[]{:S(2)}) %collective-permute-start.6) | collective-permute-done | bytes 167968 | tf_op jit(solution)/shard_map/ppermute | solution.py:257
  18.9 0.5 %shard_map.86 = (bf16[512,128]{1,0:T(8,128)(2,1)S(1)}, bf16[256,128]{1,0:T(8,128)(2,1)S(1)}, bf16[512,128]{1,0:T(8,128)(2,1)S(1)}, bf16[256,128]{1,0:T(8,128)(2,1)S(1)}) custom-call(f32[10,128]{1,0:T(8,128)S(1)} %pad.4.bounds, f32[128,128]{1,0:T(8,128)S(1)} %shard_map.84.refs_0_, f32[128,128]{1,0:T(8,128)S(1)} %shard_map.85.refs_1_, ...), custom_call_target="tpu_custom_call" | custom-call | tf_op jit(solution)/shard_map/pallas_call | solution.py:33
  19.4 1.9 %collective-permute-start.9 = (bf16[512,128]{1,0:T(8,128)(2,1)S(1)}, bf16[512,128]{1,0:T(8,128)(2,1)S(1)}, u32[]{:S(2)}, u32[]{:S(2)}) collective-permute-start(bf16[512,128]{1,0:T(8,128)(2,1)S(1)} %pad_maximum_fusion.1), channel_id=1, source_target_pairs={{0,8},{8,0},{16,24},{24,16},{1,9},{9,1},{17,25},{25,17},{2,10},{10... | collective-permute-start | bytes 393224 | tf_op jit(solution)/shard_map/ppermute | solution.py:257
  21.4 0.2 collective-permute-done.4.refs_2_
  21.6 0.0 collective-permute-done.3.refs_1_
  21.6 0.0 collective-permute-done.5.refs_3_
  21.6 0.7 %shard_map.87 = (bf16[2,128,128]{2,1,0:T(8,128)(2,1)S(1)}, bf16[1,512,128]{2,1,0:T(8,128)(2,1)S(1)}) custom-call(f32[40,128]{1,0:T(8,128)S(1)} %copy-done.3, f32[40,128]{1,0:T(8,128)S(1)} %copy-done.2, bf16[640,128]{1,0:T(8,128)(2,1)S(1)} %get-tuple-element.28.own, bf16[144,128]{1,0:T(8,128)(2,1)S(1)} %get-tuple-element.29.refs_0_, ...), custom_call_target="tpu_custom_call" | custom-call | tf_op jit(solution)/shard_map/pallas_call | solution.py:33
  22.3 0.8 %collective-permute-start.10 = (bf16[2,128,128]{2,1,0:T(8,128)(2,1)S(1)}, bf16[2,128,128]{2,1,0:T(8,128)(2,1)S(1)}, u32[]{:S(2)}, u32[]{:S(2)}) collective-permute-start(bf16[2,128,128]{2,1,0:T(8,128)(2,1)S(1)} %get-tuple-element.48), channel_id=1, source_target_pairs={{0,8},{8,0},{16,24},{24,16},{1,9},{9,1},{17,25},{25,17},{2,10},{10... | collective-permute-start | bytes 196616 | tf_op jit(solution)/shard_map/ppermute | solution.py:257
  23.1 0.5 %shard_map.89 = (bf16[512,128]{1,0:T(8,128)(2,1)S(1)}, bf16[128,128]{1,0:T(8,128)(2,1)S(1)}) custom-call(f32[10,128]{1,0:T(8,128)S(1)} %pad.4.bounds, f32[128,128]{1,0:T(8,128)S(1)} %shard_map.88.refs_0_, bf16[656,128]{1,0:T(8,128)(2,1)S(1)} %get-tuple-element.31.refs_2_.refs_4_.refs_1_, bf16[656,128]{1,0:T(8,128)(2,1)S(1)} %collective-permute-done.6.refs_3_.refs_5_.refs_2_, ...), custom_call_target="tpu_custom_call" | custom-call | tf_op jit(solution)/shard_map/pallas_call | solution.py:33
  23.6 1.8 %collective-permute-done.9 = bf16[512,128]{1,0:T(8,128)(2,1)S(1)} collective-permute-done((bf16[512,128]{1,0:T(8,128)(2,1)S(1)}, bf16[512,128]{1,0:T(8,128)(2,1)S(1)}, u32[]{:S(2)}, u32[]{:S(2)}) %collective-permute-start.9) | collective-permute-done | bytes 131104 | tf_op jit(solution)/shard_map/ppermute | solution.py:257
  25.4 0.7 %shard_map.90 = bf16[3,128,128]{2,1,0:T(8,128)(2,1)S(1)} custom-call(f32[40,128]{1,0:T(8,128)S(1)} %copy-done.2, bf16[640,128]{1,0:T(8,128)(2,1)S(1)} %get-tuple-element.28.own, bf16[1,512,128]{2,1,0:T(8,128)(2,1)S(1)} %get-tuple-element.43.normed, bf16[144,128]{1,0:T(8,128)(2,1)S(1)} %get-tuple-element.29.refs_0_, ...), custom_call_target="tpu_custom_call" | custom-call | tf_op jit(solution)/shard_map/pallas_call | solution.py:33
  26.1 0.5 %collective-permute-done.10 = bf16[2,128,128]{2,1,0:T(8,128)(2,1)S(1)} collective-permute-done((bf16[2,128,128]{2,1,0:T(8,128)(2,1)S(1)}, bf16[2,128,128]{2,1,0:T(8,128)(2,1)S(1)}, u32[]{:S(2)}, u32[]{:S(2)}) %collective-permute-start.10) | collective-permute-done | bytes 65568 | tf_op jit(solution)/shard_map/ppermute | solution.py:257
  26.7 0.7 %pad_maximum_fusion = bf16[5,128,128]{2,1,0:T(8,128)(2,1)} fusion(bf16[1,128,128]{2,1,0:T(8,128)(2,1)S(1)} %slice.29, bf16[2,128,128]{2,1,0:T(8,128)(2,1)S(1)} %get-tuple-element.50, bf16[2,128,128]{2,1,0:T(8,128)(2,1)S(1)} %get-tuple-element.49), kind=kLoop, calls=%fused_computation | loop fusion | flops 163840 | bytes 327680 | tf_op jit(solution)/shard_map/concatenate | solution.py:370
  (21 shorter events, 0.2 us)
Async XLA Ops:
  0.0 5.5 %copy-start.4 = (s32[5,8,8]{2,1,0:T(8,128)S(1)}, s32[5,8,8]{2,1,0:T(8,128)}, u32[]{:S(2)}) copy-start(s32[5,8,8]{2,1,0:T(8,128)} %block_map.2) | copy-start | bytes 3844
  1.3 4.2 %collective-permute-start = (f32[8,128]{1,0:T(8,128)S(1)}, f32[8,128]{1,0:T(8,128)S(1)}, u32[]{:S(2)}, u32[]{:S(2)}) collective-permute-start(f32[8,128]{1,0:T(8,128)S(1)} %get-tuple-element.27), channel_id=1, source_target_pairs={{0,1},{1,0},{2,3},{3,2},{4,5},{5,4},{6,7},{7,6},{8,9},{9,8},{10,11... | collective-permute-start | bytes 12296 | tf_op jit(solution)/shard_map/ppermute | solution.py:304
  1.8 14.1 %collective-permute-start.7 = (bf16[656,128]{1,0:T(8,128)(2,1)S(1)}, bf16[656,128]{1,0:T(8,128)(2,1)S(1)}, u32[]{:S(2)}, u32[]{:S(2)}) collective-permute-start(bf16[656,128]{1,0:T(8,128)(2,1)S(1)} %get-tuple-element.31.refs_2_.refs_4_.refs_1_), channel_id=1, source_target_pairs={{0,16},{8,24},{16,0},{24,8},{1,17},{9,25},{17,1},{25,9},{2,18},{10... | collective-permute-start | bytes 503816 | tf_op jit(solution)/shard_map/ppermute | solution.py:257
  5.5 3.7 %collective-permute-start.1 = (f32[8,128]{1,0:T(8,128)S(1)}, f32[8,128]{1,0:T(8,128)S(1)}, u32[]{:S(2)}, u32[]{:S(2)}) collective-permute-start(f32[8,128]{1,0:T(8,128)S(1)} %add.60), channel_id=1, source_target_pairs={{0,2},{1,3},{2,0},{3,1},{4,6},{5,7},{6,4},{7,5},{8,10},{9,11},{10,... | collective-permute-start | bytes 12296 | tf_op jit(solution)/shard_map/ppermute | solution.py:304
  7.2 11.7 %collective-permute-start.6 = (bf16[656,128]{1,0:T(8,128)(2,1)S(1)}, bf16[656,128]{1,0:T(8,128)(2,1)S(1)}, u32[]{:S(2)}, u32[]{:S(2)}) collective-permute-start(bf16[656,128]{1,0:T(8,128)(2,1)S(1)} %get-tuple-element.33), channel_id=1, source_target_pairs={{0,8},{8,0},{16,24},{24,16},{1,9},{9,1},{17,25},{25,17},{2,10},{10... | collective-permute-start | bytes 503816 | tf_op jit(solution)/shard_map/ppermute | solution.py:257
  9.2 3.7 %copy-start = (bf16[5,128,128]{2,1,0:T(8,128)(2,1)S(1)}, bf16[5,128,128]{2,1,0:T(8,128)(2,1)}, u32[]{:S(2)}) copy-start(bf16[5,128,128]{2,1,0:T(8,128)(2,1)} %query.3) | copy-start | bytes 491524
  9.2 3.7 %copy-start.1 = (bf16[5,128,128]{2,1,0:T(8,128)(2,1)S(1)}, bf16[5,128,128]{2,1,0:T(8,128)(2,1)}, u32[]{:S(2)}) copy-start(bf16[5,128,128]{2,1,0:T(8,128)(2,1)} %key.3) | copy-start | bytes 491524
  9.2 3.7 %collective-permute-start.2 = (f32[8,128]{1,0:T(8,128)S(1)}, f32[8,128]{1,0:T(8,128)S(1)}, u32[]{:S(2)}, u32[]{:S(2)}) collective-permute-start(f32[8,128]{1,0:T(8,128)S(1)} %add.61), channel_id=1, source_target_pairs={{0,4},{1,5},{2,6},{3,7},{4,0},{5,1},{6,2},{7,3},{8,12},{9,13},{10,... | collective-permute-start | bytes 12296 | tf_op jit(solution)/shard_map/ppermute | solution.py:304
  10.8 2.1 %copy-start.2 = (f32[40,128]{1,0:T(8,128)S(1)}, f32[40,128]{1,0:T(8,128)}, u32[]{:S(2)}) copy-start(f32[40,128]{1,0:T(8,128)} %k_gain.5) | copy-start | bytes 61444
  10.8 2.1 %copy-start.3 = (f32[40,128]{1,0:T(8,128)S(1)}, f32[40,128]{1,0:T(8,128)}, u32[]{:S(2)}) copy-start(f32[40,128]{1,0:T(8,128)} %q_gain.3) | copy-start | bytes 61444
  10.8 4.9 %copy-start.5 = (s32[5,4]{0,1:T(4,128)S(1)}, s32[5,4]{0,1:T(4,128)}, u32[]{:S(2)}) copy-start(s32[5,4]{0,1:T(4,128)} %param.14) | copy-start | bytes 244
  10.8 7.3 %collective-permute-start.8 = (bf16[400,128]{1,0:T(8,128)(2,1)S(1)}, bf16[400,128]{1,0:T(8,128)(2,1)S(1)}, u32[]{:S(2)}, u32[]{:S(2)}) collective-permute-start(bf16[400,128]{1,0:T(8,128)(2,1)S(1)} %get-tuple-element.35), channel_id=1, source_target_pairs={{0,24},{8,16},{16,8},{24,0},{1,25},{9,17},{17,9},{25,1},{2,26},{10... | collective-permute-start | bytes 307208 | tf_op jit(solution)/shard_map/ppermute | solution.py:257
  13.2 8.4 %collective-permute-start.3 = (bf16[144,128]{1,0:T(8,128)(2,1)S(1)}, bf16[144,128]{1,0:T(8,128)(2,1)S(1)}, u32[]{:S(2)}, u32[]{:S(2)}) collective-permute-start(bf16[144,128]{1,0:T(8,128)(2,1)S(1)} %get-tuple-element.30), channel_id=1, source_target_pairs={{0,8},{8,0},{16,24},{24,16},{1,9},{9,1},{17,25},{25,17},{2,10},{10... | collective-permute-start | bytes 110600 | tf_op jit(solution)/shard_map/ppermute | solution.py:257
  14.8 6.8 %collective-permute-start.5 = (bf16[144,128]{1,0:T(8,128)(2,1)S(1)}, bf16[144,128]{1,0:T(8,128)(2,1)S(1)}, u32[]{:S(2)}, u32[]{:S(2)}) collective-permute-start(bf16[144,128]{1,0:T(8,128)(2,1)S(1)} %get-tuple-element.30), channel_id=1, source_target_pairs={{0,24},{8,16},{16,8},{24,0},{1,25},{9,17},{17,9},{25,1},{2,26},{10... | collective-permute-start | bytes 110600 | tf_op jit(solution)/shard_map/ppermute | solution.py:257
  16.0 5.6 %collective-permute-start.4 = (bf16[144,128]{1,0:T(8,128)(2,1)S(1)}, bf16[144,128]{1,0:T(8,128)(2,1)S(1)}, u32[]{:S(2)}, u32[]{:S(2)}) collective-permute-start(bf16[144,128]{1,0:T(8,128)(2,1)S(1)} %get-tuple-element.29.refs_0_), channel_id=1, source_target_pairs={{0,16},{8,24},{16,0},{24,8},{1,17},{9,25},{17,1},{25,9},{2,18},{10... | collective-permute-start | bytes 110600 | tf_op jit(solution)/shard_map/ppermute | solution.py:257
  19.4 6.0 %collective-permute-start.9 = (bf16[512,128]{1,0:T(8,128)(2,1)S(1)}, bf16[512,128]{1,0:T(8,128)(2,1)S(1)}, u32[]{:S(2)}, u32[]{:S(2)}) collective-permute-start(bf16[512,128]{1,0:T(8,128)(2,1)S(1)} %pad_maximum_fusion.1), channel_id=1, source_target_pairs={{0,8},{8,0},{16,24},{24,16},{1,9},{9,1},{17,25},{25,17},{2,10},{10... | collective-permute-start | bytes 393224 | tf_op jit(solution)/shard_map/ppermute | solution.py:257
  22.3 4.3 %collective-permute-start.10 = (bf16[2,128,128]{2,1,0:T(8,128)(2,1)S(1)}, bf16[2,128,128]{2,1,0:T(8,128)(2,1)S(1)}, u32[]{:S(2)}, u32[]{:S(2)}) collective-permute-start(bf16[2,128,128]{2,1,0:T(8,128)(2,1)S(1)} %get-tuple-element.48), channel_id=1, source_target_pairs={{0,8},{8,0},{16,24},{24,16},{1,9},{9,1},{17,25},{25,17},{2,10},{10... | collective-permute-start | bytes 196616 | tf_op jit(solution)/shard_map/ppermute | solution.py:257

commit v6 on v5

--- a/solution.py
+++ b/solution.py
@@ -308,6 +308,7 @@
         functools.partial(norm_kernel, half, early, heads),
         [rows(half - early, 16), rows(half - early, 16), rows(kept + rest + early, 0)],
         [note, query, key, q_gain, k_gain],
+        cost=weight,
     )
     keys = [k_same] + [None] * (n - 1)
     for m in reversed(range(1, n)):
@@ -332,6 +333,7 @@
             functools.partial(blocks_kernel, half, picks),
             shapes,
             [bounds, *[tables[i] for i in picks], *values],
+            cost=1000,
         )
         for at, i in enumerate(picks):
             member[i], bias[i] = made[2 * at], made[2 * at + 1]

time: 27.5 us -> 27.5 us (level)
  no operation moved by 1% of the time
where the time goes in v6:
time: 27.5 us; the launch traced here: 27.3 us
  starting transfers between devices  17.4 us (63%)
  waiting for transfers between devices  4.77 us (17%)
  Pallas kernels  3.94 us (14%)
  other arithmetic  0.85 us (3%)
    ppermute x8, starting transfers between devices, exchange(): return lax.ppermute(rows, 'seq', [(i, i ^ m) for i in range(n)])  13.7 us
    ppermute x8, waiting for transfers between devices, exchange(): return lax.ppermute(rows, 'seq', [(i, i ^ m) for i in range(n)])  4.34 us
    ppermute x3, starting transfers between devices, local(): lax.ppermute(note, 'head', [(i, i ^ step) for i in range(head_size)])  3.66 us
    pallas_call x8, Pallas kernels, call(): pl.pallas_call(body, out_shape=shapes, in_specs=[VMEM] * len(args), out_s...  2.63 us
    pallas_call x1, Pallas kernels, local(): pl.pallas_call(functools.partial(prep_kernel, half, early, tail), out_sha...  1.32 us
    concatenate x1, other arithmetic, local(): return jnp.concatenate([lower, upper, own[half:]], axis=0)  0.69 us
  transfers between devices with their start and end apart: 11, of which 6 were waited for; matrix products, arithmetic and copies ran while one was open for 1% of the time, Pallas kernels for 10%

profile of v6, /device:TPU:0, one launch (start us, length us, event | category | flops | bytes accessed | tf_op | source)
XLA Modules:
  0.0 27.3 jit_solution(13244048536578254523)
XLA Ops:
  0.0 0.0 copy-start.4
  0.0 1.3 %shard_map.82 = (f32[8,128]{1,0:T(8,128)S(1)}, bf16[656,128]{1,0:T(8,128)(2,1)S(1)}, bf16[656,128]{1,0:T(8,128)(2,1)S(1)}, bf16[400,128]{1,0:T(8,128)(2,1)S(1)}) custom-call(bf16[5,128,128]{2,1,0:T(8,128)(2,1)} %query.3, bf16[5,128,128]{2,1,0:T(8,128)(2,1)} %key.3, bf16[5,128,128]{2,1,0:T(8,128)(2,1)} %value.1, s32[5,128]{1,0:T(8,128)} %order.1), custom_call_target="tpu_custom_call" | custom-call | tf_op jit(solution)/shard_map/pallas_call | solution.py:266
  1.3 0.5 %collective-permute-start = (f32[8,128]{1,0:T(8,128)S(1)}, f32[8,128]{1,0:T(8,128)S(1)}, u32[]{:S(2)}, u32[]{:S(2)}) collective-permute-start(f32[8,128]{1,0:T(8,128)S(1)} %get-tuple-element.27), channel_id=1, source_target_pairs={{0,1},{1,0},{2,3},{3,2},{4,5},{5,4},{6,7},{7,6},{8,9},{9,8},{10,11... | collective-permute-start | bytes 12296 | tf_op jit(solution)/shard_map/ppermute | solution.py:304
  1.8 3.7 %collective-permute-start.7 = (bf16[656,128]{1,0:T(8,128)(2,1)S(1)}, bf16[656,128]{1,0:T(8,128)(2,1)S(1)}, u32[]{:S(2)}, u32[]{:S(2)}) collective-permute-start(bf16[656,128]{1,0:T(8,128)(2,1)S(1)} %get-tuple-element.31.refs_2_.refs_4_.refs_1_), channel_id=1, source_target_pairs={{0,16},{8,24},{16,0},{24,8},{1,17},{9,25},{17,1},{25,9},{2,18},{10... | collective-permute-start | bytes 503816 | tf_op jit(solution)/shard_map/ppermute | solution.py:257
  5.5 0.0 copy-done.4
  5.5 0.0 collective-permute-done
  5.5 1.6 %collective-permute-start.1 = (f32[8,128]{1,0:T(8,128)S(1)}, f32[8,128]{1,0:T(8,128)S(1)}, u32[]{:S(2)}, u32[]{:S(2)}) collective-permute-start(f32[8,128]{1,0:T(8,128)S(1)} %add.60), channel_id=1, source_target_pairs={{0,2},{1,3},{2,0},{3,1},{4,6},{5,7},{6,4},{7,5},{8,10},{9,11},{10,... | collective-permute-start | bytes 12296 | tf_op jit(solution)/shard_map/ppermute | solution.py:304
  7.1 0.1 add.66
  7.2 1.6 %collective-permute-start.6 = (bf16[656,128]{1,0:T(8,128)(2,1)S(1)}, bf16[656,128]{1,0:T(8,128)(2,1)S(1)}, u32[]{:S(2)}, u32[]{:S(2)}) collective-permute-start(bf16[656,128]{1,0:T(8,128)(2,1)S(1)} %get-tuple-element.33), channel_id=1, source_target_pairs={{0,8},{8,0},{16,24},{24,16},{1,9},{9,1},{17,25},{25,17},{2,10},{10... | collective-permute-start | bytes 503816 | tf_op jit(solution)/shard_map/ppermute | solution.py:257
  8.8 0.4 %collective-permute-done.1 = f32[8,128]{1,0:T(8,128)S(1)} collective-permute-done((f32[8,128]{1,0:T(8,128)S(1)}, f32[8,128]{1,0:T(8,128)S(1)}, u32[]{:S(2)}, u32[]{:S(2)}) %collective-permute-start.1) | collective-permute-done | bytes 4128 | tf_op jit(solution)/shard_map/ppermute | solution.py:304
  9.2 0.0 copy-start
  9.2 0.0 copy-start.1
  9.2 0.0 copy-start.2
  9.2 0.0 copy-start.3
  9.2 1.6 %collective-permute-start.2 = (f32[8,128]{1,0:T(8,128)S(1)}, f32[8,128]{1,0:T(8,128)S(1)}, u32[]{:S(2)}, u32[]{:S(2)}) collective-permute-start(f32[8,128]{1,0:T(8,128)S(1)} %add.61), channel_id=1, source_target_pairs={{0,4},{1,5},{2,6},{3,7},{4,0},{5,1},{6,2},{7,3},{8,12},{9,13},{10,... | collective-permute-start | bytes 12296 | tf_op jit(solution)/shard_map/ppermute | solution.py:304
  10.8 2.1 %collective-permute-start.8 = (bf16[400,128]{1,0:T(8,128)(2,1)S(1)}, bf16[400,128]{1,0:T(8,128)(2,1)S(1)}, u32[]{:S(2)}, u32[]{:S(2)}) collective-permute-start(bf16[400,128]{1,0:T(8,128)(2,1)S(1)} %get-tuple-element.35), channel_id=1, source_target_pairs={{0,24},{8,16},{16,8},{24,0},{1,25},{9,17},{17,9},{25,1},{2,26},{10... | collective-permute-start | bytes 307208 | tf_op jit(solution)/shard_map/ppermute | solution.py:257
  12.9 0.0 collective-permute-done.2
  12.9 0.0 copy-done
  12.9 0.0 copy-done.1
  12.9 0.0 copy-done.2
  12.9 0.0 copy-done.3
  12.9 0.0 copy-start.5
  13.0 0.2 shard_map.83
  13.2 1.6 %collective-permute-start.3 = (bf16[144,128]{1,0:T(8,128)(2,1)S(1)}, bf16[144,128]{1,0:T(8,128)(2,1)S(1)}, u32[]{:S(2)}, u32[]{:S(2)}) collective-permute-start(bf16[144,128]{1,0:T(8,128)(2,1)S(1)} %get-tuple-element.30), channel_id=1, source_target_pairs={{0,8},{8,0},{16,24},{24,16},{1,9},{9,1},{17,25},{25,17},{2,10},{10... | collective-permute-start | bytes 110600 | tf_op jit(solution)/shard_map/ppermute | solution.py:257
  14.8 0.9 %collective-permute-start.5 = (bf16[144,128]{1,0:T(8,128)(2,1)S(1)}, bf16[144,128]{1,0:T(8,128)(2,1)S(1)}, u32[]{:S(2)}, u32[]{:S(2)}) collective-permute-start(bf16[144,128]{1,0:T(8,128)(2,1)S(1)} %get-tuple-element.30), channel_id=1, source_target_pairs={{0,24},{8,16},{16,8},{24,0},{1,25},{9,17},{17,9},{25,1},{2,26},{10... | collective-permute-start | bytes 110600 | tf_op jit(solution)/shard_map/ppermute | solution.py:257
  15.8 0.0 copy-done.5
  15.8 0.1 bitcast_add_fusion
  15.9 0.1 copy.10
  16.0 0.0 collective-permute-done.7.refs_4_.refs_6_.refs_3_
  16.0 1.1 %collective-permute-start.4 = (bf16[144,128]{1,0:T(8,128)(2,1)S(1)}, bf16[144,128]{1,0:T(8,128)(2,1)S(1)}, u32[]{:S(2)}, u32[]{:S(2)}) collective-permute-start(bf16[144,128]{1,0:T(8,128)(2,1)S(1)} %get-tuple-element.29.refs_0_), channel_id=1, source_target_pairs={{0,16},{8,24},{16,0},{24,8},{1,17},{9,25},{17,1},{25,9},{2,18},{10... | collective-permute-start | bytes 110600 | tf_op jit(solution)/shard_map/ppermute | solution.py:257
  17.1 1.0 %collective-permute-done.8.refs_5_.refs_7_.refs_4_ = bf16[400,128]{1,0:T(8,128)(2,1)S(1)} collective-permute-done((bf16[400,128]{1,0:T(8,128)(2,1)S(1)}, bf16[400,128]{1,0:T(8,128)(2,1)S(1)}, u32[]{:S(2)}, u32[]{:S(2)}) %collective-permute-start.8) | collective-permute-done | bytes 102432 | tf_op jit(solution)/shard_map/ppermute | solution.py:257
  18.1 0.8 %collective-permute-done.6.refs_3_.refs_5_.refs_2_ = bf16[656,128]{1,0:T(8,128)(2,1)S(1)} collective-permute-done((bf16[656,128]{1,0:T(8,128)(2,1)S(1)}, bf16[656,128]{1,0:T(8,128)(2,1)S(1)}, u32[]{:S(2)}, u32[]{:S(2)}) %collective-permute-start.6) | collective-permute-done | bytes 167968 | tf_op jit(solution)/shard_map/ppermute | solution.py:257
  18.9 0.5 %shard_map.86 = (bf16[512,128]{1,0:T(8,128)(2,1)S(1)}, bf16[256,128]{1,0:T(8,128)(2,1)S(1)}, bf16[512,128]{1,0:T(8,128)(2,1)S(1)}, bf16[256,128]{1,0:T(8,128)(2,1)S(1)}) custom-call(f32[10,128]{1,0:T(8,128)S(1)} %pad.4.bounds, f32[128,128]{1,0:T(8,128)S(1)} %shard_map.84.refs_0_, f32[128,128]{1,0:T(8,128)S(1)} %shard_map.85.refs_1_, ...), custom_call_target="tpu_custom_call" | custom-call | flops 1000 | tf_op jit(solution)/shard_map/pallas_call | solution.py:33
  19.4 1.9 %collective-permute-start.9 = (bf16[512,128]{1,0:T(8,128)(2,1)S(1)}, bf16[512,128]{1,0:T(8,128)(2,1)S(1)}, u32[]{:S(2)}, u32[]{:S(2)}) collective-permute-start(bf16[512,128]{1,0:T(8,128)(2,1)S(1)} %pad_maximum_fusion.1), channel_id=1, source_target_pairs={{0,8},{8,0},{16,24},{24,16},{1,9},{9,1},{17,25},{25,17},{2,10},{10... | collective-permute-start | bytes 393224 | tf_op jit(solution)/shard_map/ppermute | solution.py:257
  21.4 0.2 collective-permute-done.4.refs_2_
  21.6 0.0 collective-permute-done.3.refs_1_
  21.6 0.0 collective-permute-done.5.refs_3_
  21.6 0.7 %shard_map.87 = (bf16[2,128,128]{2,1,0:T(8,128)(2,1)S(1)}, bf16[1,512,128]{2,1,0:T(8,128)(2,1)S(1)}) custom-call(f32[40,128]{1,0:T(8,128)S(1)} %copy-done.3, f32[40,128]{1,0:T(8,128)S(1)} %copy-done.2, bf16[640,128]{1,0:T(8,128)(2,1)S(1)} %get-tuple-element.28.own, bf16[144,128]{1,0:T(8,128)(2,1)S(1)} %get-tuple-element.29.refs_0_, ...), custom_call_target="tpu_custom_call" | custom-call | tf_op jit(solution)/shard_map/pallas_call | solution.py:33
  22.3 0.8 %collective-permute-start.10 = (bf16[2,128,128]{2,1,0:T(8,128)(2,1)S(1)}, bf16[2,128,128]{2,1,0:T(8,128)(2,1)S(1)}, u32[]{:S(2)}, u32[]{:S(2)}) collective-permute-start(bf16[2,128,128]{2,1,0:T(8,128)(2,1)S(1)} %get-tuple-element.48), channel_id=1, source_target_pairs={{0,8},{8,0},{16,24},{24,16},{1,9},{9,1},{17,25},{25,17},{2,10},{10... | collective-permute-start | bytes 196616 | tf_op jit(solution)/shard_map/ppermute | solution.py:257
  23.1 0.5 %shard_map.89 = (bf16[512,128]{1,0:T(8,128)(2,1)S(1)}, bf16[128,128]{1,0:T(8,128)(2,1)S(1)}) custom-call(f32[10,128]{1,0:T(8,128)S(1)} %pad.4.bounds, f32[128,128]{1,0:T(8,128)S(1)} %shard_map.88.refs_0_, bf16[656,128]{1,0:T(8,128)(2,1)S(1)} %get-tuple-element.31.refs_2_.refs_4_.refs_1_, bf16[656,128]{1,0:T(8,128)(2,1)S(1)} %collective-permute-done.6.refs_3_.refs_5_.refs_2_, ...), custom_call_target="tpu_custom_call" | custom-call | flops 1000 | tf_op jit(solution)/shard_map/pallas_call | solution.py:33
  23.6 1.8 %collective-permute-done.9 = bf16[512,128]{1,0:T(8,128)(2,1)S(1)} collective-permute-done((bf16[512,128]{1,0:T(8,128)(2,1)S(1)}, bf16[512,128]{1,0:T(8,128)(2,1)S(1)}, u32[]{:S(2)}, u32[]{:S(2)}) %collective-permute-start.9) | collective-permute-done | bytes 131104 | tf_op jit(solution)/shard_map/ppermute | solution.py:257
  25.4 0.7 %shard_map.90 = bf16[3,128,128]{2,1,0:T(8,128)(2,1)S(1)} custom-call(f32[40,128]{1,0:T(8,128)S(1)} %copy-done.2, bf16[640,128]{1,0:T(8,128)(2,1)S(1)} %get-tuple-element.28.own, bf16[1,512,128]{2,1,0:T(8,128)(2,1)S(1)} %get-tuple-element.43.normed, bf16[144,128]{1,0:T(8,128)(2,1)S(1)} %get-tuple-element.29.refs_0_, ...), custom_call_target="tpu_custom_call" | custom-call | tf_op jit(solution)/shard_map/pallas_call | solution.py:33
  26.1 0.5 %collective-permute-done.10 = bf16[2,128,128]{2,1,0:T(8,128)(2,1)S(1)} collective-permute-done((bf16[2,128,128]{2,1,0:T(8,128)(2,1)S(1)}, bf16[2,128,128]{2,1,0:T(8,128)(2,1)S(1)}, u32[]{:S(2)}, u32[]{:S(2)}) %collective-permute-start.10) | collective-permute-done | bytes 65568 | tf_op jit(solution)/shard_map/ppermute | solution.py:257
  26.7 0.7 %pad_maximum_fusion = bf16[5,128,128]{2,1,0:T(8,128)(2,1)} fusion(bf16[1,128,128]{2,1,0:T(8,128)(2,1)S(1)} %slice.29, bf16[2,128,128]{2,1,0:T(8,128)(2,1)S(1)} %get-tuple-element.50, bf16[2,128,128]{2,1,0:T(8,128)(2,1)S(1)} %get-tuple-element.49), kind=kLoop, calls=%fused_computation | loop fusion | flops 163840 | bytes 327680 | tf_op jit(solution)/shard_map/concatenate | solution.py:372
  (21 shorter events, 0.2 us)
Async XLA Ops:
  0.0 5.5 %copy-start.4 = (s32[5,8,8]{2,1,0:T(8,128)S(1)}, s32[5,8,8]{2,1,0:T(8,128)}, u32[]{:S(2)}) copy-start(s32[5,8,8]{2,1,0:T(8,128)} %block_map.2) | copy-start | bytes 3844
  1.3 4.2 %collective-permute-start = (f32[8,128]{1,0:T(8,128)S(1)}, f32[8,128]{1,0:T(8,128)S(1)}, u32[]{:S(2)}, u32[]{:S(2)}) collective-permute-start(f32[8,128]{1,0:T(8,128)S(1)} %get-tuple-element.27), channel_id=1, source_target_pairs={{0,1},{1,0},{2,3},{3,2},{4,5},{5,4},{6,7},{7,6},{8,9},{9,8},{10,11... | collective-permute-start | bytes 12296 | tf_op jit(solution)/shard_map/ppermute | solution.py:304
  1.8 14.2 %collective-permute-start.7 = (bf16[656,128]{1,0:T(8,128)(2,1)S(1)}, bf16[656,128]{1,0:T(8,128)(2,1)S(1)}, u32[]{:S(2)}, u32[]{:S(2)}) collective-permute-start(bf16[656,128]{1,0:T(8,128)(2,1)S(1)} %get-tuple-element.31.refs_2_.refs_4_.refs_1_), channel_id=1, source_target_pairs={{0,16},{8,24},{16,0},{24,8},{1,17},{9,25},{17,1},{25,9},{2,18},{10... | collective-permute-start | bytes 503816 | tf_op jit(solution)/shard_map/ppermute | solution.py:257
  5.5 3.7 %collective-permute-start.1 = (f32[8,128]{1,0:T(8,128)S(1)}, f32[8,128]{1,0:T(8,128)S(1)}, u32[]{:S(2)}, u32[]{:S(2)}) collective-permute-start(f32[8,128]{1,0:T(8,128)S(1)} %add.60), channel_id=1, source_target_pairs={{0,2},{1,3},{2,0},{3,1},{4,6},{5,7},{6,4},{7,5},{8,10},{9,11},{10,... | collective-permute-start | bytes 12296 | tf_op jit(solution)/shard_map/ppermute | solution.py:304
  7.2 11.7 %collective-permute-start.6 = (bf16[656,128]{1,0:T(8,128)(2,1)S(1)}, bf16[656,128]{1,0:T(8,128)(2,1)S(1)}, u32[]{:S(2)}, u32[]{:S(2)}) collective-permute-start(bf16[656,128]{1,0:T(8,128)(2,1)S(1)} %get-tuple-element.33), channel_id=1, source_target_pairs={{0,8},{8,0},{16,24},{24,16},{1,9},{9,1},{17,25},{25,17},{2,10},{10... | collective-permute-start | bytes 503816 | tf_op jit(solution)/shard_map/ppermute | solution.py:257
  9.2 3.7 %copy-start = (bf16[5,128,128]{2,1,0:T(8,128)(2,1)S(1)}, bf16[5,128,128]{2,1,0:T(8,128)(2,1)}, u32[]{:S(2)}) copy-start(bf16[5,128,128]{2,1,0:T(8,128)(2,1)} %query.3) | copy-start | bytes 491524
  9.2 3.7 %copy-start.1 = (bf16[5,128,128]{2,1,0:T(8,128)(2,1)S(1)}, bf16[5,128,128]{2,1,0:T(8,128)(2,1)}, u32[]{:S(2)}) copy-start(bf16[5,128,128]{2,1,0:T(8,128)(2,1)} %key.3) | copy-start | bytes 491524
  9.2 3.7 %copy-start.2 = (f32[40,128]{1,0:T(8,128)S(1)}, f32[40,128]{1,0:T(8,128)}, u32[]{:S(2)}) copy-start(f32[40,128]{1,0:T(8,128)} %k_gain.5) | copy-start | bytes 61444
  9.2 3.7 %copy-start.3 = (f32[40,128]{1,0:T(8,128)S(1)}, f32[40,128]{1,0:T(8,128)}, u32[]{:S(2)}) copy-start(f32[40,128]{1,0:T(8,128)} %q_gain.3) | copy-start | bytes 61444
  9.2 3.7 %collective-permute-start.2 = (f32[8,128]{1,0:T(8,128)S(1)}, f32[8,128]{1,0:T(8,128)S(1)}, u32[]{:S(2)}, u32[]{:S(2)}) collective-permute-start(f32[8,128]{1,0:T(8,128)S(1)} %add.61), channel_id=1, source_target_pairs={{0,4},{1,5},{2,6},{3,7},{4,0},{5,1},{6,2},{7,3},{8,12},{9,13},{10,... | collective-permute-start | bytes 12296 | tf_op jit(solution)/shard_map/ppermute | solution.py:304
  10.8 7.3 %collective-permute-start.8 = (bf16[400,128]{1,0:T(8,128)(2,1)S(1)}, bf16[400,128]{1,0:T(8,128)(2,1)S(1)}, u32[]{:S(2)}, u32[]{:S(2)}) collective-permute-start(bf16[400,128]{1,0:T(8,128)(2,1)S(1)} %get-tuple-element.35), channel_id=1, source_target_pairs={{0,24},{8,16},{16,8},{24,0},{1,25},{9,17},{17,9},{25,1},{2,26},{10... | collective-permute-start | bytes 307208 | tf_op jit(solution)/shard_map/ppermute | solution.py:257
  12.9 2.8 %copy-start.5 = (s32[5,4]{0,1:T(4,128)S(1)}, s32[5,4]{0,1:T(4,128)}, u32[]{:S(2)}) copy-start(s32[5,4]{0,1:T(4,128)} %param.14) | copy-start | bytes 244
  13.2 8.4 %collective-permute-start.3 = (bf16[144,128]{1,0:T(8,128)(2,1)S(1)}, bf16[144,128]{1,0:T(8,128)(2,1)S(1)}, u32[]{:S(2)}, u32[]{:S(2)}) collective-permute-start(bf16[144,128]{1,0:T(8,128)(2,1)S(1)} %get-tuple-element.30), channel_id=1, source_target_pairs={{0,8},{8,0},{16,24},{24,16},{1,9},{9,1},{17,25},{25,17},{2,10},{10... | collective-permute-start | bytes 110600 | tf_op jit(solution)/shard_map/ppermute | solution.py:257
  14.8 6.8 %collective-permute-start.5 = (bf16[144,128]{1,0:T(8,128)(2,1)S(1)}, bf16[144,128]{1,0:T(8,128)(2,1)S(1)}, u32[]{:S(2)}, u32[]{:S(2)}) collective-permute-start(bf16[144,128]{1,0:T(8,128)(2,1)S(1)} %get-tuple-element.30), channel_id=1, source_target_pairs={{0,24},{8,16},{16,8},{24,0},{1,25},{9,17},{17,9},{25,1},{2,26},{10... | collective-permute-start | bytes 110600 | tf_op jit(solution)/shard_map/ppermute | solution.py:257
  16.0 5.6 %collective-permute-start.4 = (bf16[144,128]{1,0:T(8,128)(2,1)S(1)}, bf16[144,128]{1,0:T(8,128)(2,1)S(1)}, u32[]{:S(2)}, u32[]{:S(2)}) collective-permute-start(bf16[144,128]{1,0:T(8,128)(2,1)S(1)} %get-tuple-element.29.refs_0_), channel_id=1, source_target_pairs={{0,16},{8,24},{16,0},{24,8},{1,17},{9,25},{17,1},{25,9},{2,18},{10... | collective-permute-start | bytes 110600 | tf_op jit(solution)/shard_map/ppermute | solution.py:257
  19.4 6.0 %collective-permute-start.9 = (bf16[512,128]{1,0:T(8,128)(2,1)S(1)}, bf16[512,128]{1,0:T(8,128)(2,1)S(1)}, u32[]{:S(2)}, u32[]{:S(2)}) collective-permute-start(bf16[512,128]{1,0:T(8,128)(2,1)S(1)} %pad_maximum_fusion.1), channel_id=1, source_target_pairs={{0,8},{8,0},{16,24},{24,16},{1,9},{9,1},{17,25},{25,17},{2,10},{10... | collective-permute-start | bytes 393224 | tf_op jit(solution)/shard_map/ppermute | solution.py:257
  22.3 4.3 %collective-permute-start.10 = (bf16[2,128,128]{2,1,0:T(8,128)(2,1)S(1)}, bf16[2,128,128]{2,1,0:T(8,128)(2,1)S(1)}, u32[]{:S(2)}, u32[]{:S(2)}) collective-permute-start(bf16[2,128,128]{2,1,0:T(8,128)(2,1)S(1)} %get-tuple-element.48), channel_id=1, source_target_pairs={{0,8},{8,0},{16,24},{24,16},{1,9},{9,1},{17,25},{25,17},{2,10},{10... | collective-permute-start | bytes 196616 | tf_op jit(solution)/shard_map/ppermute | solution.py:257
